TPU v7x, 32 devices: a whole 2x2x4 slice. The times are simulated.
32 devices in a mesh: parts: 2 (over x), ulysses: 16 (over z, y, core).
Axes of the slice: x: 2, y: 2, z: 4, core: 2. Of those that a mesh axis runs over, the one named last changes fastest.
Arguments:
- query: bfloat16 [4096, 5120], P(('parts', 'ulysses')), parts along dimension 0, may hold values from -64 to 64
- key: bfloat16 [4096, 5120], P(('parts', 'ulysses')), parts along dimension 0, may hold values from -64 to 64
- value: bfloat16 [4096, 5120], P(('parts', 'ulysses')), parts along dimension 0, may hold values from -6 to 6
- query_gain: float32 [5120], replicated, may hold values from 1 to 4
- key_gain: float32 [5120], replicated, may hold values from 1 to 4
- key_blocks: int32 [80, 16, 12], P('parts'), parts along dimension 0, may hold values from 0 to 15, as said below
- block_counts: int32 [80, 16], P('parts'), parts along dimension 0, may hold values from 1 to 12, as said below
Outputs:
- attended: bfloat16 [4096, 5120], P(('parts', 'ulysses')), parts along dimension 0
There are 2 independent parts, one for each index of `parts`. A program takes and returns all parts, laid end to end along the dimension named above; an argument that names none is the same for every part. Nothing has to cross between parts.
Inputs may be any that keep to these rules, and one draw needn't show every extreme that they name: `key_blocks`: each row of 12 entries lists different key blocks, the first one being the query block itself. `block_counts`: some row of every draw attends all 12 listed blocks.
All inputs are finite; a program needn't handle non-finite values.
Results may differ from a plain program's by a relative error of at most 0.0013.
The roundings to bfloat16 on the way count: a program that leaves them out, or rounds other values in their place, can miss the bound.
Values may be sent and summed in bfloat16 or wider, within the bound.
No kernel may reach another device: no remote copies, remote signals or barrier semaphores. Data moves between devices by JAX's collectives and lax.ppermute only.
A program may use at most 128 MiB of HBM per device.

v0:
```python
import jax
import jax.numpy as jnp
from jax import lax
from jax.sharding import PartitionSpec as P

HEADS = 40
HEAD_DIM = 128
TILE = 128
KMAX = 12


NORM_EPS = 1e-06


def rms_norm(values_in, gain):
    widened = values_in.astype(jnp.float32)
    inverse = lax.rsqrt(jnp.mean(widened * widened, axis=-1, keepdims=True) + NORM_EPS)
    return (widened * inverse * gain).astype(jnp.bfloat16)


def pick_group():
    for group_size in (8, 4, 2, 1):
        return group_size
    return 1


def local(query, key, value, query_gain, key_gain, key_blocks, block_counts):
    devices = lax.axis_size("ulysses")
    my_index = lax.axis_index("ulysses")
    tok_dev = query.shape[0]
    blocks = tok_dev * devices // TILE
    per_device = HEADS * tok_dev // TILE
    unit_total = HEADS * blocks
    softmax_scale = HEAD_DIM ** (-0.5)
    q_norm = rms_norm(query, query_gain)
    k_norm = rms_norm(key, key_gain)
    marks_all = jnp.arange(devices + 1, dtype=jnp.int32)
    bounds = marks_all * per_device
    span_heads = min(HEADS, (per_device + blocks - 2) // blocks + 1)
    first_head = bounds[:-1] // blocks
    owner_heads = jnp.minimum(
        first_head[:, None] + jnp.arange(span_heads, dtype=jnp.int32)[None, :], HEADS - 1
    )
    packed = (
        jnp.stack([q_norm, k_norm, value], axis=0)
        .reshape(3, tok_dev, HEADS, HEAD_DIM)
        .transpose(2, 0, 1, 3)
    )
    outgoing = (
        packed[owner_heads.T]
        .transpose(0, 2, 1, 3, 4)
        .reshape(span_heads * 3, devices * tok_dev, HEAD_DIM)
    )
    arrived = lax.all_to_all(outgoing, "ulysses", split_axis=1, concat_axis=1, tiled=True)
    resident = arrived.reshape(span_heads, 3, blocks, TILE, HEAD_DIM)
    unit_start = bounds[my_index]
    unit_count = bounds[my_index + 1] - unit_start
    base_head = unit_start // blocks
    group_size = pick_group()
    results = jnp.zeros((span_heads, blocks, TILE, HEAD_DIM), jnp.bfloat16)

    def attend_group(step_index, results):
        local_units = step_index * group_size + jnp.arange(group_size, dtype=jnp.int32)
        unit_live = local_units < unit_count
        unit_ids = jnp.minimum(unit_start + local_units, unit_total - 1)
        unit_heads = unit_ids // blocks
        qblock = unit_ids % blocks
        unit_slots = jnp.clip(unit_heads - base_head, 0, span_heads - 1)
        key_lists = key_blocks[unit_heads, qblock]
        live_count = block_counts[unit_heads, qblock]
        query_matrix = resident[unit_slots, 0, qblock]
        key_panels = resident[unit_slots[:, None], 1, key_lists]
        value_panels = resident[unit_slots[:, None], 2, key_lists]
        logit_matrix = (
            jnp.einsum(
                "gqd,gjkd->gqjk", query_matrix, key_panels, preferred_element_type=jnp.float32
            )
            * softmax_scale
        )
        live_mask = (jnp.arange(KMAX, dtype=jnp.int32)[None, :] < live_count[:, None])[
            :, None, :, None
        ]
        logit_matrix = jnp.where(live_mask, logit_matrix, -1e30)
        row_peak = jnp.max(logit_matrix, axis=(2, 3), keepdims=True)
        weights = jnp.where(live_mask, jnp.exp(logit_matrix - row_peak), 0.0)
        row_denominator = jnp.sum(weights, axis=(2, 3))
        summed = jnp.einsum(
            "gqjk,gjkd->gqd",
            weights.astype(jnp.bfloat16),
            value_panels,
            preferred_element_type=jnp.float32,
        )
        combined = (summed / row_denominator[:, :, None]).astype(jnp.bfloat16)
        write_slots = jnp.where(unit_live, unit_slots, span_heads)
        return results.at[write_slots, qblock].set(combined, mode="drop")

    step_total = (unit_count + group_size - 1) // group_size
    results = lax.fori_loop(0, step_total, attend_group, results)
    leaving = results.reshape(span_heads, blocks * TILE, HEAD_DIM)
    returned = lax.all_to_all(leaving, "ulysses", split_axis=1, concat_axis=0, tiled=True)
    head_range = jnp.arange(HEADS, dtype=jnp.int32)
    selector = (owner_heads.reshape(-1)[None, :] == head_range[:, None]).astype(jnp.bfloat16)
    gathered = jnp.einsum("hs,std->thd", selector, returned, preferred_element_type=jnp.float32)
    return gathered.astype(jnp.bfloat16).reshape(tok_dev, HEADS * HEAD_DIM)


def solution(mesh):
    in_specs = (
        P(("parts", "ulysses"), None),
        P(("parts", "ulysses"), None),
        P(("parts", "ulysses"), None),
        P(),
        P(),
        P("parts", None, None),
        P("parts", None),
    )
    out_specs = P(("parts", "ulysses"), None)
    return jax.shard_map(local, mesh=mesh, in_specs=in_specs, out_specs=out_specs, check_vma=False)
```

profile of v0, /device:TPU:0, one launch (start us, length us, event | category | flops | bytes accessed | tf_op | source)
XLA Modules:
  0.0 437.5 jit_solution(12614179643249267152)
XLA Ops:
  15.7 3.4 maximum_bitcast_fusion
  19.2 6.1 %gather_fusion.5 = bf16[64,3,128,128]{3,2,1,0:T(8,128)(2,1)} fusion(bf16[40,3,128,128]{3,2,1,0:T(8,128)(2,1)} %maximum_bitcast_fusion, s32[1024]{0:T(1024)S(1)} %pad_clamp_fusion), kind=kCustom, calls=%fused_computation.5 | custom fusion | bytes 12583168 | tf_op jit(solution)/shard_map/gather | solution.py:50
  25.3 4.1 copy.45
  29.4 24.2 %copy.46 = bf16[12,2048,128]{2,0,1:T(8,128)(2,1)} copy(bf16[12,2048,128]{2,1,0:T(8,128)(2,1)S(1)} %bitcast.81) | data formatting | bytes 12582912 | tf_op jit(solution)/shard_map/reshape | solution.py:52
  53.6 7.6 %all-to-all-start = ((bf16[12,2048,128]{2,0,1:T(8,128)(2,1)}), bf16[12,2048,128]{2,0,1:T(8,128)(2,1)}, u32[]{:S(2)}, u32[]{:S(2)}) async-start(bf16[12,2048,128]{2,0,1:T(8,128)(2,1)} %copy.46), calls=%async_computation | async-start | bytes 16777216 | tf_op jit(solution)/shard_map/all_to_all | solution.py:54
  62.2 149.7 %all-to-all-done = bf16[12,2048,128]{2,0,1:T(8,128)(2,1)} async-done(((bf16[12,2048,128]{2,0,1:T(8,128)(2,1)}), bf16[12,2048,128]{2,0,1:T(8,128)(2,1)}, u32[]{:S(2)}, u32[]{:S(2)}) %all-to-all-start) | async-done | bytes 6291488 | tf_op jit(solution)/shard_map/all_to_all | solution.py:54
  211.9 7.7 %copy.47 = bf16[12,2048,128]{2,1,0:T(8,128)(2,1)} copy(bf16[12,2048,128]{2,0,1:T(8,128)(2,1)} %all-to-all-done) | data formatting | bytes 12582912 | tf_op jit(solution)/shard_map/all_to_all | solution.py:54
  221.5 130.0 %while.12 = (s32[]{:T(128)}, bf16[4,16,128,128]{3,2,1,0:T(8,128)(2,1)}, s32[]{:T(128)}, s32[]{:T(128)}, s32[]{:T(128)}, /*index=5*/s32[]{:T(128)}, s32[40,16]{0,...) while((s32[]{:T(128)}, ...), condition=%wide.region_6.7_spmd, body=%wide.region_2.6_spmd.sunk | while | flops 826015360 | bytes 64776988 | solution.py:98
  223.2 4.6 %gather_fusion.3 = bf16[96,128,128]{2,1,0:T(8,128)(2,1)S(1)} fusion(bf16[4,3,16,128,128]{4,3,2,1,0:T(8,128)(2,1)} %get-tuple-element.297, s32[96]{0:T(128)S(1)} %reshape.352), kind=kCustom, calls=%fused_computation.3.clone.1 | custom fusion | bytes 6292608 | tf_op jit(solution)/shard_map/while/body/gather | solution.py:72
  228.5 3.4 gather_fusion.4
  235.7 4.6 %gather_fusion.1 = bf16[96,128,128]{2,1,0:T(8,128)(2,1)S(1)} fusion(bf16[4,3,16,128,128]{4,3,2,1,0:T(8,128)(2,1)} %get-tuple-element.297, s32[96]{0:T(128)S(1)} %reshape.351), kind=kCustom, calls=%fused_computation.4.clone.1 | custom fusion | bytes 6292608 | tf_op jit(solution)/shard_map/while/body/gather | solution.py:73
  240.3 4.9 %fusion.65 = bf16[8,128,128]{2,1,0:T(8,128)(2,1)S(1)} fusion(bf16[8,12,128,128]{3,2,1,0:T(8,128)(2,1)S(1)} %bitcast.80, f32[8,128,12,128]{1,3,2,0:T(8,128)} %copy-done.1, f32[8,128]{1,0:T(8,128)S(1)} %get-tuple-element.267, pred[8,12]{1,0:T(8,128)(4,1)S(1)} %iota_compare_fusion.3, f32[8,128]{1,0:T(8,128)S(1)} %fusion.64), kind=kOutput, calls=%fused_computation.16.clone.1 | convolution fusion | flops 410779648 | bytes 9707616 | tf_op jit(solution)/shard_map/while/body/gqjk,gjkd->gqd/dot_general | solution.py:87
  249.2 4.6 %gather_fusion.3 = bf16[96,128,128]{2,1,0:T(8,128)(2,1)S(1)} fusion(bf16[4,3,16,128,128]{4,3,2,1,0:T(8,128)(2,1)} %get-tuple-element.297, s32[96]{0:T(128)S(1)} %reshape.352), kind=kCustom, calls=%fused_computation.3.clone.1 | custom fusion | bytes 6292608 | tf_op jit(solution)/shard_map/while/body/gather | solution.py:72
  254.5 3.4 gather_fusion.4
  261.7 4.6 %gather_fusion.1 = bf16[96,128,128]{2,1,0:T(8,128)(2,1)S(1)} fusion(bf16[4,3,16,128,128]{4,3,2,1,0:T(8,128)(2,1)} %get-tuple-element.297, s32[96]{0:T(128)S(1)} %reshape.351), kind=kCustom, calls=%fused_computation.4.clone.1 | custom fusion | bytes 6292608 | tf_op jit(solution)/shard_map/while/body/gather | solution.py:73
  266.3 4.9 %fusion.65 = bf16[8,128,128]{2,1,0:T(8,128)(2,1)S(1)} fusion(bf16[8,12,128,128]{3,2,1,0:T(8,128)(2,1)S(1)} %bitcast.80, f32[8,128,12,128]{1,3,2,0:T(8,128)} %copy-done.1, f32[8,128]{1,0:T(8,128)S(1)} %get-tuple-element.267, pred[8,12]{1,0:T(8,128)(4,1)S(1)} %iota_compare_fusion.3, f32[8,128]{1,0:T(8,128)S(1)} %fusion.64), kind=kOutput, calls=%fused_computation.16.clone.1 | convolution fusion | flops 410779648 | bytes 9707616 | tf_op jit(solution)/shard_map/while/body/gqjk,gjkd->gqd/dot_general | solution.py:87
  275.2 4.6 %gather_fusion.3 = bf16[96,128,128]{2,1,0:T(8,128)(2,1)S(1)} fusion(bf16[4,3,16,128,128]{4,3,2,1,0:T(8,128)(2,1)} %get-tuple-element.297, s32[96]{0:T(128)S(1)} %reshape.352), kind=kCustom, calls=%fused_computation.3.clone.1 | custom fusion | bytes 6292608 | tf_op jit(solution)/shard_map/while/body/gather | solution.py:72
  280.5 3.4 gather_fusion.4
  287.7 4.6 %gather_fusion.1 = bf16[96,128,128]{2,1,0:T(8,128)(2,1)S(1)} fusion(bf16[4,3,16,128,128]{4,3,2,1,0:T(8,128)(2,1)} %get-tuple-element.297, s32[96]{0:T(128)S(1)} %reshape.351), kind=kCustom, calls=%fused_computation.4.clone.1 | custom fusion | bytes 6292608 | tf_op jit(solution)/shard_map/while/body/gather | solution.py:73
  292.3 4.9 %fusion.65 = bf16[8,128,128]{2,1,0:T(8,128)(2,1)S(1)} fusion(bf16[8,12,128,128]{3,2,1,0:T(8,128)(2,1)S(1)} %bitcast.80, f32[8,128,12,128]{1,3,2,0:T(8,128)} %copy-done.1, f32[8,128]{1,0:T(8,128)S(1)} %get-tuple-element.267, pred[8,12]{1,0:T(8,128)(4,1)S(1)} %iota_compare_fusion.3, f32[8,128]{1,0:T(8,128)S(1)} %fusion.64), kind=kOutput, calls=%fused_computation.16.clone.1 | convolution fusion | flops 410779648 | bytes 9707616 | tf_op jit(solution)/shard_map/while/body/gqjk,gjkd->gqd/dot_general | solution.py:87
  297.2 2.3 scatter_fusion
  301.2 4.6 %gather_fusion.3 = bf16[96,128,128]{2,1,0:T(8,128)(2,1)S(1)} fusion(bf16[4,3,16,128,128]{4,3,2,1,0:T(8,128)(2,1)} %get-tuple-element.297, s32[96]{0:T(128)S(1)} %reshape.352), kind=kCustom, calls=%fused_computation.3.clone.1 | custom fusion | bytes 6292608 | tf_op jit(solution)/shard_map/while/body/gather | solution.py:72
  306.5 3.4 gather_fusion.4
  313.7 4.6 %gather_fusion.1 = bf16[96,128,128]{2,1,0:T(8,128)(2,1)S(1)} fusion(bf16[4,3,16,128,128]{4,3,2,1,0:T(8,128)(2,1)} %get-tuple-element.297, s32[96]{0:T(128)S(1)} %reshape.351), kind=kCustom, calls=%fused_computation.4.clone.1 | custom fusion | bytes 6292608 | tf_op jit(solution)/shard_map/while/body/gather | solution.py:73
  318.3 4.9 %fusion.65 = bf16[8,128,128]{2,1,0:T(8,128)(2,1)S(1)} fusion(bf16[8,12,128,128]{3,2,1,0:T(8,128)(2,1)S(1)} %bitcast.80, f32[8,128,12,128]{1,3,2,0:T(8,128)} %copy-done.1, f32[8,128]{1,0:T(8,128)S(1)} %get-tuple-element.267, pred[8,12]{1,0:T(8,128)(4,1)S(1)} %iota_compare_fusion.3, f32[8,128]{1,0:T(8,128)S(1)} %fusion.64), kind=kOutput, calls=%fused_computation.16.clone.1 | convolution fusion | flops 410779648 | bytes 9707616 | tf_op jit(solution)/shard_map/while/body/gqjk,gjkd->gqd/dot_general | solution.py:87
  327.2 4.6 %gather_fusion.3 = bf16[96,128,128]{2,1,0:T(8,128)(2,1)S(1)} fusion(bf16[4,3,16,128,128]{4,3,2,1,0:T(8,128)(2,1)} %get-tuple-element.297, s32[96]{0:T(128)S(1)} %reshape.352), kind=kCustom, calls=%fused_computation.3.clone.1 | custom fusion | bytes 6292608 | tf_op jit(solution)/shard_map/while/body/gather | solution.py:72
  332.6 3.4 gather_fusion.4
  339.7 4.6 %gather_fusion.1 = bf16[96,128,128]{2,1,0:T(8,128)(2,1)S(1)} fusion(bf16[4,3,16,128,128]{4,3,2,1,0:T(8,128)(2,1)} %get-tuple-element.297, s32[96]{0:T(128)S(1)} %reshape.351), kind=kCustom, calls=%fused_computation.4.clone.1 | custom fusion | bytes 6292608 | tf_op jit(solution)/shard_map/while/body/gather | solution.py:73
  344.3 4.9 %fusion.65 = bf16[8,128,128]{2,1,0:T(8,128)(2,1)S(1)} fusion(bf16[8,12,128,128]{3,2,1,0:T(8,128)(2,1)S(1)} %bitcast.80, f32[8,128,12,128]{1,3,2,0:T(8,128)} %copy-done.1, f32[8,128]{1,0:T(8,128)S(1)} %get-tuple-element.267, pred[8,12]{1,0:T(8,128)(4,1)S(1)} %iota_compare_fusion.3, f32[8,128]{1,0:T(8,128)S(1)} %fusion.64), kind=kOutput, calls=%fused_computation.16.clone.1 | convolution fusion | flops 410779648 | bytes 9707616 | tf_op jit(solution)/shard_map/while/body/gqjk,gjkd->gqd/dot_general | solution.py:87
  351.5 4.7 %copy.49 = bf16[4,16,128,128]{3,0,2,1:T(4,128)(2,1)} copy(bf16[4,16,128,128]{3,2,1,0:T(8,128)(2,1)} %get-tuple-element.124) | data formatting | bytes 4194304 | tf_op jit(solution)/shard_map/while | solution.py:98
  356.2 36.5 %all-to-all-start.1 = ((bf16[4,2048,128]{2,0,1:T(4,128)(2,1)}), bf16[4,2048,128]{2,0,1:T(4,128)(2,1)S(1)}, u32[]{:S(2)}, u32[]{:S(2)}) async-start(bf16[4,2048,128]{2,0,1:T(4,128)(2,1)} %bitcast.83), calls=%async_computation.1 | async-start | bytes 4194304 | tf_op jit(solution)/shard_map/all_to_all | solution.py:100
  392.9 40.9 %all-to-all-done.1 = bf16[4,2048,128]{2,0,1:T(4,128)(2,1)S(1)} async-done(((bf16[4,2048,128]{2,0,1:T(4,128)(2,1)}), bf16[4,2048,128]{2,0,1:T(4,128)(2,1)S(1)}, u32[]{:S(2)}, u32[]{:S(2)}) %all-to-all-start.1) | async-done | bytes 2097184 | tf_op jit(solution)/shard_map/all_to_all | solution.py:100
  (104 shorter events, 62.5 us)
Async XLA Ops:
  0.0 2.5 copy-start.4
  4.7 3.9 copy-start.5
  12.3 3.4 copy-start.2
  53.6 7.6 %copy-start.3 = (s32[40,16,12]{0,1,2:T(8,128)S(1)}, s32[40,16,12]{0,1,2:T(8,128)}, u32[]{:S(2)}) copy-start(s32[40,16,12]{0,1,2:T(8,128)} %param.14) | copy-start | bytes 92164
  53.6 158.3 %all-to-all-start = ((bf16[12,2048,128]{2,0,1:T(8,128)(2,1)}), bf16[12,2048,128]{2,0,1:T(8,128)(2,1)}, u32[]{:S(2)}, u32[]{:S(2)}) async-start(bf16[12,2048,128]{2,0,1:T(8,128)(2,1)} %copy.46), calls=%async_computation | async-start | bytes 16777216 | tf_op jit(solution)/shard_map/all_to_all | solution.py:54
  62.2 159.3 %copy-start = (s32[40,16]{0,1:T(8,128)S(1)}, s32[40,16]{0,1:T(8,128)}, u32[]{:S(2)}) copy-start(s32[40,16]{0,1:T(8,128)} %param.15) | copy-start | bytes 7684
  233.0 2.7 copy-start.1
  259.0 2.7 copy-start.1
  285.0 2.7 copy-start.1
  311.0 2.7 copy-start.1
  337.0 2.7 copy-start.1
  356.2 77.6 %all-to-all-start.1 = ((bf16[4,2048,128]{2,0,1:T(4,128)(2,1)}), bf16[4,2048,128]{2,0,1:T(4,128)(2,1)S(1)}, u32[]{:S(2)}, u32[]{:S(2)}) async-start(bf16[4,2048,128]{2,0,1:T(4,128)(2,1)} %bitcast.83), calls=%async_computation.1 | async-start | bytes 4194304 | tf_op jit(solution)/shard_map/all_to_all | solution.py:100
where the time goes:
time: 445 us; the launch traced here: 438 us
  waiting for transfers between devices  191 us (43%)
  local copies, waits for them, and re-layouts  152 us (34%)
  starting transfers between devices  44.1 us (10%)
  matrix products  30.2 us (7%)
  other arithmetic  19.9 us (4%)
    all_to_all x1, waiting for transfers between devices, local(): lax.all_to_all(outgoing, 'ulysses', split_axis=1, concat_axis=1, tiled=True)  150 us
    all_to_all x1, waiting for transfers between devices, local(): lax.all_to_all(leaving, 'ulysses', split_axis=1, concat_axis=0, tiled=True)  40.9 us
    all_to_all x1, starting transfers between devices, local(): lax.all_to_all(leaving, 'ulysses', split_axis=1, concat_axis=0, tiled=True)  36.5 us
    dot_general x5, matrix products, attend_group(): jnp.einsum('gqjk,gjkd->gqd', weights.astype(jnp.bfloat16), value_panels,...  24.4 us
    reshape x1, local copies, waits for them, and re-layouts, local(): outgoing = packed[owner_heads.T].transpose(0, 2, 1, 3, 4).reshape(span_he...  24.2 us
    gather x5, local copies, waits for them, and re-layouts, attend_group(): key_panels = resident[unit_slots[:, None], 1, key_lists]  22.9 us
    gather x5, local copies, waits for them, and re-layouts, attend_group(): value_panels = resident[unit_slots[:, None], 2, key_lists]  22.9 us
    gather x5, local copies, waits for them, and re-layouts, attend_group(): query_matrix = resident[unit_slots, 0, qblock]  17 us
  transfers between devices with their start and end apart: 2, of which 2 were waited for; matrix products, arithmetic and copies ran while one was open for 0% of the time, Pallas kernels for 0%

commit v1 on v0

--- a/solution.py
+++ b/solution.py
@@ -1,15 +1,31 @@
+import functools
+import math
+
 import jax
 import jax.numpy as jnp
 from jax import lax
+from jax.experimental import pallas as pl
+from jax.experimental.pallas import tpu as pltpu
 from jax.sharding import PartitionSpec as P
 
 HEADS = 40
 HEAD_DIM = 128
 TILE = 128
 KMAX = 12
-
+HALF = TILE // 2
 
 NORM_EPS = 1e-06
+MASKED = -1e30
+EXP2_SCALE = HEAD_DIM ** (-0.5) * math.log2(math.e)
+UNROLLS = (1, 2, 3, 4, 6, 8, 10, 12)
+VMEM_LIMIT = 48 * 1024 * 1024
+
+ROWS_X = 3 * TILE + HALF + TILE
+ROWS_Y = 3 * TILE
+
+ANY = pl.BlockSpec(memory_space=pl.ANY)
+SMEM = pl.BlockSpec(memory_space=pltpu.SMEM)
+VMEM = pl.BlockSpec(memory_space=pltpu.VMEM)
 
 
 def rms_norm(values_in, gain):
@@ -18,13 +34,364 @@
     return (widened * inverse * gain).astype(jnp.bfloat16)
 
 
+def head_of(device, which, heads_pair):
+    base = (device // 2) * heads_pair
+    core = device % 2
+    if which == 2:
+        return base + 2
+    return base + core * 3 + which
+
+
+def lanes_of(head):
+    return pl.ds(pl.multiple_of(head * HEAD_DIM, HEAD_DIM), HEAD_DIM)
+
+
+def partner_order(devices):
+    half = devices // 2
+    far = list(range(half, devices))
+    near = list(range(1, half))
+    order = []
+    for index in range(half):
+        order.append(far[index])
+        if index < len(near):
+            order.append(near[index])
+    return order
+
+
+def pack_kernel(devices, heads_pair, me_ref, q_ref, k_ref, v_ref, qg_ref, kg_ref, *rest):
+    x_refs, y_refs = rest[:devices], rest[devices : 2 * devices]
+    q_norm, k_norm = rest[2 * devices :]
+    me = me_ref[0]
+    width = q_ref.shape[1]
+    step = 8 * HEAD_DIM
+    for src, gain, dst in ((q_ref, qg_ref, q_norm), (k_ref, kg_ref, k_norm)):
+        total = jnp.zeros((TILE, HEAD_DIM), jnp.float32)
+        for lane in range(0, width, HEAD_DIM):
+            part = src[:, lane : lane + HEAD_DIM].astype(jnp.float32)
+            total += part * part
+        mean = jnp.sum(total, axis=1, keepdims=True) * (1.0 / width)
+        inverse = lax.rsqrt(mean + NORM_EPS)
+        for lane in range(0, width, step):
+            part = src[:, lane : lane + step].astype(jnp.float32)
+            dst[:, lane : lane + step] = (part * inverse * gain[:, lane : lane + step]).astype(
+                jnp.bfloat16
+            )
+    for mask in range(devices):
+        to = lax.bitwise_xor(me, mask)
+        core = to % 2
+        first = lanes_of(head_of(to, 0, heads_pair))
+        second = lanes_of(head_of(to, 1, heads_pair))
+        shared = lanes_of(head_of(to, 2, heads_pair))
+        x_out, y_out = x_refs[mask], y_refs[mask]
+        x_out[0:TILE] = q_norm[:, first]
+        x_out[TILE : 2 * TILE] = k_norm[:, first]
+        x_out[2 * TILE : 3 * TILE] = v_ref[:, first]
+        half = pl.ds(pl.multiple_of(core * HALF, HALF), HALF)
+        x_out[3 * TILE : 3 * TILE + HALF] = q_norm[half, shared]
+
+        @pl.when(core == 0)
+        def _():
+            x_out[3 * TILE + HALF : ROWS_X] = k_norm[:, shared]
+
+        @pl.when(core == 1)
+        def _():
+            x_out[3 * TILE + HALF : ROWS_X] = v_ref[:, shared]
+
+        y_out[0:TILE] = q_norm[:, second]
+        y_out[TILE : 2 * TILE] = k_norm[:, second]
+        y_out[2 * TILE : 3 * TILE] = v_ref[:, second]
+
+
+def pack(me, query, key, value, query_gain, key_gain, devices, heads_pair):
+    shapes = [jax.ShapeDtypeStruct((ROWS_X, HEAD_DIM), jnp.bfloat16)] * devices
+    shapes += [jax.ShapeDtypeStruct((ROWS_Y, HEAD_DIM), jnp.bfloat16)] * devices
+    outs = pl.pallas_call(
+        functools.partial(pack_kernel, devices, heads_pair),
+        out_shape=shapes,
+        in_specs=[SMEM] + [VMEM] * 5,
+        out_specs=[VMEM] * (2 * devices),
+        scratch_shapes=[pltpu.VMEM(query.shape, jnp.bfloat16)] * 2,
+        compiler_params=pltpu.CompilerParams(vmem_limit_bytes=VMEM_LIMIT),
+        name="norm_pack",
+    )(me, query, key, value, query_gain[None, :], key_gain[None, :])
+    return outs[:devices], outs[devices:]
+
+
+def collect_kernel(devices, me_ref, *rest):
+    x_refs, out_ref, sems = rest[:devices], rest[devices], rest[devices + 1]
+    me = me_ref[0]
+    copies = []
+    for mask in range(devices):
+        copies.append(
+            pltpu.make_async_copy(
+                x_refs[mask].at[pl.ds(3 * TILE + HALF, TILE)],
+                out_ref.at[lax.bitwise_xor(me, mask)],
+                sems.at[mask],
+            )
+        )
+    for copy in copies:
+        copy.start()
+    for copy in copies:
+        copy.wait()
+
+
+def collect(me, x_in, devices):
+    return pl.pallas_call(
+        functools.partial(collect_kernel, devices),
+        out_shape=jax.ShapeDtypeStruct((devices, TILE, HEAD_DIM), jnp.bfloat16),
+        in_specs=[SMEM] + [ANY] * devices,
+        out_specs=ANY,
+        scratch_shapes=[pltpu.SemaphoreType.DMA((devices,))],
+        name="collect_shared",
+    )(me, *x_in)
+
+
+def attend_unit(count, list_at, query_of, key_of, value_of, store):
+    least = 0
+    for size in UNROLLS:
+
+        @pl.when((count > least) & (count <= size))
+        def _(size=size, least=least):
+            blocks = [list_at(slot) for slot in range(size)]
+            query = query_of()
+            keys = jnp.concatenate([key_of(block) for block in blocks], axis=0)
+            scores = lax.dot_general(
+                query, keys, (((1,), (1,)), ((), ())), preferred_element_type=jnp.float32
+            )
+            if size > least + 1:
+                column = lax.broadcasted_iota(jnp.int32, scores.shape, 1)
+                scores = jnp.where(column < count * TILE, scores, MASKED)
+            peak = jnp.max(scores, axis=1, keepdims=True)
+            weights = jnp.exp2((scores - peak) * EXP2_SCALE)
+            total = jnp.sum(weights, axis=1, keepdims=True)
+            values = jnp.concatenate([value_of(block) for block in blocks], axis=0)
+            summed = jnp.dot(
+                weights.astype(jnp.bfloat16), values, preferred_element_type=jnp.float32
+            )
+            store((summed / total).astype(jnp.bfloat16))
+
+        least = size
+
+
+def load_all(me, refs, held, sems):
+    copies = [
+        pltpu.make_async_copy(ref, held.at[lax.bitwise_xor(me, mask)], sems.at[mask])
+        for mask, ref in enumerate(refs)
+    ]
+    for copy in copies:
+        copy.start()
+    return copies
+
+
+def send_all(me, held, refs, sems):
+    copies = [
+        pltpu.make_async_copy(held.at[lax.bitwise_xor(me, mask)], ref, sems.at[mask])
+        for mask, ref in enumerate(refs)
+    ]
+    for copy in copies:
+        copy.start()
+    for copy in copies:
+        copy.wait()
+
+
+def attend_x_kernel(
+    devices, me_ref, lists_ref, counts_ref, shared_lists_ref, shared_counts_ref, *rest
+):
+    x_refs = rest[:devices]
+    own_ref, other_ref = rest[devices : devices + 2]
+    out_refs = rest[devices + 2 : 2 * devices + 2]
+    held, shared, results, sems, shared_sems, out_sems = rest[2 * devices + 2 :]
+    me = me_ref[0]
+    core = me % 2
+    copies = load_all(me, x_refs, held, sems)
+    own = pltpu.make_async_copy(own_ref, shared.at[core], shared_sems.at[0])
+    other = pltpu.make_async_copy(other_ref, shared.at[1 - core], shared_sems.at[1])
+    own.start()
+    other.start()
+    for copy in copies:
+        copy.wait()
+    own.wait()
+    other.wait()
+
+    def step(block, carry):
+        def store(values):
+            results[block, 0:TILE] = values
+
+        def store_shared(values):
+            results[block, TILE : TILE + HALF] = values
+
+        attend_unit(
+            counts_ref[block],
+            lambda slot: lists_ref[block * KMAX + slot],
+            lambda: held[block, 0:TILE],
+            lambda at: held[at, TILE : 2 * TILE],
+            lambda at: held[at, 2 * TILE : 3 * TILE],
+            store,
+        )
+        attend_unit(
+            shared_counts_ref[block],
+            lambda slot: shared_lists_ref[block * KMAX + slot],
+            lambda: held[block, 3 * TILE : 3 * TILE + HALF],
+            lambda at: shared[0, at],
+            lambda at: shared[1, at],
+            store_shared,
+        )
+        return carry
+
+    lax.fori_loop(0, devices, step, 0)
+    send_all(me, results, out_refs, out_sems)
+
+
+def attend_y_kernel(devices, me_ref, lists_ref, counts_ref, *rest):
+    y_refs = rest[:devices]
+    out_refs = rest[devices : 2 * devices]
+    held, results, sems, out_sems = rest[2 * devices :]
+    me = me_ref[0]
+    for copy in load_all(me, y_refs, held, sems):
+        copy.wait()
+
+    def step(block, carry):
+        def store(values):
+            results[block] = values
+
+        attend_unit(
+            counts_ref[block],
+            lambda slot: lists_ref[block * KMAX + slot],
+            lambda: held[block, 0:TILE],
+            lambda at: held[at, TILE : 2 * TILE],
+            lambda at: held[at, 2 * TILE : 3 * TILE],
+            store,
+        )
+        return carry
+
+    lax.fori_loop(0, devices, step, 0)
+    send_all(me, results, out_refs, out_sems)
+
+
+def attend_cost(units):
+    return pl.CostEstimate(
+        flops=units * 4 * 4 * TILE * TILE * HEAD_DIM,
+        bytes_accessed=units * 4 * TILE * HEAD_DIM * 2,
+        transcendentals=units * 4 * TILE * TILE,
+    )
+
+
+def attend_x(me, tables, x_in, own, other, devices):
+    rows = TILE + HALF
+    return pl.pallas_call(
+        functools.partial(attend_x_kernel, devices),
+        out_shape=[jax.ShapeDtypeStruct((rows, HEAD_DIM), jnp.bfloat16)] * devices,
+        in_specs=[SMEM] * 5 + [ANY] * (devices + 2),
+        out_specs=[ANY] * devices,
+        scratch_shapes=[
+            pltpu.VMEM((devices, ROWS_X, HEAD_DIM), jnp.bfloat16),
+            pltpu.VMEM((2, devices, TILE, HEAD_DIM), jnp.bfloat16),
+            pltpu.VMEM((devices, rows, HEAD_DIM), jnp.bfloat16),
+            pltpu.SemaphoreType.DMA((devices,)),
+            pltpu.SemaphoreType.DMA((2,)),
+            pltpu.SemaphoreType.DMA((devices,)),
+        ],
+        compiler_params=pltpu.CompilerParams(vmem_limit_bytes=VMEM_LIMIT),
+        cost_estimate=attend_cost(24),
+        name="attend_x",
+    )(me, *tables, *x_in, own, other)
+
+
+def attend_y(me, tables, y_in, devices):
+    return pl.pallas_call(
+        functools.partial(attend_y_kernel, devices),
+        out_shape=[jax.ShapeDtypeStruct((TILE, HEAD_DIM), jnp.bfloat16)] * devices,
+        in_specs=[SMEM] * 3 + [ANY] * devices,
+        out_specs=[ANY] * devices,
+        scratch_shapes=[
+            pltpu.VMEM((devices, ROWS_Y, HEAD_DIM), jnp.bfloat16),
+            pltpu.VMEM((devices, TILE, HEAD_DIM), jnp.bfloat16),
+            pltpu.SemaphoreType.DMA((devices,)),
+            pltpu.SemaphoreType.DMA((devices,)),
+        ],
+        compiler_params=pltpu.CompilerParams(vmem_limit_bytes=VMEM_LIMIT),
+        cost_estimate=attend_cost(16),
+        name="attend_y",
+    )(me, *tables, *y_in)
+
+
+def assemble_kernel(devices, heads_pair, me_ref, *rest):
+    x_refs, y_refs = rest[:devices], rest[devices : 2 * devices]
+    out_ref, sems = rest[2 * devices :]
+    me = me_ref[0]
+    copies = []
+
+    def add(src, dst):
+        copies.append(pltpu.make_async_copy(src, dst, sems.at[len(copies)]))
+
+    for mask in range(devices):
+        source = lax.bitwise_xor(me, mask)
+        core = source % 2
+        first = lanes_of(head_of(source, 0, heads_pair))
+        second = lanes_of(head_of(source, 1, heads_pair))
+        shared = lanes_of(head_of(source, 2, heads_pair))
+        half = pl.ds(pl.multiple_of(core * HALF, HALF), HALF)
+        add(x_refs[mask].at[pl.ds(0, TILE)], out_ref.at[:, first])
+        add(x_refs[mask].at[pl.ds(TILE, HALF)], out_ref.at[half, shared])
+        add(y_refs[mask], out_ref.at[:, second])
+    for copy in copies:
+        copy.start()
+    for copy in copies:
+        copy.wait()
+
+
+def assemble(me, x_back, y_back, width, devices, heads_pair):
+    return pl.pallas_call(
+        functools.partial(assemble_kernel, devices, heads_pair),
+        out_shape=jax.ShapeDtypeStruct((TILE, width), jnp.bfloat16),
+        in_specs=[SMEM] + [ANY] * (2 * devices),
+        out_specs=ANY,
+        scratch_shapes=[pltpu.SemaphoreType.DMA((3 * devices,))],
+        name="assemble",
+    )(me, *x_back, *y_back)
+
+
+def exchange(parts, devices):
+    arrived = [None] * devices
+    arrived[0] = parts[0]
+    for mask in partner_order(devices):
+        arrived[mask] = lax.ppermute(
+            parts[mask], "ulysses", [(index, index ^ mask) for index in range(devices)]
+        )
+    return arrived
+
+
+def local_pairs(query, key, value, query_gain, key_gain, key_blocks, block_counts):
+    devices = lax.axis_size("ulysses")
+    heads_pair = 2 * HEADS // devices
+    index = lax.axis_index("ulysses")
+    me = index.astype(jnp.int32).reshape(1)
+
+    def tables(which):
+        head = head_of(index, which, heads_pair)
+        lists = lax.dynamic_index_in_dim(key_blocks, head, 0, False).reshape(-1)
+        counts = lax.dynamic_index_in_dim(block_counts, head, 0, False)
+        return lists, counts
+
+    x_out, y_out = pack(me, query, key, value, query_gain, key_gain, devices, heads_pair)
+    x_in = exchange(x_out, devices)
+    y_in = exchange(y_out, devices)
+    own = collect(me, x_in, devices)
+    other = lax.ppermute(own, "ulysses", [(at, at ^ 1) for at in range(devices)])
+    x_results = attend_x(me, tables(0) + tables(2), x_in, own, other, devices)
+    x_back = exchange(x_results, devices)
+    y_results = attend_y(me, tables(1), y_in, devices)
+    y_back = exchange(y_results, devices)
+    return assemble(me, x_back, y_back, query.shape[1], devices, heads_pair)
+
+
 def pick_group():
     for group_size in (8, 4, 2, 1):
         return group_size
     return 1
 
 
-def local(query, key, value, query_gain, key_gain, key_blocks, block_counts):
+def local_any(query, key, value, query_gain, key_gain, key_blocks, block_counts):
     devices = lax.axis_size("ulysses")
     my_index = lax.axis_index("ulysses")
     tok_dev = query.shape[0]
@@ -80,7 +447,7 @@
         live_mask = (jnp.arange(KMAX, dtype=jnp.int32)[None, :] < live_count[:, None])[
             :, None, :, None
         ]
-        logit_matrix = jnp.where(live_mask, logit_matrix, -1e30)
+        logit_matrix = jnp.where(live_mask, logit_matrix, MASKED)
         row_peak = jnp.max(logit_matrix, axis=(2, 3), keepdims=True)
         weights = jnp.where(live_mask, jnp.exp(logit_matrix - row_peak), 0.0)
         row_denominator = jnp.sum(weights, axis=(2, 3))
@@ -102,6 +469,15 @@
     selector = (owner_heads.reshape(-1)[None, :] == head_range[:, None]).astype(jnp.bfloat16)
     gathered = jnp.einsum("hs,std->thd", selector, returned, preferred_element_type=jnp.float32)
     return gathered.astype(jnp.bfloat16).reshape(tok_dev, HEADS * HEAD_DIM)
+
+
+def local(query, *rest):
+    devices = lax.axis_size("ulysses")
+    power_of_two = devices & (devices - 1) == 0
+    five_a_pair = devices % 2 == 0 and devices * 5 == HEADS * 2
+    if power_of_two and five_a_pair and query.shape[0] == TILE:
+        return local_pairs(query, *rest)
+    return local_any(query, *rest)
 
 
 def solution(mesh):

time: 445 us -> 278 us (0.62); the launches traced: 438 us -> 276 us
  waiting for transfers between devices: 191 us -> 23.2 us
  local copies, waits for them, and re-layouts: 152 us -> 32 us
  Pallas kernels: 0 us -> 95.2 us
  starting transfers between devices: 44.1 us -> 125 us
  matrix products: 30.2 us -> 0 us
  other arithmetic: 19.9 us -> 0 us
    all_to_all x2 -> x0, waiting for transfers between devices: 191 us -> none  [the longest x1 150 us: local(): lax.all_to_all(outgoing, 'ulysses', split_axis=1, concat_axis=1, tiled=True)]
    ppermute x0 -> x61, starting transfers between devices: none -> 125 us  [the longest x60 124 us: exchange(): lax.ppermute(parts[mask], 'ulysses', [(index, index ^ mask) for index in...]
    pallas_call x0 -> x5, Pallas kernels: none -> 95.2 us  [the longest x1 41.2 us: assemble(): pl.pallas_call(functools.partial(assemble_kernel, devices, heads_pair), o...]
    gather x27 -> x0, local copies, waits for them, and re-layouts: 84 us -> none  [the longest x5 22.9 us: attend_group(): key_panels = resident[unit_slots[:, None], 1, key_lists]]
    all_to_all x2 -> x0, starting transfers between devices: 44.1 us -> none  [the longest x1 36.5 us: local(): lax.all_to_all(leaving, 'ulysses', split_axis=1, concat_axis=0, tiled=True)]
    dot_general x11 -> x0, matrix products: 30.2 us -> none  [the longest x5 24.4 us: attend_group(): jnp.einsum('gqjk,gjkd->gqd', weights.astype(jnp.bfloat16), value_panels,...]
    reshape x1 -> x3, local copies, waits for them, and re-layouts: 24.2 us -> 0.95 us  [tables(): lists = lax.dynamic_index_in_dim(key_blocks, head, 0, False).reshape(-1)]
    ppermute x0 -> x61, waiting for transfers between devices: none -> 23.2 us  [the longest x60 23.2 us: exchange(): lax.ppermute(parts[mask], 'ulysses', [(index, index ^ mask) for index in...]
  transfers between devices with their start and end apart: 2 -> 61, of which waited for: 2 -> 13; matrix products, arithmetic and copies ran while one was open for 0% -> 3% of each run, Pallas kernels for 0% -> 18%
where the time goes in v1:
time: 278 us; the launch traced here: 276 us
  starting transfers between devices  125 us (45%)
  Pallas kernels  95.2 us (34%)
  local copies, waits for them, and re-layouts  32 us (12%)
  waiting for transfers between devices  23.2 us (8%)
    ppermute x60, starting transfers between devices, exchange(): lax.ppermute(parts[mask], 'ulysses', [(index, index ^ mask) for index in...  124 us
    pallas_call x1, Pallas kernels, assemble(): pl.pallas_call(functools.partial(assemble_kernel, devices, heads_pair), o...  41.2 us
    unnamed x182, local copies, waits for them, and re-layouts  24.9 us
    ppermute x60, waiting for transfers between devices, exchange(): lax.ppermute(parts[mask], 'ulysses', [(index, index ^ mask) for index in...  23.2 us
    pallas_call x1, Pallas kernels, attend_x(): pl.pallas_call(functools.partial(attend_x_kernel, devices), out_shape=[ja...  19.5 us
    pallas_call x1, Pallas kernels, collect(): pl.pallas_call(functools.partial(collect_kernel, devices), out_shape=jax....  17.1 us
    pallas_call x1, Pallas kernels, attend_y(): pl.pallas_call(functools.partial(attend_y_kernel, devices), out_shape=[ja...  12.2 us
    dynamic_slice x4, local copies, waits for them, and re-layouts, tables(): lists = lax.dynamic_index_in_dim(key_blocks, head, 0, False).reshape(-1)  5.91 us
  transfers between devices with their start and end apart: 61, of which 13 were waited for; matrix products, arithmetic and copies ran while one was open for 3% of the time, Pallas kernels for 18%

profile of v1, /device:TPU:0, one launch (start us, length us, event | category | flops | bytes accessed | tf_op | source)
XLA Modules:
  0.0 276.5 jit_solution(13170031946985793037)
XLA Ops:
  2.8 5.2 %norm_pack.1 = (bf16[576,128]{1,0:T(8,128)(2,1)S(1)}, bf16[576,128]{1,0:T(8,128)(2,1)S(1)}, bf16[576,128]{1,0:T(8,128)(2,1)S(1)}, bf16[576,128]{1,0:T(8,128)(2,1...) custom-call(s32[1]{0:T(128)} %bitcast.me_ref, ...), custom_call_target="tpu_custom_call" | custom-call | tf_op jit(solution)/shard_map/norm_pack/pallas_call | solution.py:108
  10.3 2.5 collective-permute-start.1
  14.8 2.6 collective-permute-start.5
  20.3 2.6 collective-permute-start.7
  23.1 3.5 %collective-permute-start.9 = (bf16[576,128]{1,0:T(8,128)(2,1)S(1)}, bf16[576,128]{1,0:T(8,128)(2,1)S(1)}, u32[]{:S(2)}, u32[]{:S(2)}) collective-permute-start(bf16[576,128]{1,0:T(8,128)(2,1)S(1)} %get-tuple-element.79), channel_id=1, source_target_pairs={{0,10},{1,11},{2,8},{3,9},{4,14},{5,15},{6,12},{7,13},{8,2},{9,3},... | collective-permute-start | bytes 442376 | tf_op jit(solution)/shard_map/ppermute | solution.py:358
  26.7 6.9 %collective-permute-done.5.rest_6_ = bf16[576,128]{1,0:T(8,128)(2,1)S(1)} collective-permute-done((bf16[576,128]{1,0:T(8,128)(2,1)S(1)}, bf16[576,128]{1,0:T(8,128)(2,1)S(1)}, u32[]{:S(2)}, u32[]{:S(2)}) %collective-permute-start.5) | collective-permute-done | bytes 147488 | tf_op jit(solution)/shard_map/ppermute | solution.py:358
  36.8 2.3 collective-permute-start.12
  39.0 14.8 %collective-permute-start.13 = (bf16[576,128]{1,0:T(8,128)(2,1)S(1)}, bf16[576,128]{1,0:T(8,128)(2,1)S(1)}, u32[]{:S(2)}, u32[]{:S(2)}) collective-permute-start(bf16[576,128]{1,0:T(8,128)(2,1)S(1)} %get-tuple-element.83), channel_id=1, source_target_pairs={{0,14},{1,15},{2,12},{3,13},{4,10},{5,11},{6,8},{7,9},{8,6},{9,7},... | collective-permute-start | bytes 442376 | tf_op jit(solution)/shard_map/ppermute | solution.py:358
  54.2 2.5 collective-permute-start.14
  56.7 3.1 %collective-permute-done.10.rest_11_ = bf16[576,128]{1,0:T(8,128)(2,1)S(1)} collective-permute-done((bf16[576,128]{1,0:T(8,128)(2,1)S(1)}, bf16[576,128]{1,0:T(8,128)(2,1)S(1)}, u32[]{:S(2)}, u32[]{:S(2)}) %collective-permute-start.10) | collective-permute-done | bytes 147488 | tf_op jit(solution)/shard_map/ppermute | solution.py:358
  59.7 3.8 %collective-permute-start.31 = (bf16[384,128]{1,0:T(8,128)(2,1)}, bf16[384,128]{1,0:T(8,128)(2,1)S(1)}, u32[]{:S(2)}, u32[]{:S(2)}) collective-permute-start(bf16[384,128]{1,0:T(8,128)(2,1)} %get-tuple-element.102), channel_id=1, source_target_pairs={{0,1},{1,0},{2,3},{3,2},{4,5},{5,4},{6,7},{7,6},{8,9},{9,8},{10,11... | collective-permute-start | bytes 294920 | tf_op jit(solution)/shard_map/ppermute | solution.py:358
  65.7 17.1 %collect_shared.1.rest_16_ = bf16[16,128,128]{2,1,0:T(8,128)(2,1)} custom-call(s32[1]{0:T(128)} %bitcast.me_ref, bf16[576,128]{1,0:T(8,128)(2,1)} %copy-done.2, bf16[576,128]{1,0:T(8,128)(2,1)} %copy-done.4, bf16[576,128]{1,0:T(8,128)(2,1)} %copy-done.6, bf16[576,128]{1,0:T(8,128)(2,1)} %copy-done.8, bf16[576,128]{1,0:T(8,128)(2,1)} %copy-done.10, ...), custom_call_target="tpu_custom_call" | custom-call | tf_op jit(solution)/shard_map/collect_shared/pallas_call | solution.py:139
  83.6 10.7 %collective-permute-start.34 = (bf16[384,128]{1,0:T(8,128)(2,1)}, bf16[384,128]{1,0:T(8,128)(2,1)S(1)}, u32[]{:S(2)}, u32[]{:S(2)}) collective-permute-start(bf16[384,128]{1,0:T(8,128)(2,1)} %copy-done.53), channel_id=1, source_target_pairs={{0,4},{1,5},{2,6},{3,7},{4,0},{5,1},{6,2},{7,3},{8,12},{9,13},{10,... | collective-permute-start | bytes 294920 | tf_op jit(solution)/shard_map/ppermute | solution.py:358
  95.6 2.2 collective-permute-start.36
  98.6 4.3 %collective-permute-start.38 = (bf16[384,128]{1,0:T(8,128)(2,1)S(1)}, bf16[384,128]{1,0:T(8,128)(2,1)S(1)}, u32[]{:S(2)}, u32[]{:S(2)}) collective-permute-start(bf16[384,128]{1,0:T(8,128)(2,1)S(1)} %get-tuple-element.109), channel_id=1, source_target_pairs={{0,8},{1,9},{2,10},{3,11},{4,12},{5,13},{6,14},{7,15},{8,0},{9,1},... | collective-permute-start | bytes 294920 | tf_op jit(solution)/shard_map/ppermute | solution.py:358
  105.3 2.6 collective-permute-start.40
  110.5 7.4 %collective-permute-start.42 = (bf16[384,128]{1,0:T(8,128)(2,1)}, bf16[384,128]{1,0:T(8,128)(2,1)}, u32[]{:S(2)}, u32[]{:S(2)}) collective-permute-start(bf16[384,128]{1,0:T(8,128)(2,1)} %get-tuple-element.113), channel_id=1, source_target_pairs={{0,12},{1,13},{2,14},{3,15},{4,8},{5,9},{6,10},{7,11},{8,4},{9,5},... | collective-permute-start | bytes 294920 | tf_op jit(solution)/shard_map/ppermute | solution.py:358
  119.4 2.6 collective-permute-done.40.rest_10_
  124.7 4.1 %collective-permute-start.45 = (bf16[384,128]{1,0:T(8,128)(2,1)}, bf16[384,128]{1,0:T(8,128)(2,1)}, u32[]{:S(2)}, u32[]{:S(2)}) collective-permute-start(bf16[384,128]{1,0:T(8,128)(2,1)} %get-tuple-element.116), channel_id=1, source_target_pairs={{0,15},{1,14},{2,13},{3,12},{4,11},{5,10},{6,9},{7,8},{8,7},{9,6},... | collective-permute-start | bytes 294920 | tf_op jit(solution)/shard_map/ppermute | solution.py:358
  128.8 1.9 constant_dynamic-slice_fusion
  141.5 12.2 %attend_y.1 = (bf16[128,128]{1,0:T(8,128)(2,1)S(1)}, bf16[128,128]{1,0:T(8,128)(2,1)S(1)}, bf16[128,128]{1,0:T(8,128)(2,1)S(1)}, bf16[128,128]{1,0:T(8,128)(2,1)...) custom-call(s32[1]{0:T(128)} %bitcast.me_ref, ...), custom_call_target="tpu_custom_call" | custom-call | flops 536870912 | bytes 2097152 | tf_op jit(solution)/shard_map/attend_y/pallas_call | solution.py:301
  158.6 7.7 %collective-permute-start.49 = (bf16[128,128]{1,0:T(8,128)(2,1)S(1)}, bf16[128,128]{1,0:T(8,128)(2,1)S(1)}, u32[]{:S(2)}, u32[]{:S(2)}) collective-permute-start(bf16[128,128]{1,0:T(8,128)(2,1)S(1)} %get-tuple-element.121), channel_id=1, source_target_pairs={{0,4},{1,5},{2,6},{3,7},{4,0},{5,1},{6,2},{7,3},{8,12},{9,13},{10,... | collective-permute-start | bytes 98312 | tf_op jit(solution)/shard_map/ppermute | solution.py:358
  177.1 2.6 collective-permute-start.56
  184.9 2.8 collective-permute-start.60
  187.8 19.5 %attend_x.1 = (bf16[192,128]{1,0:T(8,128)(2,1)S(1)}, bf16[192,128]{1,0:T(8,128)(2,1)S(1)}, bf16[192,128]{1,0:T(8,128)(2,1)S(1)}, bf16[192,128]{1,0:T(8,128)(2,1)...) custom-call(s32[1]{0:T(128)} %bitcast.me_ref, ...), custom_call_target="tpu_custom_call" | custom-call | flops 805306368 | bytes 3145728 | tf_op jit(solution)/shard_map/attend_x/pallas_call | solution.py:281
  210.8 2.1 collective-permute-start.20
  215.4 2.7 collective-permute-start.24
  219.0 2.3 collective-permute-start.26
  223.0 2.2 collective-permute-start.28
  229.7 2.6 collective-permute-done.29.rest_14_
  232.3 2.2 collective-permute-done.30.rest_15_
  235.1 41.2 %assemble.1 = bf16[128,5120]{1,0:T(8,128)(2,1)} custom-call(s32[1]{0:T(128)} %bitcast.me_ref, bf16[192,128]{1,0:T(8,128)(2,1)} %copy-done.34, bf16[192,128]{1,0:T(8,128)(2,1)} %copy-done.65, bf16[192,128]{1,0:T(8,128)(2,1)} %copy-done.66, bf16[192,128]{1,0:T(8,128)(2,1)} %copy-done.67, bf16[192,128]{1,0:T(8,128)(2,1)} %copy-done.68, ...), custom_call_target="tpu_custom_call" | custom-call | tf_op jit(solution)/shard_map/assemble/pallas_call | solution.py:344
  (285 shorter events, 73.0 us)
Async XLA Ops:
  14.8 18.8 %collective-permute-start.5 = (bf16[576,128]{1,0:T(8,128)(2,1)S(1)}, bf16[576,128]{1,0:T(8,128)(2,1)S(1)}, u32[]{:S(2)}, u32[]{:S(2)}) collective-permute-start(bf16[576,128]{1,0:T(8,128)(2,1)S(1)} %get-tuple-element.75), channel_id=1, source_target_pairs={{0,6},{1,7},{2,4},{3,5},{4,2},{5,3},{6,0},{7,1},{8,14},{9,15},{10,... | collective-permute-start | bytes 442376 | tf_op jit(solution)/shard_map/ppermute | solution.py:358
  17.5 17.9 %collective-permute-start.6 = (bf16[576,128]{1,0:T(8,128)(2,1)S(1)}, bf16[576,128]{1,0:T(8,128)(2,1)S(1)}, u32[]{:S(2)}, u32[]{:S(2)}) collective-permute-start(bf16[576,128]{1,0:T(8,128)(2,1)S(1)} %get-tuple-element.76), channel_id=1, source_target_pairs={{0,7},{1,6},{2,5},{3,4},{4,3},{5,2},{6,1},{7,0},{8,15},{9,14},{10,... | collective-permute-start | bytes 442376 | tf_op jit(solution)/shard_map/ppermute | solution.py:358
  20.3 16.4 %collective-permute-start.7 = (bf16[576,128]{1,0:T(8,128)(2,1)S(1)}, bf16[576,128]{1,0:T(8,128)(2,1)S(1)}, u32[]{:S(2)}, u32[]{:S(2)}) collective-permute-start(bf16[576,128]{1,0:T(8,128)(2,1)S(1)} %get-tuple-element.77), channel_id=1, source_target_pairs={{0,8},{1,9},{2,10},{3,11},{4,12},{5,13},{6,14},{7,15},{8,0},{9,1},... | collective-permute-start | bytes 442376 | tf_op jit(solution)/shard_map/ppermute | solution.py:358
  22.9 16.1 %collective-permute-start.8 = (bf16[576,128]{1,0:T(8,128)(2,1)S(1)}, bf16[576,128]{1,0:T(8,128)(2,1)S(1)}, u32[]{:S(2)}, u32[]{:S(2)}) collective-permute-start(bf16[576,128]{1,0:T(8,128)(2,1)S(1)} %get-tuple-element.78), channel_id=1, source_target_pairs={{0,9},{1,8},{2,11},{3,10},{4,13},{5,12},{6,15},{7,14},{8,1},{9,0},... | collective-permute-start | bytes 442376 | tf_op jit(solution)/shard_map/ppermute | solution.py:358
  23.1 31.0 %collective-permute-start.9 = (bf16[576,128]{1,0:T(8,128)(2,1)S(1)}, bf16[576,128]{1,0:T(8,128)(2,1)S(1)}, u32[]{:S(2)}, u32[]{:S(2)}) collective-permute-start(bf16[576,128]{1,0:T(8,128)(2,1)S(1)} %get-tuple-element.79), channel_id=1, source_target_pairs={{0,10},{1,11},{2,8},{3,9},{4,14},{5,15},{6,12},{7,13},{8,2},{9,3},... | collective-permute-start | bytes 442376 | tf_op jit(solution)/shard_map/ppermute | solution.py:358
  33.6 26.2 %collective-permute-start.10 = (bf16[576,128]{1,0:T(8,128)(2,1)S(1)}, bf16[576,128]{1,0:T(8,128)(2,1)S(1)}, u32[]{:S(2)}, u32[]{:S(2)}) collective-permute-start(bf16[576,128]{1,0:T(8,128)(2,1)S(1)} %get-tuple-element.80), channel_id=1, source_target_pairs={{0,11},{1,10},{2,9},{3,8},{4,15},{5,14},{6,13},{7,12},{8,3},{9,2},... | collective-permute-start | bytes 442376 | tf_op jit(solution)/shard_map/ppermute | solution.py:358
  35.4 28.1 %collective-permute-start.11 = (bf16[576,128]{1,0:T(8,128)(2,1)S(1)}, bf16[576,128]{1,0:T(8,128)(2,1)S(1)}, u32[]{:S(2)}, u32[]{:S(2)}) collective-permute-start(bf16[576,128]{1,0:T(8,128)(2,1)S(1)} %get-tuple-element.81), channel_id=1, source_target_pairs={{0,12},{1,13},{2,14},{3,15},{4,8},{5,9},{6,10},{7,11},{8,4},{9,5},... | collective-permute-start | bytes 442376 | tf_op jit(solution)/shard_map/ppermute | solution.py:358
  36.8 27.2 %collective-permute-start.12 = (bf16[576,128]{1,0:T(8,128)(2,1)S(1)}, bf16[576,128]{1,0:T(8,128)(2,1)S(1)}, u32[]{:S(2)}, u32[]{:S(2)}) collective-permute-start(bf16[576,128]{1,0:T(8,128)(2,1)S(1)} %get-tuple-element.82), channel_id=1, source_target_pairs={{0,13},{1,12},{2,15},{3,14},{4,9},{5,8},{6,11},{7,10},{8,5},{9,4},... | collective-permute-start | bytes 442376 | tf_op jit(solution)/shard_map/ppermute | solution.py:358
  39.0 25.9 %collective-permute-start.13 = (bf16[576,128]{1,0:T(8,128)(2,1)S(1)}, bf16[576,128]{1,0:T(8,128)(2,1)S(1)}, u32[]{:S(2)}, u32[]{:S(2)}) collective-permute-start(bf16[576,128]{1,0:T(8,128)(2,1)S(1)} %get-tuple-element.83), channel_id=1, source_target_pairs={{0,14},{1,15},{2,12},{3,13},{4,10},{5,11},{6,8},{7,9},{8,6},{9,7},... | collective-permute-start | bytes 442376 | tf_op jit(solution)/shard_map/ppermute | solution.py:358
  54.2 10.8 %collective-permute-start.14 = (bf16[576,128]{1,0:T(8,128)(2,1)S(1)}, bf16[576,128]{1,0:T(8,128)(2,1)S(1)}, u32[]{:S(2)}, u32[]{:S(2)}) collective-permute-start(bf16[576,128]{1,0:T(8,128)(2,1)S(1)} %get-tuple-element.84), channel_id=1, source_target_pairs={{0,15},{1,14},{2,13},{3,12},{4,11},{5,10},{6,9},{7,8},{8,7},{9,6},... | collective-permute-start | bytes 442376 | tf_op jit(solution)/shard_map/ppermute | solution.py:358
  59.7 34.5 %collective-permute-start.31 = (bf16[384,128]{1,0:T(8,128)(2,1)}, bf16[384,128]{1,0:T(8,128)(2,1)S(1)}, u32[]{:S(2)}, u32[]{:S(2)}) collective-permute-start(bf16[384,128]{1,0:T(8,128)(2,1)} %get-tuple-element.102), channel_id=1, source_target_pairs={{0,1},{1,0},{2,3},{3,2},{4,5},{5,4},{6,7},{7,6},{8,9},{9,8},{10,11... | collective-permute-start | bytes 294920 | tf_op jit(solution)/shard_map/ppermute | solution.py:358
  63.5 31.4 %collective-permute-start.32 = (bf16[384,128]{1,0:T(8,128)(2,1)}, bf16[384,128]{1,0:T(8,128)(2,1)S(1)}, u32[]{:S(2)}, u32[]{:S(2)}) collective-permute-start(bf16[384,128]{1,0:T(8,128)(2,1)} %get-tuple-element.103), channel_id=1, source_target_pairs={{0,2},{1,3},{2,0},{3,1},{4,6},{5,7},{6,4},{7,5},{8,10},{9,11},{10,... | collective-permute-start | bytes 294920 | tf_op jit(solution)/shard_map/ppermute | solution.py:358
  64.0 33.8 %collective-permute-start.33 = (bf16[384,128]{1,0:T(8,128)(2,1)}, bf16[384,128]{1,0:T(8,128)(2,1)}, u32[]{:S(2)}, u32[]{:S(2)}) collective-permute-start(bf16[384,128]{1,0:T(8,128)(2,1)} %get-tuple-element.104), channel_id=1, source_target_pairs={{0,3},{1,2},{2,1},{3,0},{4,7},{5,6},{6,5},{7,4},{8,11},{9,10},{10,... | collective-permute-start | bytes 294920 | tf_op jit(solution)/shard_map/ppermute | solution.py:358
  82.8 102.1 %collective-permute-start.15 = (bf16[16,128,128]{2,1,0:T(8,128)(2,1)}, bf16[16,128,128]{2,1,0:T(8,128)(2,1)S(1)}, u32[]{:S(2)}, u32[]{:S(2)}) collective-permute-start(bf16[16,128,128]{2,1,0:T(8,128)(2,1)} %collect_shared.1.rest_16_), channel_id=1, source_target_pairs={{0,1},{1,0},{2,3},{3,2},{4,5},{5,4},{6,7},{7,6},{8,9},{9,8},{10,11... | collective-permute-start | bytes 1572872 | tf_op jit(solution)/shard_map/ppermute | solution.py:380
  83.6 14.4 %collective-permute-start.34 = (bf16[384,128]{1,0:T(8,128)(2,1)}, bf16[384,128]{1,0:T(8,128)(2,1)S(1)}, u32[]{:S(2)}, u32[]{:S(2)}) collective-permute-start(bf16[384,128]{1,0:T(8,128)(2,1)} %copy-done.53), channel_id=1, source_target_pairs={{0,4},{1,5},{2,6},{3,7},{4,0},{5,1},{6,2},{7,3},{8,12},{9,13},{10,... | collective-permute-start | bytes 294920 | tf_op jit(solution)/shard_map/ppermute | solution.py:358
  97.8 10.2 %collective-permute-start.37 = (bf16[384,128]{1,0:T(8,128)(2,1)S(1)}, bf16[384,128]{1,0:T(8,128)(2,1)S(1)}, u32[]{:S(2)}, u32[]{:S(2)}) collective-permute-start(bf16[384,128]{1,0:T(8,128)(2,1)S(1)} %get-tuple-element.108), channel_id=1, source_target_pairs={{0,7},{1,6},{2,5},{3,4},{4,3},{5,2},{6,1},{7,0},{8,15},{9,14},{10,... | collective-permute-start | bytes 294920 | tf_op jit(solution)/shard_map/ppermute | solution.py:358
  98.6 11.3 %collective-permute-start.38 = (bf16[384,128]{1,0:T(8,128)(2,1)S(1)}, bf16[384,128]{1,0:T(8,128)(2,1)S(1)}, u32[]{:S(2)}, u32[]{:S(2)}) collective-permute-start(bf16[384,128]{1,0:T(8,128)(2,1)S(1)} %get-tuple-element.109), channel_id=1, source_target_pairs={{0,8},{1,9},{2,10},{3,11},{4,12},{5,13},{6,14},{7,15},{8,0},{9,1},... | collective-permute-start | bytes 294920 | tf_op jit(solution)/shard_map/ppermute | solution.py:358
  103.5 15.1 %collective-permute-start.39 = (bf16[384,128]{1,0:T(8,128)(2,1)S(1)}, bf16[384,128]{1,0:T(8,128)(2,1)S(1)}, u32[]{:S(2)}, u32[]{:S(2)}) collective-permute-start(bf16[384,128]{1,0:T(8,128)(2,1)S(1)} %get-tuple-element.110), channel_id=1, source_target_pairs={{0,9},{1,8},{2,11},{3,10},{4,13},{5,12},{6,15},{7,14},{8,1},{9,0},... | collective-permute-start | bytes 294920 | tf_op jit(solution)/shard_map/ppermute | solution.py:358
  105.3 16.6 %collective-permute-start.40 = (bf16[384,128]{1,0:T(8,128)(2,1)S(1)}, bf16[384,128]{1,0:T(8,128)(2,1)S(1)}, u32[]{:S(2)}, u32[]{:S(2)}) collective-permute-start(bf16[384,128]{1,0:T(8,128)(2,1)S(1)} %get-tuple-element.111), channel_id=1, source_target_pairs={{0,10},{1,11},{2,8},{3,9},{4,14},{5,15},{6,12},{7,13},{8,2},{9,3},... | collective-permute-start | bytes 294920 | tf_op jit(solution)/shard_map/ppermute | solution.py:358
  108.6 15.4 %collective-permute-start.41 = (bf16[384,128]{1,0:T(8,128)(2,1)S(1)}, bf16[384,128]{1,0:T(8,128)(2,1)S(1)}, u32[]{:S(2)}, u32[]{:S(2)}) collective-permute-start(bf16[384,128]{1,0:T(8,128)(2,1)S(1)} %get-tuple-element.112), channel_id=1, source_target_pairs={{0,11},{1,10},{2,9},{3,8},{4,15},{5,14},{6,13},{7,12},{8,3},{9,2},... | collective-permute-start | bytes 294920 | tf_op jit(solution)/shard_map/ppermute | solution.py:358
  110.5 21.8 %collective-permute-start.42 = (bf16[384,128]{1,0:T(8,128)(2,1)}, bf16[384,128]{1,0:T(8,128)(2,1)}, u32[]{:S(2)}, u32[]{:S(2)}) collective-permute-start(bf16[384,128]{1,0:T(8,128)(2,1)} %get-tuple-element.113), channel_id=1, source_target_pairs={{0,12},{1,13},{2,14},{3,15},{4,8},{5,9},{6,10},{7,11},{8,4},{9,5},... | collective-permute-start | bytes 294920 | tf_op jit(solution)/shard_map/ppermute | solution.py:358
  119.3 13.1 %collective-permute-start.43 = (bf16[384,128]{1,0:T(8,128)(2,1)}, bf16[384,128]{1,0:T(8,128)(2,1)}, u32[]{:S(2)}, u32[]{:S(2)}) collective-permute-start(bf16[384,128]{1,0:T(8,128)(2,1)} %get-tuple-element.114), channel_id=1, source_target_pairs={{0,13},{1,12},{2,15},{3,14},{4,9},{5,8},{6,11},{7,10},{8,5},{9,4},... | collective-permute-start | bytes 294920 | tf_op jit(solution)/shard_map/ppermute | solution.py:358
  158.6 11.0 %collective-permute-start.49 = (bf16[128,128]{1,0:T(8,128)(2,1)S(1)}, bf16[128,128]{1,0:T(8,128)(2,1)S(1)}, u32[]{:S(2)}, u32[]{:S(2)}) collective-permute-start(bf16[128,128]{1,0:T(8,128)(2,1)S(1)} %get-tuple-element.121), channel_id=1, source_target_pairs={{0,4},{1,5},{2,6},{3,7},{4,0},{5,1},{6,2},{7,3},{8,12},{9,13},{10,... | collective-permute-start | bytes 98312 | tf_op jit(solution)/shard_map/ppermute | solution.py:358
  170.4 11.0 %collective-permute-start.54 = (bf16[128,128]{1,0:T(8,128)(2,1)}, bf16[128,128]{1,0:T(8,128)(2,1)}, u32[]{:S(2)}, u32[]{:S(2)}) collective-permute-start(bf16[128,128]{1,0:T(8,128)(2,1)} %get-tuple-element.126), channel_id=1, source_target_pairs={{0,9},{1,8},{2,11},{3,10},{4,13},{5,12},{6,15},{7,14},{8,1},{9,0},... | collective-permute-start | bytes 98312 | tf_op jit(solution)/shard_map/ppermute | solution.py:358
  172.3 10.9 %collective-permute-start.55 = (bf16[128,128]{1,0:T(8,128)(2,1)}, bf16[128,128]{1,0:T(8,128)(2,1)}, u32[]{:S(2)}, u32[]{:S(2)}) collective-permute-start(bf16[128,128]{1,0:T(8,128)(2,1)} %get-tuple-element.127), channel_id=1, source_target_pairs={{0,10},{1,11},{2,8},{3,9},{4,14},{5,15},{6,12},{7,13},{8,2},{9,3},... | collective-permute-start | bytes 98312 | tf_op jit(solution)/shard_map/ppermute | solution.py:358
  177.1 30.9 %collective-permute-start.56 = (bf16[128,128]{1,0:T(8,128)(2,1)}, bf16[128,128]{1,0:T(8,128)(2,1)S(1)}, u32[]{:S(2)}, u32[]{:S(2)}) collective-permute-start(bf16[128,128]{1,0:T(8,128)(2,1)} %copy-done.63), channel_id=1, source_target_pairs={{0,11},{1,10},{2,9},{3,8},{4,15},{5,14},{6,13},{7,12},{8,3},{9,2},... | collective-permute-start | bytes 98312 | tf_op jit(solution)/shard_map/ppermute | solution.py:358
  179.7 29.6 %collective-permute-start.57 = (bf16[128,128]{1,0:T(8,128)(2,1)}, bf16[128,128]{1,0:T(8,128)(2,1)S(1)}, u32[]{:S(2)}, u32[]{:S(2)}) collective-permute-start(bf16[128,128]{1,0:T(8,128)(2,1)} %copy-done.62), channel_id=1, source_target_pairs={{0,12},{1,13},{2,14},{3,15},{4,8},{5,9},{6,10},{7,11},{8,4},{9,5},... | collective-permute-start | bytes 98312 | tf_op jit(solution)/shard_map/ppermute | solution.py:358
  181.4 29.0 %collective-permute-start.58 = (bf16[128,128]{1,0:T(8,128)(2,1)}, bf16[128,128]{1,0:T(8,128)(2,1)S(1)}, u32[]{:S(2)}, u32[]{:S(2)}) collective-permute-start(bf16[128,128]{1,0:T(8,128)(2,1)} %copy-done.61), channel_id=1, source_target_pairs={{0,13},{1,12},{2,15},{3,14},{4,9},{5,8},{6,11},{7,10},{8,5},{9,4},... | collective-permute-start | bytes 98312 | tf_op jit(solution)/shard_map/ppermute | solution.py:358
  183.1 27.6 %collective-permute-start.59 = (bf16[128,128]{1,0:T(8,128)(2,1)}, bf16[128,128]{1,0:T(8,128)(2,1)S(1)}, u32[]{:S(2)}, u32[]{:S(2)}) collective-permute-start(bf16[128,128]{1,0:T(8,128)(2,1)} %copy-done.60), channel_id=1, source_target_pairs={{0,14},{1,15},{2,12},{3,13},{4,10},{5,11},{6,8},{7,9},{8,6},{9,7},... | collective-permute-start | bytes 98312 | tf_op jit(solution)/shard_map/ppermute | solution.py:358
  184.9 25.8 %collective-permute-start.60 = (bf16[128,128]{1,0:T(8,128)(2,1)S(1)}, bf16[128,128]{1,0:T(8,128)(2,1)S(1)}, u32[]{:S(2)}, u32[]{:S(2)}) collective-permute-start(bf16[128,128]{1,0:T(8,128)(2,1)S(1)} %get-tuple-element.132), channel_id=1, source_target_pairs={{0,15},{1,14},{2,13},{3,12},{4,11},{5,10},{6,9},{7,8},{8,7},{9,6},... | collective-permute-start | bytes 98312 | tf_op jit(solution)/shard_map/ppermute | solution.py:358
  218.1 10.0 %collective-permute-start.25 = (bf16[192,128]{1,0:T(8,128)(2,1)S(1)}, bf16[192,128]{1,0:T(8,128)(2,1)S(1)}, u32[]{:S(2)}, u32[]{:S(2)}) collective-permute-start(bf16[192,128]{1,0:T(8,128)(2,1)S(1)} %get-tuple-element.95), channel_id=1, source_target_pairs={{0,10},{1,11},{2,8},{3,9},{4,14},{5,15},{6,12},{7,13},{8,2},{9,3},... | collective-permute-start | bytes 147464 | tf_op jit(solution)/shard_map/ppermute | solution.py:358
  219.0 10.6 %collective-permute-start.26 = (bf16[192,128]{1,0:T(8,128)(2,1)S(1)}, bf16[192,128]{1,0:T(8,128)(2,1)S(1)}, u32[]{:S(2)}, u32[]{:S(2)}) collective-permute-start(bf16[192,128]{1,0:T(8,128)(2,1)S(1)} %get-tuple-element.96), channel_id=1, source_target_pairs={{0,11},{1,10},{2,9},{3,8},{4,15},{5,14},{6,13},{7,12},{8,3},{9,2},... | collective-permute-start | bytes 147464 | tf_op jit(solution)/shard_map/ppermute | solution.py:358
  (120 other events, 2012.9 us)

commit v2 on v1

--- a/solution.py
+++ b/solution.py
@@ -18,10 +18,12 @@
 MASKED = -1e30
 EXP2_SCALE = HEAD_DIM ** (-0.5) * math.log2(math.e)
 UNROLLS = (1, 2, 3, 4, 6, 8, 10, 12)
-VMEM_LIMIT = 48 * 1024 * 1024
+VMEM_LIMIT = 12 * 1024 * 1024
 
 ROWS_X = 3 * TILE + HALF + TILE
 ROWS_Y = 3 * TILE
+
+IN_FLIGHT = 5
 
 ANY = pl.BlockSpec(memory_space=pl.ANY)
 SMEM = pl.BlockSpec(memory_space=pltpu.SMEM)
@@ -46,11 +48,11 @@
     return pl.ds(pl.multiple_of(head * HEAD_DIM, HEAD_DIM), HEAD_DIM)
 
 
-def partner_order(devices):
+def masks_of(devices):
     half = devices // 2
     far = list(range(half, devices))
     near = list(range(1, half))
-    order = []
+    order = [0]
     for index in range(half):
         order.append(far[index])
         if index < len(near):
@@ -76,13 +78,12 @@
             dst[:, lane : lane + step] = (part * inverse * gain[:, lane : lane + step]).astype(
                 jnp.bfloat16
             )
-    for mask in range(devices):
+    for mask, x_out, y_out in zip(masks_of(devices), x_refs, y_refs):
         to = lax.bitwise_xor(me, mask)
         core = to % 2
         first = lanes_of(head_of(to, 0, heads_pair))
         second = lanes_of(head_of(to, 1, heads_pair))
         shared = lanes_of(head_of(to, 2, heads_pair))
-        x_out, y_out = x_refs[mask], y_refs[mask]
         x_out[0:TILE] = q_norm[:, first]
         x_out[TILE : 2 * TILE] = k_norm[:, first]
         x_out[2 * TILE : 3 * TILE] = v_ref[:, first]
@@ -118,30 +119,19 @@
 
 
 def collect_kernel(devices, me_ref, *rest):
-    x_refs, out_ref, sems = rest[:devices], rest[devices], rest[devices + 1]
+    x_refs, out_ref = rest[:devices], rest[devices]
     me = me_ref[0]
-    copies = []
-    for mask in range(devices):
-        copies.append(
-            pltpu.make_async_copy(
-                x_refs[mask].at[pl.ds(3 * TILE + HALF, TILE)],
-                out_ref.at[lax.bitwise_xor(me, mask)],
-                sems.at[mask],
-            )
-        )
-    for copy in copies:
-        copy.start()
-    for copy in copies:
-        copy.wait()
+    for mask, x_ref in zip(masks_of(devices), x_refs):
+        out_ref[lax.bitwise_xor(me, mask)] = x_ref[3 * TILE + HALF : ROWS_X]
 
 
 def collect(me, x_in, devices):
     return pl.pallas_call(
         functools.partial(collect_kernel, devices),
         out_shape=jax.ShapeDtypeStruct((devices, TILE, HEAD_DIM), jnp.bfloat16),
-        in_specs=[SMEM] + [ANY] * devices,
-        out_specs=ANY,
-        scratch_shapes=[pltpu.SemaphoreType.DMA((devices,))],
+        in_specs=[SMEM] + [VMEM] * devices,
+        out_specs=VMEM,
+        compiler_params=pltpu.CompilerParams(vmem_limit_bytes=VMEM_LIMIT),
         name="collect_shared",
     )(me, *x_in)
 
@@ -176,7 +166,7 @@
 def load_all(me, refs, held, sems):
     copies = [
         pltpu.make_async_copy(ref, held.at[lax.bitwise_xor(me, mask)], sems.at[mask])
-        for mask, ref in enumerate(refs)
+        for mask, ref in zip(masks_of(len(refs)), refs)
     ]
     for copy in copies:
         copy.start()
@@ -186,7 +176,7 @@
 def send_all(me, held, refs, sems):
     copies = [
         pltpu.make_async_copy(held.at[lax.bitwise_xor(me, mask)], ref, sems.at[mask])
-        for mask, ref in enumerate(refs)
+        for mask, ref in zip(masks_of(len(refs)), refs)
     ]
     for copy in copies:
         copy.start()
@@ -324,16 +314,16 @@
     def add(src, dst):
         copies.append(pltpu.make_async_copy(src, dst, sems.at[len(copies)]))
 
-    for mask in range(devices):
+    for mask, x_ref, y_ref in zip(masks_of(devices), x_refs, y_refs):
         source = lax.bitwise_xor(me, mask)
         core = source % 2
         first = lanes_of(head_of(source, 0, heads_pair))
         second = lanes_of(head_of(source, 1, heads_pair))
         shared = lanes_of(head_of(source, 2, heads_pair))
         half = pl.ds(pl.multiple_of(core * HALF, HALF), HALF)
-        add(x_refs[mask].at[pl.ds(0, TILE)], out_ref.at[:, first])
-        add(x_refs[mask].at[pl.ds(TILE, HALF)], out_ref.at[half, shared])
-        add(y_refs[mask], out_ref.at[:, second])
+        add(x_ref.at[pl.ds(0, TILE)], out_ref.at[:, first])
+        add(x_ref.at[pl.ds(TILE, HALF)], out_ref.at[half, shared])
+        add(y_ref, out_ref.at[:, second])
     for copy in copies:
         copy.start()
     for copy in copies:
@@ -344,21 +334,21 @@
     return pl.pallas_call(
         functools.partial(assemble_kernel, devices, heads_pair),
         out_shape=jax.ShapeDtypeStruct((TILE, width), jnp.bfloat16),
-        in_specs=[SMEM] + [ANY] * (2 * devices),
+        in_specs=[SMEM] + [VMEM] * (2 * devices),
         out_specs=ANY,
         scratch_shapes=[pltpu.SemaphoreType.DMA((3 * devices,))],
+        compiler_params=pltpu.CompilerParams(vmem_limit_bytes=VMEM_LIMIT),
         name="assemble",
     )(me, *x_back, *y_back)
 
 
-def exchange(parts, devices):
-    arrived = [None] * devices
-    arrived[0] = parts[0]
-    for mask in partner_order(devices):
-        arrived[mask] = lax.ppermute(
-            parts[mask], "ulysses", [(index, index ^ mask) for index in range(devices)]
-        )
-    return arrived
+def exchange(parts, devices, masks):
+    return [
+        part
+        if mask == 0
+        else lax.ppermute(part, "ulysses", [(index, index ^ mask) for index in range(devices)])
+        for mask, part in zip(masks, parts)
+    ]
 
 
 def local_pairs(query, key, value, query_gain, key_gain, key_blocks, block_counts):
@@ -374,14 +364,23 @@
         return lists, counts
 
     x_out, y_out = pack(me, query, key, value, query_gain, key_gain, devices, heads_pair)
-    x_in = exchange(x_out, devices)
-    y_in = exchange(y_out, devices)
+    masks = masks_of(devices)
+    x_in = exchange(x_out, devices, masks)
     own = collect(me, x_in, devices)
     other = lax.ppermute(own, "ulysses", [(at, at ^ 1) for at in range(devices)])
+    far = [place for place, mask in enumerate(masks) if mask >= devices // 2]
+    early = far[:IN_FLIGHT - 1]
+    late = [place for place in range(1, devices) if place not in early]
+    y_in = [y_out[0]] + [None] * (devices - 1)
+    y_early = exchange([y_out[at] for at in early], devices, [masks[at] for at in early])
     x_results = attend_x(me, tables(0) + tables(2), x_in, own, other, devices)
-    x_back = exchange(x_results, devices)
+    y_late, x_results = lax.optimization_barrier(([y_out[at] for at in late], x_results))
+    y_late = exchange(y_late, devices, [masks[at] for at in late])
+    for at, part in zip(early + late, y_early + y_late):
+        y_in[at] = part
+    x_back = exchange(x_results, devices, masks)
     y_results = attend_y(me, tables(1), y_in, devices)
-    y_back = exchange(y_results, devices)
+    y_back = exchange(y_results, devices, masks)
     return assemble(me, x_back, y_back, query.shape[1], devices, heads_pair)
 
 

time: 278 us -> 179 us (0.64)
  Pallas kernels: 95.2 us -> 36.1 us
  starting transfers between devices: 125 us -> 97.4 us
  local copies, waits for them, and re-layouts: 32 us -> 12.8 us
  waiting for transfers between devices: 23.2 us -> 31.5 us
    pallas_call x1, Pallas kernels: 41.2 us -> 1.45 us  [assemble(): pl.pallas_call(functools.partial(assemble_kernel, devices, heads_pair), o...]
    ppermute x60, starting transfers between devices: 124 us -> 96.4 us  [exchange(): lax.ppermute(part, 'ulysses', [(index, index ^ mask) for index in range(d...]
    pallas_call x1, Pallas kernels: 17.1 us -> 0.04 us  [collect(): pl.pallas_call(functools.partial(collect_kernel, devices), out_shape=jax....]
    unnamed x182 -> x50, local copies, waits for them, and re-layouts: 24.9 us -> 8.19 us
    ppermute x60, waiting for transfers between devices: 23.2 us -> 31.5 us  [exchange(): lax.ppermute(part, 'ulysses', [(index, index ^ mask) for index in range(d...]
  transfers between devices with their start and end apart: 61 -> 61, of which waited for: 13 -> 13; matrix products, arithmetic and copies ran while one was open for 3% -> 3% of each run, Pallas kernels for 18% -> 17%
where the time goes in v2:
time: 179 us; the launch traced here: 178 us
  starting transfers between devices  97.4 us (54%)
  Pallas kernels  36.1 us (20%)
  waiting for transfers between devices  31.5 us (18%)
  local copies, waits for them, and re-layouts  12.8 us (7%)
    ppermute x60, starting transfers between devices, exchange(): lax.ppermute(part, 'ulysses', [(index, index ^ mask) for index in range(d...  96.4 us
    ppermute x60, waiting for transfers between devices, exchange(): lax.ppermute(part, 'ulysses', [(index, index ^ mask) for index in range(d...  31.5 us
    pallas_call x1, Pallas kernels, attend_x(): pl.pallas_call(functools.partial(attend_x_kernel, devices), out_shape=[ja...  19.9 us
    pallas_call x1, Pallas kernels, attend_y(): pl.pallas_call(functools.partial(attend_y_kernel, devices), out_shape=[ja...  11.1 us
    unnamed x50, local copies, waits for them, and re-layouts  8.19 us
    dynamic_slice x4, local copies, waits for them, and re-layouts, tables(): lists = lax.dynamic_index_in_dim(key_blocks, head, 0, False).reshape(-1)  4.1 us
    pallas_call x1, Pallas kernels, pack(): pl.pallas_call(functools.partial(pack_kernel, devices, heads_pair), out_s...  3.62 us
  transfers between devices with their start and end apart: 61, of which 13 were waited for; matrix products, arithmetic and copies ran while one was open for 3% of the time, Pallas kernels for 17%

profile of v2, /device:TPU:0, one launch (start us, length us, event | category | flops | bytes accessed | tf_op | source)
XLA Modules:
  0.0 178.2 jit_solution(17643071823344639016)
XLA Ops:
  5.4 3.6 %norm_pack.1 = (bf16[576,128]{1,0:T(8,128)(2,1)S(1)}, bf16[576,128]{1,0:T(8,128)(2,1)S(1)}, bf16[576,128]{1,0:T(8,128)(2,1)S(1)}, bf16[576,128]{1,0:T(8,128)(2,1...) custom-call(s32[1]{0:T(128)} %bitcast.me_ref, ...), custom_call_target="tpu_custom_call" | custom-call | tf_op jit(solution)/shard_map/norm_pack/pallas_call | solution.py:109
  9.1 4.1 %collective-permute-start = (bf16[576,128]{1,0:T(8,128)(2,1)S(1)}, bf16[576,128]{1,0:T(8,128)(2,1)S(1)}, u32[]{:S(2)}, u32[]{:S(2)}) collective-permute-start(bf16[576,128]{1,0:T(8,128)(2,1)S(1)} %get-tuple-element.108), channel_id=1, source_target_pairs={{0,8},{1,9},{2,10},{3,11},{4,12},{5,13},{6,14},{7,15},{8,0},{9,1},... | collective-permute-start | bytes 442376 | tf_op jit(solution)/shard_map/ppermute | solution.py:349
  15.2 2.5 %collective-permute-start.4 = (bf16[576,128]{1,0:T(8,128)(2,1)S(1)}, bf16[576,128]{1,0:T(8,128)(2,1)S(1)}, u32[]{:S(2)}, u32[]{:S(2)}) collective-permute-start(bf16[576,128]{1,0:T(8,128)(2,1)S(1)} %get-tuple-element.112), channel_id=1, source_target_pairs={{0,10},{1,11},{2,8},{3,9},{4,14},{5,15},{6,12},{7,13},{8,2},{9,3},... | collective-permute-start | bytes 442376 | tf_op jit(solution)/shard_map/ppermute | solution.py:349
  17.7 9.7 %collective-permute-done.rest_1_ = bf16[576,128]{1,0:T(8,128)(2,1)S(1)} collective-permute-done((bf16[576,128]{1,0:T(8,128)(2,1)S(1)}, bf16[576,128]{1,0:T(8,128)(2,1)S(1)}, u32[]{:S(2)}, u32[]{:S(2)}) %collective-permute-start) | collective-permute-done | bytes 147488 | tf_op jit(solution)/shard_map/ppermute | solution.py:349
  28.8 3.1 %collective-permute-start.7 = (bf16[576,128]{1,0:T(8,128)(2,1)S(1)}, bf16[576,128]{1,0:T(8,128)(2,1)S(1)}, u32[]{:S(2)}, u32[]{:S(2)}) collective-permute-start(bf16[576,128]{1,0:T(8,128)(2,1)S(1)} %get-tuple-element.115), channel_id=1, source_target_pairs={{0,4},{1,5},{2,6},{3,7},{4,0},{5,1},{6,2},{7,3},{8,12},{9,13},{10,... | collective-permute-start | bytes 442376 | tf_op jit(solution)/shard_map/ppermute | solution.py:349
  33.1 5.1 %collective-permute-done.4.rest_5_ = bf16[576,128]{1,0:T(8,128)(2,1)S(1)} collective-permute-done((bf16[576,128]{1,0:T(8,128)(2,1)S(1)}, bf16[576,128]{1,0:T(8,128)(2,1)S(1)}, u32[]{:S(2)}, u32[]{:S(2)}) %collective-permute-start.4) | collective-permute-done | bytes 147488 | tf_op jit(solution)/shard_map/ppermute | solution.py:349
  38.2 1.9 %collective-permute-start.10 = (bf16[576,128]{1,0:T(8,128)(2,1)S(1)}, bf16[576,128]{1,0:T(8,128)(2,1)S(1)}, u32[]{:S(2)}, u32[]{:S(2)}) collective-permute-start(bf16[576,128]{1,0:T(8,128)(2,1)S(1)} %get-tuple-element.118), channel_id=1, source_target_pairs={{0,13},{1,12},{2,15},{3,14},{4,9},{5,8},{6,11},{7,10},{8,5},{9,4},... | collective-permute-start | bytes 442376 | tf_op jit(solution)/shard_map/ppermute | solution.py:349
  40.1 4.0 %collective-permute-start.11 = (bf16[576,128]{1,0:T(8,128)(2,1)S(1)}, bf16[576,128]{1,0:T(8,128)(2,1)S(1)}, u32[]{:S(2)}, u32[]{:S(2)}) collective-permute-start(bf16[576,128]{1,0:T(8,128)(2,1)S(1)} %get-tuple-element.119), channel_id=1, source_target_pairs={{0,6},{1,7},{2,4},{3,5},{4,2},{5,3},{6,0},{7,1},{8,14},{9,15},{10,... | collective-permute-start | bytes 442376 | tf_op jit(solution)/shard_map/ppermute | solution.py:349
  44.1 9.1 %collective-permute-start.12 = (bf16[576,128]{1,0:T(8,128)(2,1)S(1)}, bf16[576,128]{1,0:T(8,128)(2,1)S(1)}, u32[]{:S(2)}, u32[]{:S(2)}) collective-permute-start(bf16[576,128]{1,0:T(8,128)(2,1)S(1)} %get-tuple-element.120), channel_id=1, source_target_pairs={{0,14},{1,15},{2,12},{3,13},{4,10},{5,11},{6,8},{7,9},{8,6},{9,7},... | collective-permute-start | bytes 442376 | tf_op jit(solution)/shard_map/ppermute | solution.py:349
  53.2 4.4 %collective-permute-start.14 = (bf16[576,128]{1,0:T(8,128)(2,1)S(1)}, bf16[576,128]{1,0:T(8,128)(2,1)S(1)}, u32[]{:S(2)}, u32[]{:S(2)}) collective-permute-start(bf16[576,128]{1,0:T(8,128)(2,1)S(1)} %get-tuple-element.122), channel_id=1, source_target_pairs={{0,15},{1,14},{2,13},{3,12},{4,11},{5,10},{6,9},{7,8},{8,7},{9,6},... | collective-permute-start | bytes 442376 | tf_op jit(solution)/shard_map/ppermute | solution.py:349
  59.2 2.2 %collective-permute-done.13.rest_14_ = bf16[576,128]{1,0:T(8,128)(2,1)S(1)} collective-permute-done((bf16[576,128]{1,0:T(8,128)(2,1)S(1)}, bf16[576,128]{1,0:T(8,128)(2,1)S(1)}, u32[]{:S(2)}, u32[]{:S(2)}) %collective-permute-start.13) | collective-permute-done | bytes 147488 | tf_op jit(solution)/shard_map/ppermute | solution.py:349
  61.3 2.3 %collective-permute-done.14.rest_15_ = bf16[576,128]{1,0:T(8,128)(2,1)S(1)} collective-permute-done((bf16[576,128]{1,0:T(8,128)(2,1)S(1)}, bf16[576,128]{1,0:T(8,128)(2,1)S(1)}, u32[]{:S(2)}, u32[]{:S(2)}) %collective-permute-start.14) | collective-permute-done | bytes 147488 | tf_op jit(solution)/shard_map/ppermute | solution.py:349
  64.8 3.5 %collective-permute-start.31 = (bf16[384,128]{1,0:T(8,128)(2,1)}, bf16[384,128]{1,0:T(8,128)(2,1)}, u32[]{:S(2)}, u32[]{:S(2)}) collective-permute-start(bf16[384,128]{1,0:T(8,128)(2,1)} %get-tuple-element.156), channel_id=1, source_target_pairs={{0,8},{1,9},{2,10},{3,11},{4,12},{5,13},{6,14},{7,15},{8,0},{9,1},... | collective-permute-start | bytes 294920 | tf_op jit(solution)/shard_map/ppermute | solution.py:349
  68.4 2.1 %collective-permute-start.35 = (bf16[384,128]{1,0:T(8,128)(2,1)}, bf16[384,128]{1,0:T(8,128)(2,1)}, u32[]{:S(2)}, u32[]{:S(2)}) collective-permute-start(bf16[384,128]{1,0:T(8,128)(2,1)} %get-tuple-element.160), channel_id=1, source_target_pairs={{0,10},{1,11},{2,8},{3,9},{4,14},{5,15},{6,12},{7,13},{8,2},{9,3},... | collective-permute-start | bytes 294920 | tf_op jit(solution)/shard_map/ppermute | solution.py:349
  75.1 19.9 %attend_x.1 = (bf16[192,128]{1,0:T(8,128)(2,1)S(1)}, bf16[192,128]{1,0:T(8,128)(2,1)S(1)}, bf16[192,128]{1,0:T(8,128)(2,1)S(1)}, bf16[192,128]{1,0:T(8,128)(2,1)...) custom-call(s32[1]{0:T(128)} %bitcast.me_ref, ...), custom_call_target="tpu_custom_call" | custom-call | flops 805306368 | bytes 3145728 | tf_op jit(solution)/shard_map/attend_x/pallas_call | solution.py:271
  96.9 3.8 %collective-permute-start.16 = (bf16[192,128]{1,0:T(8,128)(2,1)S(1)}, bf16[192,128]{1,0:T(8,128)(2,1)S(1)}, u32[]{:S(2)}, u32[]{:S(2)}) collective-permute-start(bf16[192,128]{1,0:T(8,128)(2,1)S(1)} %get-tuple-element.140), channel_id=1, source_target_pairs={{0,8},{1,9},{2,10},{3,11},{4,12},{5,13},{6,14},{7,15},{8,0},{9,1},... | collective-permute-start | bytes 147464 | tf_op jit(solution)/shard_map/ppermute | solution.py:349
  101.8 3.4 %collective-permute-start.20 = (bf16[192,128]{1,0:T(8,128)(2,1)S(1)}, bf16[192,128]{1,0:T(8,128)(2,1)S(1)}, u32[]{:S(2)}, u32[]{:S(2)}) collective-permute-start(bf16[192,128]{1,0:T(8,128)(2,1)S(1)} %get-tuple-element.144), channel_id=1, source_target_pairs={{0,10},{1,11},{2,8},{3,9},{4,14},{5,15},{6,12},{7,13},{8,2},{9,3},... | collective-permute-start | bytes 147464 | tf_op jit(solution)/shard_map/ppermute | solution.py:349
  107.4 3.1 %collective-permute-start.23 = (bf16[192,128]{1,0:T(8,128)(2,1)S(1)}, bf16[192,128]{1,0:T(8,128)(2,1)S(1)}, u32[]{:S(2)}, u32[]{:S(2)}) collective-permute-start(bf16[192,128]{1,0:T(8,128)(2,1)S(1)} %get-tuple-element.147), channel_id=1, source_target_pairs={{0,4},{1,5},{2,6},{3,7},{4,0},{5,1},{6,2},{7,3},{8,12},{9,13},{10,... | collective-permute-start | bytes 147464 | tf_op jit(solution)/shard_map/ppermute | solution.py:349
  114.5 2.1 %collective-permute-done.24.rest_9_ = bf16[192,128]{1,0:T(8,128)(2,1)S(1)} collective-permute-done((bf16[192,128]{1,0:T(8,128)(2,1)S(1)}, bf16[192,128]{1,0:T(8,128)(2,1)S(1)}, u32[]{:S(2)}, u32[]{:S(2)}) %collective-permute-start.24) | collective-permute-done | bytes 49184 | tf_op jit(solution)/shard_map/ppermute | solution.py:349
  116.7 2.2 %collective-permute-start.39 = (bf16[384,128]{1,0:T(8,128)(2,1)S(1)}, bf16[384,128]{1,0:T(8,128)(2,1)S(1)}, u32[]{:S(2)}, u32[]{:S(2)}) collective-permute-start(bf16[384,128]{1,0:T(8,128)(2,1)S(1)} %copy-done.10), channel_id=1, source_target_pairs={{0,12},{1,13},{2,14},{3,15},{4,8},{5,9},{6,10},{7,11},{8,4},{9,5},... | collective-permute-start | bytes 294920 | tf_op jit(solution)/shard_map/ppermute | solution.py:349
  118.9 2.5 %collective-permute-start.41 = (bf16[384,128]{1,0:T(8,128)(2,1)}, bf16[384,128]{1,0:T(8,128)(2,1)S(1)}, u32[]{:S(2)}, u32[]{:S(2)}) collective-permute-start(bf16[384,128]{1,0:T(8,128)(2,1)} %get-tuple-element.166), channel_id=1, source_target_pairs={{0,13},{1,12},{2,15},{3,14},{4,9},{5,8},{6,11},{7,10},{8,5},{9,4},... | collective-permute-start | bytes 294920 | tf_op jit(solution)/shard_map/ppermute | solution.py:349
  121.4 1.9 %collective-permute-done.38.rest_8_ = bf16[384,128]{1,0:T(8,128)(2,1)S(1)} collective-permute-done((bf16[384,128]{1,0:T(8,128)(2,1)S(1)}, bf16[384,128]{1,0:T(8,128)(2,1)S(1)}, u32[]{:S(2)}, u32[]{:S(2)}) %collective-permute-start.38) | collective-permute-done | bytes 98336 | tf_op jit(solution)/shard_map/ppermute | solution.py:349
  125.5 2.7 %collective-permute-start.45 = (bf16[384,128]{1,0:T(8,128)(2,1)}, bf16[384,128]{1,0:T(8,128)(2,1)S(1)}, u32[]{:S(2)}, u32[]{:S(2)}) collective-permute-start(bf16[384,128]{1,0:T(8,128)(2,1)} %get-tuple-element.170), channel_id=1, source_target_pairs={{0,15},{1,14},{2,13},{3,12},{4,11},{5,10},{6,9},{7,8},{8,7},{9,6},... | collective-permute-start | bytes 294920 | tf_op jit(solution)/shard_map/ppermute | solution.py:349
  132.6 3.0 %collective-permute-start.28 = (bf16[192,128]{1,0:T(8,128)(2,1)}, bf16[192,128]{1,0:T(8,128)(2,1)S(1)}, u32[]{:S(2)}, u32[]{:S(2)}) collective-permute-start(bf16[192,128]{1,0:T(8,128)(2,1)} %copy-done.20), channel_id=1, source_target_pairs={{0,14},{1,15},{2,12},{3,13},{4,10},{5,11},{6,8},{7,9},{8,6},{9,7},... | collective-permute-start | bytes 147464 | tf_op jit(solution)/shard_map/ppermute | solution.py:349
  136.1 3.3 %collective-permute-start.30 = (bf16[192,128]{1,0:T(8,128)(2,1)S(1)}, bf16[192,128]{1,0:T(8,128)(2,1)S(1)}, u32[]{:S(2)}, u32[]{:S(2)}) collective-permute-start(bf16[192,128]{1,0:T(8,128)(2,1)S(1)} %get-tuple-element.154), channel_id=1, source_target_pairs={{0,15},{1,14},{2,13},{3,12},{4,11},{5,10},{6,9},{7,8},{8,7},{9,6},... | collective-permute-start | bytes 147464 | tf_op jit(solution)/shard_map/ppermute | solution.py:349
  140.2 11.1 %attend_y.1 = (bf16[128,128]{1,0:T(8,128)(2,1)S(1)}, bf16[128,128]{1,0:T(8,128)(2,1)S(1)}, bf16[128,128]{1,0:T(8,128)(2,1)S(1)}, bf16[128,128]{1,0:T(8,128)(2,1)...) custom-call(s32[1]{0:T(128)} %bitcast.me_ref, ...), custom_call_target="tpu_custom_call" | custom-call | flops 536870912 | bytes 2097152 | tf_op jit(solution)/shard_map/attend_y/pallas_call | solution.py:291
  151.4 3.4 %collective-permute-start.46 = (bf16[128,128]{1,0:T(8,128)(2,1)S(1)}, bf16[128,128]{1,0:T(8,128)(2,1)S(1)}, u32[]{:S(2)}, u32[]{:S(2)}) collective-permute-start(bf16[128,128]{1,0:T(8,128)(2,1)S(1)} %get-tuple-element.172), channel_id=1, source_target_pairs={{0,8},{1,9},{2,10},{3,11},{4,12},{5,13},{6,14},{7,15},{8,0},{9,1},... | collective-permute-start | bytes 98312 | tf_op jit(solution)/shard_map/ppermute | solution.py:349
  155.3 4.0 %collective-permute-start.50 = (bf16[128,128]{1,0:T(8,128)(2,1)S(1)}, bf16[128,128]{1,0:T(8,128)(2,1)S(1)}, u32[]{:S(2)}, u32[]{:S(2)}) collective-permute-start(bf16[128,128]{1,0:T(8,128)(2,1)S(1)} %get-tuple-element.176), channel_id=1, source_target_pairs={{0,10},{1,11},{2,8},{3,9},{4,14},{5,15},{6,12},{7,13},{8,2},{9,3},... | collective-permute-start | bytes 98312 | tf_op jit(solution)/shard_map/ppermute | solution.py:349
  162.8 2.1 %collective-permute-start.54 = (bf16[128,128]{1,0:T(8,128)(2,1)S(1)}, bf16[128,128]{1,0:T(8,128)(2,1)S(1)}, u32[]{:S(2)}, u32[]{:S(2)}) collective-permute-start(bf16[128,128]{1,0:T(8,128)(2,1)S(1)} %get-tuple-element.180), channel_id=1, source_target_pairs={{0,12},{1,13},{2,14},{3,15},{4,8},{5,9},{6,10},{7,11},{8,4},{9,5},... | collective-permute-start | bytes 98312 | tf_op jit(solution)/shard_map/ppermute | solution.py:349
  166.2 2.7 %collective-permute-start.57 = (bf16[128,128]{1,0:T(8,128)(2,1)S(1)}, bf16[128,128]{1,0:T(8,128)(2,1)S(1)}, u32[]{:S(2)}, u32[]{:S(2)}) collective-permute-start(bf16[128,128]{1,0:T(8,128)(2,1)S(1)} %get-tuple-element.183), channel_id=1, source_target_pairs={{0,6},{1,7},{2,4},{3,5},{4,2},{5,3},{6,0},{7,1},{8,14},{9,15},{10,... | collective-permute-start | bytes 98312 | tf_op jit(solution)/shard_map/ppermute | solution.py:349
  170.5 2.2 %collective-permute-start.60 = (bf16[128,128]{1,0:T(8,128)(2,1)S(1)}, bf16[128,128]{1,0:T(8,128)(2,1)S(1)}, u32[]{:S(2)}, u32[]{:S(2)}) collective-permute-start(bf16[128,128]{1,0:T(8,128)(2,1)S(1)} %get-tuple-element.186), channel_id=1, source_target_pairs={{0,15},{1,14},{2,13},{3,12},{4,11},{5,10},{6,9},{7,8},{8,7},{9,6},... | collective-permute-start | bytes 98312 | tf_op jit(solution)/shard_map/ppermute | solution.py:349
  172.7 2.8 %collective-permute-done.58.rest_29_ = bf16[128,128]{1,0:T(8,128)(2,1)S(1)} collective-permute-done((bf16[128,128]{1,0:T(8,128)(2,1)S(1)}, bf16[128,128]{1,0:T(8,128)(2,1)S(1)}, u32[]{:S(2)}, u32[]{:S(2)}) %collective-permute-start.58) | collective-permute-done | bytes 32800 | tf_op jit(solution)/shard_map/ppermute | solution.py:349
  (153 shorter events, 44.2 us)
Async XLA Ops:
  9.1 18.3 %collective-permute-start = (bf16[576,128]{1,0:T(8,128)(2,1)S(1)}, bf16[576,128]{1,0:T(8,128)(2,1)S(1)}, u32[]{:S(2)}, u32[]{:S(2)}) collective-permute-start(bf16[576,128]{1,0:T(8,128)(2,1)S(1)} %get-tuple-element.108), channel_id=1, source_target_pairs={{0,8},{1,9},{2,10},{3,11},{4,12},{5,13},{6,14},{7,15},{8,0},{9,1},... | collective-permute-start | bytes 442376 | tf_op jit(solution)/shard_map/ppermute | solution.py:349
  13.2 14.2 %collective-permute-start.1 = (bf16[576,128]{1,0:T(8,128)(2,1)S(1)}, bf16[576,128]{1,0:T(8,128)(2,1)S(1)}, u32[]{:S(2)}, u32[]{:S(2)}) collective-permute-start(bf16[576,128]{1,0:T(8,128)(2,1)S(1)} %get-tuple-element.109), channel_id=1, source_target_pairs={{0,1},{1,0},{2,3},{3,2},{4,5},{5,4},{6,7},{7,6},{8,9},{9,8},{10,11... | collective-permute-start | bytes 442376 | tf_op jit(solution)/shard_map/ppermute | solution.py:349
  13.2 15.7 %collective-permute-start.2 = (bf16[576,128]{1,0:T(8,128)(2,1)S(1)}, bf16[576,128]{1,0:T(8,128)(2,1)S(1)}, u32[]{:S(2)}, u32[]{:S(2)}) collective-permute-start(bf16[576,128]{1,0:T(8,128)(2,1)S(1)} %get-tuple-element.110), channel_id=1, source_target_pairs={{0,9},{1,8},{2,11},{3,10},{4,13},{5,12},{6,15},{7,14},{8,1},{9,0},... | collective-permute-start | bytes 442376 | tf_op jit(solution)/shard_map/ppermute | solution.py:349
  13.4 18.5 %collective-permute-start.3 = (bf16[576,128]{1,0:T(8,128)(2,1)S(1)}, bf16[576,128]{1,0:T(8,128)(2,1)S(1)}, u32[]{:S(2)}, u32[]{:S(2)}) collective-permute-start(bf16[576,128]{1,0:T(8,128)(2,1)S(1)} %get-tuple-element.111), channel_id=1, source_target_pairs={{0,2},{1,3},{2,0},{3,1},{4,6},{5,7},{6,4},{7,5},{8,10},{9,11},{10,... | collective-permute-start | bytes 442376 | tf_op jit(solution)/shard_map/ppermute | solution.py:349
  15.2 23.1 %collective-permute-start.4 = (bf16[576,128]{1,0:T(8,128)(2,1)S(1)}, bf16[576,128]{1,0:T(8,128)(2,1)S(1)}, u32[]{:S(2)}, u32[]{:S(2)}) collective-permute-start(bf16[576,128]{1,0:T(8,128)(2,1)S(1)} %get-tuple-element.112), channel_id=1, source_target_pairs={{0,10},{1,11},{2,8},{3,9},{4,14},{5,15},{6,12},{7,13},{8,2},{9,3},... | collective-permute-start | bytes 442376 | tf_op jit(solution)/shard_map/ppermute | solution.py:349
  27.3 10.9 %collective-permute-start.5 = (bf16[576,128]{1,0:T(8,128)(2,1)S(1)}, bf16[576,128]{1,0:T(8,128)(2,1)S(1)}, u32[]{:S(2)}, u32[]{:S(2)}) collective-permute-start(bf16[576,128]{1,0:T(8,128)(2,1)S(1)} %get-tuple-element.113), channel_id=1, source_target_pairs={{0,3},{1,2},{2,1},{3,0},{4,7},{5,6},{6,5},{7,4},{8,11},{9,10},{10,... | collective-permute-start | bytes 442376 | tf_op jit(solution)/shard_map/ppermute | solution.py:349
  27.3 12.8 %collective-permute-start.6 = (bf16[576,128]{1,0:T(8,128)(2,1)S(1)}, bf16[576,128]{1,0:T(8,128)(2,1)S(1)}, u32[]{:S(2)}, u32[]{:S(2)}) collective-permute-start(bf16[576,128]{1,0:T(8,128)(2,1)S(1)} %get-tuple-element.114), channel_id=1, source_target_pairs={{0,11},{1,10},{2,9},{3,8},{4,15},{5,14},{6,13},{7,12},{8,3},{9,2},... | collective-permute-start | bytes 442376 | tf_op jit(solution)/shard_map/ppermute | solution.py:349
  28.8 15.3 %collective-permute-start.7 = (bf16[576,128]{1,0:T(8,128)(2,1)S(1)}, bf16[576,128]{1,0:T(8,128)(2,1)S(1)}, u32[]{:S(2)}, u32[]{:S(2)}) collective-permute-start(bf16[576,128]{1,0:T(8,128)(2,1)S(1)} %get-tuple-element.115), channel_id=1, source_target_pairs={{0,4},{1,5},{2,6},{3,7},{4,0},{5,1},{6,2},{7,3},{8,12},{9,13},{10,... | collective-permute-start | bytes 442376 | tf_op jit(solution)/shard_map/ppermute | solution.py:349
  31.9 21.3 %collective-permute-start.8 = (bf16[576,128]{1,0:T(8,128)(2,1)S(1)}, bf16[576,128]{1,0:T(8,128)(2,1)S(1)}, u32[]{:S(2)}, u32[]{:S(2)}) collective-permute-start(bf16[576,128]{1,0:T(8,128)(2,1)S(1)} %get-tuple-element.116), channel_id=1, source_target_pairs={{0,12},{1,13},{2,14},{3,15},{4,8},{5,9},{6,10},{7,11},{8,4},{9,5},... | collective-permute-start | bytes 442376 | tf_op jit(solution)/shard_map/ppermute | solution.py:349
  38.2 15.0 %collective-permute-start.9 = (bf16[576,128]{1,0:T(8,128)(2,1)S(1)}, bf16[576,128]{1,0:T(8,128)(2,1)S(1)}, u32[]{:S(2)}, u32[]{:S(2)}) collective-permute-start(bf16[576,128]{1,0:T(8,128)(2,1)S(1)} %get-tuple-element.117), channel_id=1, source_target_pairs={{0,5},{1,4},{2,7},{3,6},{4,1},{5,0},{6,3},{7,2},{8,13},{9,12},{10,... | collective-permute-start | bytes 442376 | tf_op jit(solution)/shard_map/ppermute | solution.py:349
  38.2 19.4 %collective-permute-start.10 = (bf16[576,128]{1,0:T(8,128)(2,1)S(1)}, bf16[576,128]{1,0:T(8,128)(2,1)S(1)}, u32[]{:S(2)}, u32[]{:S(2)}) collective-permute-start(bf16[576,128]{1,0:T(8,128)(2,1)S(1)} %get-tuple-element.118), channel_id=1, source_target_pairs={{0,13},{1,12},{2,15},{3,14},{4,9},{5,8},{6,11},{7,10},{8,5},{9,4},... | collective-permute-start | bytes 442376 | tf_op jit(solution)/shard_map/ppermute | solution.py:349
  40.1 19.1 %collective-permute-start.11 = (bf16[576,128]{1,0:T(8,128)(2,1)S(1)}, bf16[576,128]{1,0:T(8,128)(2,1)S(1)}, u32[]{:S(2)}, u32[]{:S(2)}) collective-permute-start(bf16[576,128]{1,0:T(8,128)(2,1)S(1)} %get-tuple-element.119), channel_id=1, source_target_pairs={{0,6},{1,7},{2,4},{3,5},{4,2},{5,3},{6,0},{7,1},{8,14},{9,15},{10,... | collective-permute-start | bytes 442376 | tf_op jit(solution)/shard_map/ppermute | solution.py:349
  44.1 15.1 %collective-permute-start.12 = (bf16[576,128]{1,0:T(8,128)(2,1)S(1)}, bf16[576,128]{1,0:T(8,128)(2,1)S(1)}, u32[]{:S(2)}, u32[]{:S(2)}) collective-permute-start(bf16[576,128]{1,0:T(8,128)(2,1)S(1)} %get-tuple-element.120), channel_id=1, source_target_pairs={{0,14},{1,15},{2,12},{3,13},{4,10},{5,11},{6,8},{7,9},{8,6},{9,7},... | collective-permute-start | bytes 442376 | tf_op jit(solution)/shard_map/ppermute | solution.py:349
  53.2 10.5 %collective-permute-start.14 = (bf16[576,128]{1,0:T(8,128)(2,1)S(1)}, bf16[576,128]{1,0:T(8,128)(2,1)S(1)}, u32[]{:S(2)}, u32[]{:S(2)}) collective-permute-start(bf16[576,128]{1,0:T(8,128)(2,1)S(1)} %get-tuple-element.122), channel_id=1, source_target_pairs={{0,15},{1,14},{2,13},{3,12},{4,11},{5,10},{6,9},{7,8},{8,7},{9,6},... | collective-permute-start | bytes 442376 | tf_op jit(solution)/shard_map/ppermute | solution.py:349
  63.8 11.3 %collective-permute-start.15 = (bf16[16,128,128]{2,1,0:T(8,128)(2,1)S(1)}, bf16[16,128,128]{2,1,0:T(8,128)(2,1)S(1)}, u32[]{:S(2)}, u32[]{:S(2)}) collective-permute-start(bf16[16,128,128]{2,1,0:T(8,128)(2,1)S(1)} %collect_shared.1.rest_16_), channel_id=1, source_target_pairs={{0,1},{1,0},{2,3},{3,2},{4,5},{5,4},{6,7},{7,6},{8,9},{9,8},{10,11... | collective-permute-start | bytes 1572872 | tf_op jit(solution)/shard_map/ppermute | solution.py:370
  64.8 35.8 %collective-permute-start.31 = (bf16[384,128]{1,0:T(8,128)(2,1)}, bf16[384,128]{1,0:T(8,128)(2,1)}, u32[]{:S(2)}, u32[]{:S(2)}) collective-permute-start(bf16[384,128]{1,0:T(8,128)(2,1)} %get-tuple-element.156), channel_id=1, source_target_pairs={{0,8},{1,9},{2,10},{3,11},{4,12},{5,13},{6,14},{7,15},{8,0},{9,1},... | collective-permute-start | bytes 294920 | tf_op jit(solution)/shard_map/ppermute | solution.py:349
  68.3 32.5 %collective-permute-start.33 = (bf16[384,128]{1,0:T(8,128)(2,1)}, bf16[384,128]{1,0:T(8,128)(2,1)}, u32[]{:S(2)}, u32[]{:S(2)}) collective-permute-start(bf16[384,128]{1,0:T(8,128)(2,1)} %get-tuple-element.158), channel_id=1, source_target_pairs={{0,9},{1,8},{2,11},{3,10},{4,13},{5,12},{6,15},{7,14},{8,1},{9,0},... | collective-permute-start | bytes 294920 | tf_op jit(solution)/shard_map/ppermute | solution.py:349
  68.4 32.5 %collective-permute-start.35 = (bf16[384,128]{1,0:T(8,128)(2,1)}, bf16[384,128]{1,0:T(8,128)(2,1)}, u32[]{:S(2)}, u32[]{:S(2)}) collective-permute-start(bf16[384,128]{1,0:T(8,128)(2,1)} %get-tuple-element.160), channel_id=1, source_target_pairs={{0,10},{1,11},{2,8},{3,9},{4,14},{5,15},{6,12},{7,13},{8,2},{9,3},... | collective-permute-start | bytes 294920 | tf_op jit(solution)/shard_map/ppermute | solution.py:349
  70.4 31.4 %collective-permute-start.37 = (bf16[384,128]{1,0:T(8,128)(2,1)}, bf16[384,128]{1,0:T(8,128)(2,1)}, u32[]{:S(2)}, u32[]{:S(2)}) collective-permute-start(bf16[384,128]{1,0:T(8,128)(2,1)} %get-tuple-element.162), channel_id=1, source_target_pairs={{0,11},{1,10},{2,9},{3,8},{4,15},{5,14},{6,13},{7,12},{8,3},{9,2},... | collective-permute-start | bytes 294920 | tf_op jit(solution)/shard_map/ppermute | solution.py:349
  101.8 8.7 %collective-permute-start.20 = (bf16[192,128]{1,0:T(8,128)(2,1)S(1)}, bf16[192,128]{1,0:T(8,128)(2,1)S(1)}, u32[]{:S(2)}, u32[]{:S(2)}) collective-permute-start(bf16[192,128]{1,0:T(8,128)(2,1)S(1)} %get-tuple-element.144), channel_id=1, source_target_pairs={{0,10},{1,11},{2,8},{3,9},{4,14},{5,15},{6,12},{7,13},{8,2},{9,3},... | collective-permute-start | bytes 147464 | tf_op jit(solution)/shard_map/ppermute | solution.py:349
  105.2 13.6 %collective-permute-start.32 = (bf16[384,128]{1,0:T(8,128)(2,1)S(1)}, bf16[384,128]{1,0:T(8,128)(2,1)S(1)}, u32[]{:S(2)}, u32[]{:S(2)}) collective-permute-start(bf16[384,128]{1,0:T(8,128)(2,1)S(1)} %copy-done.18), channel_id=1, source_target_pairs={{0,1},{1,0},{2,3},{3,2},{4,5},{5,4},{6,7},{7,6},{8,9},{9,8},{10,11... | collective-permute-start | bytes 294920 | tf_op jit(solution)/shard_map/ppermute | solution.py:349
  118.9 10.5 %collective-permute-start.41 = (bf16[384,128]{1,0:T(8,128)(2,1)}, bf16[384,128]{1,0:T(8,128)(2,1)S(1)}, u32[]{:S(2)}, u32[]{:S(2)}) collective-permute-start(bf16[384,128]{1,0:T(8,128)(2,1)} %get-tuple-element.166), channel_id=1, source_target_pairs={{0,13},{1,12},{2,15},{3,14},{4,9},{5,8},{6,11},{7,10},{8,5},{9,4},... | collective-permute-start | bytes 294920 | tf_op jit(solution)/shard_map/ppermute | solution.py:349
  121.3 9.4 %collective-permute-start.42 = (bf16[384,128]{1,0:T(8,128)(2,1)}, bf16[384,128]{1,0:T(8,128)(2,1)S(1)}, u32[]{:S(2)}, u32[]{:S(2)}) collective-permute-start(bf16[384,128]{1,0:T(8,128)(2,1)} %get-tuple-element.167), channel_id=1, source_target_pairs={{0,6},{1,7},{2,4},{3,5},{4,2},{5,3},{6,0},{7,1},{8,14},{9,15},{10,... | collective-permute-start | bytes 294920 | tf_op jit(solution)/shard_map/ppermute | solution.py:349
  123.3 9.3 %collective-permute-start.43 = (bf16[384,128]{1,0:T(8,128)(2,1)}, bf16[384,128]{1,0:T(8,128)(2,1)S(1)}, u32[]{:S(2)}, u32[]{:S(2)}) collective-permute-start(bf16[384,128]{1,0:T(8,128)(2,1)} %get-tuple-element.168), channel_id=1, source_target_pairs={{0,14},{1,15},{2,12},{3,13},{4,10},{5,11},{6,8},{7,9},{8,6},{9,7},... | collective-permute-start | bytes 294920 | tf_op jit(solution)/shard_map/ppermute | solution.py:349
  124.7 11.0 %collective-permute-start.44 = (bf16[384,128]{1,0:T(8,128)(2,1)}, bf16[384,128]{1,0:T(8,128)(2,1)S(1)}, u32[]{:S(2)}, u32[]{:S(2)}) collective-permute-start(bf16[384,128]{1,0:T(8,128)(2,1)} %get-tuple-element.169), channel_id=1, source_target_pairs={{0,7},{1,6},{2,5},{3,4},{4,3},{5,2},{6,1},{7,0},{8,15},{9,14},{10,... | collective-permute-start | bytes 294920 | tf_op jit(solution)/shard_map/ppermute | solution.py:349
  125.5 10.5 %collective-permute-start.45 = (bf16[384,128]{1,0:T(8,128)(2,1)}, bf16[384,128]{1,0:T(8,128)(2,1)S(1)}, u32[]{:S(2)}, u32[]{:S(2)}) collective-permute-start(bf16[384,128]{1,0:T(8,128)(2,1)} %get-tuple-element.170), channel_id=1, source_target_pairs={{0,15},{1,14},{2,13},{3,12},{4,11},{5,10},{6,9},{7,8},{8,7},{9,6},... | collective-permute-start | bytes 294920 | tf_op jit(solution)/shard_map/ppermute | solution.py:349
  129.4 22.0 %collective-permute-start.26 = (bf16[192,128]{1,0:T(8,128)(2,1)}, bf16[192,128]{1,0:T(8,128)(2,1)S(1)}, u32[]{:S(2)}, u32[]{:S(2)}) collective-permute-start(bf16[192,128]{1,0:T(8,128)(2,1)} %copy-done.22), channel_id=1, source_target_pairs={{0,13},{1,12},{2,15},{3,14},{4,9},{5,8},{6,11},{7,10},{8,5},{9,4},... | collective-permute-start | bytes 147464 | tf_op jit(solution)/shard_map/ppermute | solution.py:349
  130.8 24.0 %collective-permute-start.27 = (bf16[192,128]{1,0:T(8,128)(2,1)}, bf16[192,128]{1,0:T(8,128)(2,1)S(1)}, u32[]{:S(2)}, u32[]{:S(2)}) collective-permute-start(bf16[192,128]{1,0:T(8,128)(2,1)} %copy-done.21), channel_id=1, source_target_pairs={{0,6},{1,7},{2,4},{3,5},{4,2},{5,3},{6,0},{7,1},{8,14},{9,15},{10,... | collective-permute-start | bytes 147464 | tf_op jit(solution)/shard_map/ppermute | solution.py:349
  132.6 22.2 %collective-permute-start.28 = (bf16[192,128]{1,0:T(8,128)(2,1)}, bf16[192,128]{1,0:T(8,128)(2,1)S(1)}, u32[]{:S(2)}, u32[]{:S(2)}) collective-permute-start(bf16[192,128]{1,0:T(8,128)(2,1)} %copy-done.20), channel_id=1, source_target_pairs={{0,14},{1,15},{2,12},{3,13},{4,10},{5,11},{6,8},{7,9},{8,6},{9,7},... | collective-permute-start | bytes 147464 | tf_op jit(solution)/shard_map/ppermute | solution.py:349
  135.6 19.3 %collective-permute-start.29 = (bf16[192,128]{1,0:T(8,128)(2,1)}, bf16[192,128]{1,0:T(8,128)(2,1)S(1)}, u32[]{:S(2)}, u32[]{:S(2)}) collective-permute-start(bf16[192,128]{1,0:T(8,128)(2,1)} %copy-done.19), channel_id=1, source_target_pairs={{0,7},{1,6},{2,5},{3,4},{4,3},{5,2},{6,1},{7,0},{8,15},{9,14},{10,... | collective-permute-start | bytes 147464 | tf_op jit(solution)/shard_map/ppermute | solution.py:349
  136.1 19.2 %collective-permute-start.30 = (bf16[192,128]{1,0:T(8,128)(2,1)S(1)}, bf16[192,128]{1,0:T(8,128)(2,1)S(1)}, u32[]{:S(2)}, u32[]{:S(2)}) collective-permute-start(bf16[192,128]{1,0:T(8,128)(2,1)S(1)} %get-tuple-element.154), channel_id=1, source_target_pairs={{0,15},{1,14},{2,13},{3,12},{4,11},{5,10},{6,9},{7,8},{8,7},{9,6},... | collective-permute-start | bytes 147464 | tf_op jit(solution)/shard_map/ppermute | solution.py:349
  155.3 9.6 %collective-permute-start.50 = (bf16[128,128]{1,0:T(8,128)(2,1)S(1)}, bf16[128,128]{1,0:T(8,128)(2,1)S(1)}, u32[]{:S(2)}, u32[]{:S(2)}) collective-permute-start(bf16[128,128]{1,0:T(8,128)(2,1)S(1)} %get-tuple-element.176), channel_id=1, source_target_pairs={{0,10},{1,11},{2,8},{3,9},{4,14},{5,15},{6,12},{7,13},{8,2},{9,3},... | collective-permute-start | bytes 98312 | tf_op jit(solution)/shard_map/ppermute | solution.py:349
  (54 other events, 862.0 us)

commit v3 on v0

--- a/solution.py
+++ b/solution.py
@@ -1,15 +1,36 @@
+import functools
+import math
+
 import jax
 import jax.numpy as jnp
 from jax import lax
+from jax.experimental import pallas as pl
+from jax.experimental.pallas import tpu as pltpu
 from jax.sharding import PartitionSpec as P
 
 HEADS = 40
 HEAD_DIM = 128
 TILE = 128
 KMAX = 12
-
+HALF = TILE // 2
 
 NORM_EPS = 1e-06
+MASKED = -1e30
+EXP2_SCALE = HEAD_DIM ** (-0.5) * math.log2(math.e)
+SIZES = (2, 4, 6, 8, 10, 12)
+TOGETHER = 4
+VMEM_LIMIT = 12 * 1024 * 1024
+
+HEAD_ROWS = 3 * TILE
+SHARED_Q = 2 * HEAD_ROWS
+SHARED_KV = SHARED_Q + HALF
+ROWS = SHARED_KV + TILE
+BACK_ROWS = 2 * TILE + HALF
+
+HBM = pl.BlockSpec(memory_space=pltpu.HBM)
+SMEM = pl.BlockSpec(memory_space=pltpu.SMEM)
+VMEM = pl.BlockSpec(memory_space=pltpu.VMEM)
+PARAMS = pltpu.CompilerParams(vmem_limit_bytes=VMEM_LIMIT)
 
 
 def rms_norm(values_in, gain):
@@ -18,13 +39,398 @@
     return (widened * inverse * gain).astype(jnp.bfloat16)
 
 
+def head_of(device, which, heads_pair):
+    base = (device // 2) * heads_pair
+    core = device % 2
+    if which == 2:
+        return base + 2
+    return base + core * 3 + which
+
+
+def lanes_of(head):
+    return pl.ds(pl.multiple_of(head * HEAD_DIM, HEAD_DIM), HEAD_DIM)
+
+
+def alternate(far, near):
+    order = []
+    for index in range(max(len(far), len(near))):
+        order += far[index : index + 1] + near[index : index + 1]
+    return order
+
+
+def partners(devices):
+    half = devices // 2
+    far = list(range(devices - 1, half - 1, -1))
+    near = list(range(half // 2, half)) + list(range(1, half // 2))
+    return far, near
+
+
+def pack_kernel(masks, heads_pair, me_ref, q_hbm, k_hbm, v_hbm, qg_hbm, kg_hbm, *rest):
+    out_refs = rest[: len(masks)]
+    q_ref, k_ref, v_ref, qg_ref, kg_ref, q_norm, k_norm, sems = rest[len(masks) :]
+    me = me_ref[0]
+    loads = [
+        pltpu.make_async_copy(src, dst, sems.at[at])
+        for at, (src, dst) in enumerate(
+            (
+                (qg_hbm, qg_ref),
+                (kg_hbm, kg_ref),
+                (q_hbm, q_ref),
+                (k_hbm, k_ref),
+                (v_hbm, v_ref),
+            )
+        )
+    ]
+    for load in loads:
+        load.start()
+    loads[0].wait()
+    loads[1].wait()
+    width = q_ref.shape[1]
+    step = 8 * HEAD_DIM
+    for load, src, gain, dst in (
+        (loads[2], q_ref, qg_ref, q_norm),
+        (loads[3], k_ref, kg_ref, k_norm),
+    ):
+        load.wait()
+        total = jnp.zeros((TILE, HEAD_DIM), jnp.float32)
+        for lane in range(0, width, HEAD_DIM):
+            part = src[:, lane : lane + HEAD_DIM].astype(jnp.float32)
+            total += part * part
+        mean = jnp.sum(total, axis=1, keepdims=True) * (1.0 / width)
+        inverse = lax.rsqrt(mean + NORM_EPS)
+        for lane in range(0, width, step):
+            part = src[:, lane : lane + step].astype(jnp.float32)
+            dst[:, lane : lane + step] = (part * inverse * gain[:, lane : lane + step]).astype(
+                jnp.bfloat16
+            )
+    loads[4].wait()
+    for mask, out in zip(masks, out_refs):
+        to = lax.bitwise_xor(me, mask)
+        core = to % 2
+        for which in range(2):
+            lanes = lanes_of(head_of(to, which, heads_pair))
+            row = which * HEAD_ROWS
+            out[row : row + TILE] = q_norm[:, lanes]
+            out[row + TILE : row + 2 * TILE] = k_norm[:, lanes]
+            out[row + 2 * TILE : row + 3 * TILE] = v_ref[:, lanes]
+        lanes = lanes_of(head_of(to, 2, heads_pair))
+        half = pl.ds(pl.multiple_of(core * HALF, HALF), HALF)
+        out[SHARED_Q:SHARED_KV] = q_norm[half, lanes]
+
+        @pl.when(core == 0)
+        def _(out=out, lanes=lanes):
+            out[SHARED_KV:ROWS] = k_norm[:, lanes]
+
+        @pl.when(core == 1)
+        def _(out=out, lanes=lanes):
+            out[SHARED_KV:ROWS] = v_ref[:, lanes]
+
+
+def pack(me, query, key, value, query_gain, key_gain, masks, heads_pair):
+    gain = pltpu.VMEM((1, query.shape[1]), jnp.float32)
+    return pl.pallas_call(
+        functools.partial(pack_kernel, masks, heads_pair),
+        out_shape=[jax.ShapeDtypeStruct((ROWS, HEAD_DIM), jnp.bfloat16)] * len(masks),
+        in_specs=[SMEM] + [HBM] * 5,
+        out_specs=[VMEM] * len(masks),
+        scratch_shapes=[pltpu.VMEM(query.shape, jnp.bfloat16)] * 3
+        + [gain] * 2
+        + [pltpu.VMEM(query.shape, jnp.bfloat16)] * 2
+        + [pltpu.SemaphoreType.DMA((5,))],
+        compiler_params=PARAMS,
+        name="norm_pack",
+    )(me, query, key, value, query_gain[None, :], key_gain[None, :])
+
+
+def collect_kernel(masks, me_ref, *rest):
+    in_refs, out_ref = rest[: len(masks)], rest[len(masks)]
+    me = me_ref[0]
+    for mask, ref in zip(masks, in_refs):
+        out_ref[lax.bitwise_xor(me, mask)] = ref[SHARED_KV:ROWS]
+
+
+def collect(me, arrived, masks):
+    return pl.pallas_call(
+        functools.partial(collect_kernel, masks),
+        out_shape=jax.ShapeDtypeStruct((len(masks), TILE, HEAD_DIM), jnp.bfloat16),
+        in_specs=[SMEM] + [VMEM] * len(masks),
+        out_specs=VMEM,
+        compiler_params=PARAMS,
+        name="collect_shared",
+    )(me, *arrived)
+
+
+def attend_together(counts, list_at, query_of, key_of, value_of, store):
+    longest = functools.reduce(jnp.maximum, counts)
+    least = 0
+    for size in SIZES:
+
+        @pl.when((longest > least) & (longest <= size))
+        def _(size=size):
+            column = lax.broadcasted_iota(jnp.int32, (1, size * TILE), 1)
+            units = range(len(counts))
+            picked = [[list_at(unit, slot) for slot in range(size)] for unit in units]
+            scores = []
+            for unit in units:
+                keys = jnp.concatenate([key_of(block) for block in picked[unit]], axis=0)
+                scores.append(
+                    lax.dot_general(
+                        query_of(unit),
+                        keys,
+                        (((1,), (1,)), ((), ())),
+                        preferred_element_type=jnp.float32,
+                    )
+                    + jnp.where(column < counts[unit] * TILE, 0.0, MASKED)
+                )
+            weights, totals = [], []
+            for unit in units:
+                peak = jnp.max(scores[unit], axis=1, keepdims=True)
+                wide = jnp.exp2((scores[unit] - peak) * EXP2_SCALE)
+                totals.append(jnp.sum(wide, axis=1, keepdims=True))
+                weights.append(wide.astype(jnp.bfloat16))
+            summed = []
+            for unit in units:
+                values = jnp.concatenate([value_of(block) for block in picked[unit]], axis=0)
+                summed.append(
+                    jnp.dot(weights[unit], values, preferred_element_type=jnp.float32)
+                )
+            for unit in units:
+                store(unit, (summed[unit] / totals[unit]).astype(jnp.bfloat16))
+
+        least = size
+
+
+def attend_own(me, masks, head, lists_ref, counts_ref, held, store):
+    blocks = [lax.bitwise_xor(me, mask) for mask in masks]
+    devices = held.shape[0]
+    row = head * HEAD_ROWS
+    rows = [pl.ds(pl.multiple_of(row + part * TILE, TILE), TILE) for part in range(3)]
+    attend_together(
+        [counts_ref[head * devices + block] for block in blocks],
+        lambda unit, slot: lists_ref[(head * devices + blocks[unit]) * KMAX + slot],
+        lambda unit: held[blocks[unit], rows[0]],
+        lambda at: held[at, rows[1]],
+        lambda at: held[at, rows[2]],
+        store,
+    )
+
+
+def attend_shared(me, masks, lists_ref, counts_ref, held, shared, store):
+    blocks = [lax.bitwise_xor(me, mask) for mask in masks]
+    devices = held.shape[0]
+    attend_together(
+        [counts_ref[2 * devices + block] for block in blocks],
+        lambda unit, slot: lists_ref[(2 * devices + blocks[unit]) * KMAX + slot],
+        lambda unit: held[blocks[unit], SHARED_Q:SHARED_KV],
+        lambda at: shared[0, at],
+        lambda at: shared[1, at],
+        store,
+    )
+
+
+def attend_first_kernel(masks, first, me_ref, lists_ref, counts_ref, *rest):
+    in_refs = rest[: len(masks)]
+    held, results = rest[len(masks) :]
+    me = me_ref[0]
+    for mask, ref in zip(masks, in_refs):
+        held[lax.bitwise_xor(me, mask)] = ref[0:SHARED_KV]
+
+    def step(head, carry):
+        def store(unit, values):
+            results[unit, pl.ds(pl.multiple_of(head * TILE, TILE), TILE)] = values
+
+        attend_own(me, first, head, lists_ref, counts_ref, held, store)
+        return carry
+
+    lax.fori_loop(0, 2, step, 0)
+
+
+def attend_first(me, tables, arrived, masks, first):
+    devices = len(masks)
+    return pl.pallas_call(
+        functools.partial(attend_first_kernel, masks, first),
+        out_shape=[
+            jax.ShapeDtypeStruct((devices, SHARED_KV, HEAD_DIM), jnp.bfloat16),
+            jax.ShapeDtypeStruct((len(first), 2 * TILE, HEAD_DIM), jnp.bfloat16),
+        ],
+        in_specs=[SMEM] * 3 + [VMEM] * devices,
+        out_specs=[VMEM] * 2,
+        compiler_params=PARAMS,
+        cost_estimate=attend_cost(2 * len(first)),
+        name="attend_first",
+    )(me, *tables, *arrived)
+
+
+def attend_second_kernel(
+    first, me_ref, lists_ref, counts_ref, held, own_ref, other_ref, begun, shared, *out_refs
+):
+    me = me_ref[0]
+    core = me % 2
+    shared[core] = own_ref[...]
+    shared[1 - core] = other_ref[...]
+    for unit, out in enumerate(out_refs):
+        out[0 : 2 * TILE] = begun[unit]
+
+    def store(unit, values):
+        out_refs[unit][2 * TILE : BACK_ROWS] = values
+
+    attend_shared(me, first, lists_ref, counts_ref, held, shared, store)
+
+
+def attend_second(me, tables, held, own, other, begun, first):
+    devices = held.shape[0]
+    back = jax.ShapeDtypeStruct((BACK_ROWS, HEAD_DIM), jnp.bfloat16)
+    outs = pl.pallas_call(
+        functools.partial(attend_second_kernel, first),
+        out_shape=[jax.ShapeDtypeStruct((2, devices, TILE, HEAD_DIM), jnp.bfloat16)]
+        + [back] * len(first),
+        in_specs=[SMEM] * 3 + [VMEM] * 4,
+        out_specs=[VMEM] * (1 + len(first)),
+        compiler_params=PARAMS,
+        cost_estimate=attend_cost(len(first)),
+        name="attend_second",
+    )(me, *tables, held, own, other, begun)
+    return outs[0], list(outs[1:])
+
+
+def attend_rest_kernel(masks, me_ref, lists_ref, counts_ref, held, shared, *rest):
+    out_refs, results = rest[: len(masks)], rest[len(masks)]
+    me = me_ref[0]
+    groups = len(masks) // TOGETHER
+
+    def own_step(index, carry):
+        group, head = index // 2, index % 2
+        start = group * TOGETHER
+
+        def store(unit, values):
+            results[start + unit, pl.ds(pl.multiple_of(head * TILE, TILE), TILE)] = values
+
+        some = [start + unit for unit in range(TOGETHER)]
+        attend_own(me, some, head, lists_ref, counts_ref, held, store)
+        return carry
+
+    def shared_step(group, carry):
+        start = group * TOGETHER
+
+        def store(unit, values):
+            results[start + unit, 2 * TILE : BACK_ROWS] = values
+
+        some = [start + unit for unit in range(TOGETHER)]
+        attend_shared(me, some, lists_ref, counts_ref, held, shared, store)
+        return carry
+
+    lax.fori_loop(0, 2 * groups, own_step, 0)
+    lax.fori_loop(0, groups, shared_step, 0)
+    for mask, out in zip(masks, out_refs):
+        out[...] = results[mask]
+
+
+def attend_rest(me, tables, held, shared, masks):
+    back = jax.ShapeDtypeStruct((BACK_ROWS, HEAD_DIM), jnp.bfloat16)
+    return pl.pallas_call(
+        functools.partial(attend_rest_kernel, masks),
+        out_shape=[back] * len(masks),
+        in_specs=[SMEM] * 3 + [VMEM] * 2,
+        out_specs=[VMEM] * len(masks),
+        scratch_shapes=[pltpu.VMEM((len(masks), BACK_ROWS, HEAD_DIM), jnp.bfloat16)],
+        compiler_params=PARAMS,
+        cost_estimate=attend_cost(3 * len(masks)),
+        name="attend_rest",
+    )(me, *tables, held, shared)
+
+
+def attend_cost(units):
+    return pl.CostEstimate(
+        flops=units * 4 * 4 * TILE * TILE * HEAD_DIM,
+        bytes_accessed=units * 4 * TILE * HEAD_DIM * 2,
+        transcendentals=units * 4 * TILE * TILE,
+    )
+
+
+def assemble_kernel(masks, heads_pair, me_ref, *rest):
+    in_refs = rest[: len(masks)]
+    out_ref, sems = rest[len(masks) :]
+    me = me_ref[0]
+    copies = []
+
+    def add(src, dst):
+        copies.append(pltpu.make_async_copy(src, dst, sems.at[len(copies)]))
+
+    for mask, ref in zip(masks, in_refs):
+        source = lax.bitwise_xor(me, mask)
+        for which in range(2):
+            lanes = lanes_of(head_of(source, which, heads_pair))
+            add(ref.at[pl.ds(which * TILE, TILE)], out_ref.at[:, lanes])
+        lanes = lanes_of(head_of(source, 2, heads_pair))
+        half = pl.ds(pl.multiple_of(source % 2 * HALF, HALF), HALF)
+        add(ref.at[pl.ds(2 * TILE, HALF)], out_ref.at[half, lanes])
+    for copy in copies:
+        copy.start()
+    for copy in copies:
+        copy.wait()
+
+
+def assemble(me, back, width, masks, heads_pair):
+    return pl.pallas_call(
+        functools.partial(assemble_kernel, masks, heads_pair),
+        out_shape=jax.ShapeDtypeStruct((TILE, width), jnp.bfloat16),
+        in_specs=[SMEM] + [VMEM] * len(masks),
+        out_specs=pl.BlockSpec(memory_space=pl.ANY),
+        scratch_shapes=[pltpu.SemaphoreType.DMA((3 * len(masks),))],
+        compiler_params=PARAMS,
+        name="assemble",
+    )(me, *back)
+
+
+def exchange(parts, masks, devices):
+    return [
+        part
+        if mask == 0
+        else lax.ppermute(part, "ulysses", [(index, index ^ mask) for index in range(devices)])
+        for mask, part in zip(masks, parts)
+    ]
+
+
+def local_pairs(query, key, value, query_gain, key_gain, key_blocks, block_counts):
+    devices = lax.axis_size("ulysses")
+    heads_pair = 2 * HEADS // devices
+    index = lax.axis_index("ulysses")
+    me = index.astype(jnp.int32).reshape(1)
+    far, near = partners(devices)
+    masks = [0] + alternate(far, near)
+    first, later = far[:TOGETHER], far[TOGETHER:]
+    rest = alternate(later, near) + [0]
+
+    leaving = pack(me, query, key, value, query_gain, key_gain, masks, heads_pair)
+    early = exchange(leaving[:2], masks[:2], devices)
+    early[1], key_blocks, block_counts = lax.optimization_barrier(
+        (early[1], key_blocks, block_counts)
+    )
+    heads = [head_of(index, which, heads_pair) for which in range(3)]
+    lists = [lax.dynamic_index_in_dim(key_blocks, head, 0, False) for head in heads]
+    counts = [lax.dynamic_index_in_dim(block_counts, head, 0, False) for head in heads]
+    tables = (jnp.stack(lists).reshape(-1), jnp.stack(counts).reshape(-1))
+    middle = len(masks) - 2
+    late, tables = lax.optimization_barrier((leaving[middle:], tables))
+    arrived = early + exchange(leaving[2:middle] + late, masks[2:], devices)
+    own = collect(me, arrived, masks)
+    (other,) = exchange([own], [1], devices)
+    held, begun = attend_first(me, tables, arrived, masks, first)
+    shared, results = attend_second(me, tables, held, own, other, begun, first)
+    back = exchange(results, first, devices)
+    back[0], held = lax.optimization_barrier((back[0], held))
+    results = attend_rest(me, tables, held, shared, rest)
+    back += exchange(results, rest, devices)
+    return assemble(me, back, query.shape[1], first + rest, heads_pair)
+
+
 def pick_group():
     for group_size in (8, 4, 2, 1):
         return group_size
     return 1
 
 
-def local(query, key, value, query_gain, key_gain, key_blocks, block_counts):
+def local_any(query, key, value, query_gain, key_gain, key_blocks, block_counts):
     devices = lax.axis_size("ulysses")
     my_index = lax.axis_index("ulysses")
     tok_dev = query.shape[0]
@@ -80,7 +486,7 @@
         live_mask = (jnp.arange(KMAX, dtype=jnp.int32)[None, :] < live_count[:, None])[
             :, None, :, None
         ]
-        logit_matrix = jnp.where(live_mask, logit_matrix, -1e30)
+        logit_matrix = jnp.where(live_mask, logit_matrix, MASKED)
         row_peak = jnp.max(logit_matrix, axis=(2, 3), keepdims=True)
         weights = jnp.where(live_mask, jnp.exp(logit_matrix - row_peak), 0.0)
         row_denominator = jnp.sum(weights, axis=(2, 3))
@@ -104,6 +510,15 @@
     return gathered.astype(jnp.bfloat16).reshape(tok_dev, HEADS * HEAD_DIM)
 
 
+def local(query, *rest):
+    devices = lax.axis_size("ulysses")
+    power_of_two = devices & (devices - 1) == 0
+    five_a_pair = devices % 2 == 0 and devices * 5 == HEADS * 2
+    if power_of_two and five_a_pair and query.shape[0] == TILE:
+        return local_pairs(query, *rest)
+    return local_any(query, *rest)
+
+
 def solution(mesh):
     in_specs = (
         P(("parts", "ulysses"), None),

time: 445 us -> 148 us (0.33); the launches traced: 438 us -> 147 us
  local copies, waits for them, and re-layouts: 152 us -> 9.51 us
  waiting for transfers between devices: 191 us -> 66.6 us
  matrix products: 30.2 us -> 0 us
  Pallas kernels: 0 us -> 20.5 us
  other arithmetic: 19.9 us -> 0.08 us
  starting transfers between devices: 44.1 us -> 50.4 us
    all_to_all x2 -> x0, waiting for transfers between devices: 191 us -> none  [the longest x1 150 us: local(): lax.all_to_all(outgoing, 'ulysses', split_axis=1, concat_axis=1, tiled=True)]
    gather x27 -> x0, local copies, waits for them, and re-layouts: 84 us -> none  [the longest x5 22.9 us: attend_group(): key_panels = resident[unit_slots[:, None], 1, key_lists]]
    ppermute x0 -> x31, waiting for transfers between devices: none -> 66.6 us  [exchange(): lax.ppermute(part, 'ulysses', [(index, index ^ mask) for index in range(d...]
    ppermute x0 -> x31, starting transfers between devices: none -> 50.4 us  [exchange(): lax.ppermute(part, 'ulysses', [(index, index ^ mask) for index in range(d...]
    all_to_all x2 -> x0, starting transfers between devices: 44.1 us -> none  [the longest x1 36.5 us: local(): lax.all_to_all(leaving, 'ulysses', split_axis=1, concat_axis=0, tiled=True)]
    dot_general x11 -> x0, matrix products: 30.2 us -> none  [the longest x5 24.4 us: attend_group(): jnp.einsum('gqjk,gjkd->gqd', weights.astype(jnp.bfloat16), value_panels,...]
    reshape x1 -> x2, local copies, waits for them, and re-layouts: 24.2 us -> 0.18 us  [local_pairs(): tables = (jnp.stack(lists).reshape(-1), jnp.stack(counts).reshape(-1))]
    pallas_call x0 -> x6, Pallas kernels: none -> 20.5 us  [the longest x1 9.83 us: attend_rest(): pl.pallas_call(functools.partial(attend_rest_kernel, masks), out_shape=[b...]
  transfers between devices with their start and end apart: 2 -> 31, of which waited for: 2 -> 17; matrix products, arithmetic and copies ran while one was open for 0% -> 1% of each run, Pallas kernels for 0% -> 9%
where the time goes in v3:
time: 148 us; the launch traced here: 147 us
  waiting for transfers between devices  66.6 us (45%)
  starting transfers between devices  50.4 us (34%)
  Pallas kernels  20.5 us (14%)
  local copies, waits for them, and re-layouts  9.51 us (6%)
    ppermute x31, waiting for transfers between devices, exchange(): lax.ppermute(part, 'ulysses', [(index, index ^ mask) for index in range(d...  66.6 us
    ppermute x31, starting transfers between devices, exchange(): lax.ppermute(part, 'ulysses', [(index, index ^ mask) for index in range(d...  50.4 us
    pallas_call x1, Pallas kernels, attend_rest(): pl.pallas_call(functools.partial(attend_rest_kernel, masks), out_shape=[b...  9.83 us
    unnamed x20, local copies, waits for them, and re-layouts  7.5 us
    pallas_call x1, Pallas kernels, pack(): pl.pallas_call(functools.partial(pack_kernel, masks, heads_pair), out_sha...  4.27 us
    pallas_call x1, Pallas kernels, attend_first(): pl.pallas_call(functools.partial(attend_first_kernel, masks, first), out_...  3.13 us
  transfers between devices with their start and end apart: 31, of which 17 were waited for; matrix products, arithmetic and copies ran while one was open for 1% of the time, Pallas kernels for 9%

profile of v3, /device:TPU:0, one launch (start us, length us, event | category | flops | bytes accessed | tf_op | source)
XLA Modules:
  0.0 147.4 jit_solution(14924411362643528629)
XLA Ops:
  5.4 4.3 %norm_pack.1 = (bf16[960,128]{1,0:T(8,128)(2,1)S(1)}, bf16[960,128]{1,0:T(8,128)(2,1)S(1)}, bf16[960,128]{1,0:T(8,128)(2,1)S(1)}, bf16[960,128]{1,0:T(8,128)(2,1...) custom-call(s32[1]{0:T(128)} %bitcast.me_ref, ...), custom_call_target="tpu_custom_call" | custom-call | tf_op jit(solution)/shard_map/norm_pack/pallas_call | solution.py:131
  11.8 5.4 %collective-permute-start = (bf16[960,128]{1,0:T(8,128)(2,1)S(1)}, bf16[960,128]{1,0:T(8,128)(2,1)S(1)}, u32[]{:S(2)}, u32[]{:S(2)}) collective-permute-start(bf16[960,128]{1,0:T(8,128)(2,1)S(1)} %get-tuple-element.51), channel_id=1, source_target_pairs={{0,15},{1,14},{2,13},{3,12},{4,11},{5,10},{6,9},{7,8},{8,7},{9,6},... | collective-permute-start | bytes 737288 | tf_op jit(solution)/shard_map/ppermute | solution.py:389
  19.3 2.6 %collective-permute-start.4 = (bf16[960,128]{1,0:T(8,128)(2,1)S(1)}, bf16[960,128]{1,0:T(8,128)(2,1)S(1)}, u32[]{:S(2)}, u32[]{:S(2)}) collective-permute-start(bf16[960,128]{1,0:T(8,128)(2,1)S(1)} %get-tuple-element.61), channel_id=1, source_target_pairs={{0,13},{1,12},{2,15},{3,14},{4,9},{5,8},{6,11},{7,10},{8,5},{9,4},... | collective-permute-start | bytes 737288 | tf_op jit(solution)/shard_map/ppermute | solution.py:389
  21.9 1.8 %collective-permute-done.rest_1_ = bf16[960,128]{1,0:T(8,128)(2,1)S(1)} collective-permute-done((bf16[960,128]{1,0:T(8,128)(2,1)S(1)}, bf16[960,128]{1,0:T(8,128)(2,1)S(1)}, u32[]{:S(2)}, u32[]{:S(2)}) %collective-permute-start) | collective-permute-done | bytes 245792 | tf_op jit(solution)/shard_map/ppermute | solution.py:389
  23.6 6.5 %collective-permute-start.5 = (bf16[960,128]{1,0:T(8,128)(2,1)}, bf16[960,128]{1,0:T(8,128)(2,1)S(1)}, u32[]{:S(2)}, u32[]{:S(2)}) collective-permute-start(bf16[960,128]{1,0:T(8,128)(2,1)} %get-tuple-element.62), channel_id=1, source_target_pairs={{0,6},{1,7},{2,4},{3,5},{4,2},{5,3},{6,0},{7,1},{8,14},{9,15},{10,... | collective-permute-start | bytes 737288 | tf_op jit(solution)/shard_map/ppermute | solution.py:389
  30.3 2.5 %collective-permute-start.6 = (bf16[960,128]{1,0:T(8,128)(2,1)}, bf16[960,128]{1,0:T(8,128)(2,1)S(1)}, u32[]{:S(2)}, u32[]{:S(2)}) collective-permute-start(bf16[960,128]{1,0:T(8,128)(2,1)} %get-tuple-element.63), channel_id=1, source_target_pairs={{0,12},{1,13},{2,14},{3,15},{4,8},{5,9},{6,10},{7,11},{8,4},{9,5},... | collective-permute-start | bytes 737288 | tf_op jit(solution)/shard_map/ppermute | solution.py:389
  32.8 2.5 %collective-permute-done.2.rest_3_ = bf16[960,128]{1,0:T(8,128)(2,1)S(1)} collective-permute-done((bf16[960,128]{1,0:T(8,128)(2,1)S(1)}, bf16[960,128]{1,0:T(8,128)(2,1)S(1)}, u32[]{:S(2)}, u32[]{:S(2)}) %collective-permute-start.2) | collective-permute-done | bytes 245792 | tf_op jit(solution)/shard_map/ppermute | solution.py:389
  35.2 5.2 %collective-permute-start.7 = (bf16[960,128]{1,0:T(8,128)(2,1)}, bf16[960,128]{1,0:T(8,128)(2,1)S(1)}, u32[]{:S(2)}, u32[]{:S(2)}) collective-permute-start(bf16[960,128]{1,0:T(8,128)(2,1)} %get-tuple-element.64), channel_id=1, source_target_pairs={{0,7},{1,6},{2,5},{3,4},{4,3},{5,2},{6,1},{7,0},{8,15},{9,14},{10,... | collective-permute-start | bytes 737288 | tf_op jit(solution)/shard_map/ppermute | solution.py:389
  41.5 4.1 %collective-permute-done.4.rest_5_ = bf16[960,128]{1,0:T(8,128)(2,1)S(1)} collective-permute-done((bf16[960,128]{1,0:T(8,128)(2,1)S(1)}, bf16[960,128]{1,0:T(8,128)(2,1)S(1)}, u32[]{:S(2)}, u32[]{:S(2)}) %collective-permute-start.4) | collective-permute-done | bytes 245792 | tf_op jit(solution)/shard_map/ppermute | solution.py:389
  47.6 3.4 %collective-permute-done.5.rest_6_ = bf16[960,128]{1,0:T(8,128)(2,1)S(1)} collective-permute-done((bf16[960,128]{1,0:T(8,128)(2,1)}, bf16[960,128]{1,0:T(8,128)(2,1)S(1)}, u32[]{:S(2)}, u32[]{:S(2)}) %collective-permute-start.5) | collective-permute-done | bytes 245792 | tf_op jit(solution)/shard_map/ppermute | solution.py:389
  51.0 2.6 %collective-permute-start.10 = (bf16[960,128]{1,0:T(8,128)(2,1)}, bf16[960,128]{1,0:T(8,128)(2,1)S(1)}, u32[]{:S(2)}, u32[]{:S(2)}) collective-permute-start(bf16[960,128]{1,0:T(8,128)(2,1)} %copy-done.6), channel_id=1, source_target_pairs={{0,10},{1,11},{2,8},{3,9},{4,14},{5,15},{6,12},{7,13},{8,2},{9,3},... | collective-permute-start | bytes 737288 | tf_op jit(solution)/shard_map/ppermute | solution.py:389
  53.6 2.6 %collective-permute-done.6.rest_7_ = bf16[960,128]{1,0:T(8,128)(2,1)S(1)} collective-permute-done((bf16[960,128]{1,0:T(8,128)(2,1)}, bf16[960,128]{1,0:T(8,128)(2,1)S(1)}, u32[]{:S(2)}, u32[]{:S(2)}) %collective-permute-start.6) | collective-permute-done | bytes 245792 | tf_op jit(solution)/shard_map/ppermute | solution.py:389
  56.9 4.0 %collective-permute-done.7.rest_8_ = bf16[960,128]{1,0:T(8,128)(2,1)S(1)} collective-permute-done((bf16[960,128]{1,0:T(8,128)(2,1)}, bf16[960,128]{1,0:T(8,128)(2,1)S(1)}, u32[]{:S(2)}, u32[]{:S(2)}) %collective-permute-start.7) | collective-permute-done | bytes 245792 | tf_op jit(solution)/shard_map/ppermute | solution.py:389
  61.8 19.3 %collective-permute-done.8.rest_9_ = bf16[960,128]{1,0:T(8,128)(2,1)S(1)} collective-permute-done((bf16[960,128]{1,0:T(8,128)(2,1)}, bf16[960,128]{1,0:T(8,128)(2,1)S(1)}, u32[]{:S(2)}, u32[]{:S(2)}) %collective-permute-start.8) | collective-permute-done | bytes 245792 | tf_op jit(solution)/shard_map/ppermute | solution.py:389
  82.6 9.5 %collective-permute-done.10.rest_11_ = bf16[960,128]{1,0:T(8,128)(2,1)S(1)} collective-permute-done((bf16[960,128]{1,0:T(8,128)(2,1)}, bf16[960,128]{1,0:T(8,128)(2,1)S(1)}, u32[]{:S(2)}, u32[]{:S(2)}) %collective-permute-start.10) | collective-permute-done | bytes 245792 | tf_op jit(solution)/shard_map/ppermute | solution.py:389
  92.1 5.2 %collective-permute-done.12.rest_13_ = bf16[960,128]{1,0:T(8,128)(2,1)S(1)} collective-permute-done((bf16[960,128]{1,0:T(8,128)(2,1)S(1)}, bf16[960,128]{1,0:T(8,128)(2,1)S(1)}, u32[]{:S(2)}, u32[]{:S(2)}) %collective-permute-start.12) | collective-permute-done | bytes 245792 | tf_op jit(solution)/shard_map/ppermute | solution.py:389
  97.2 5.3 %collective-permute-done.14.rest_15_ = bf16[960,128]{1,0:T(8,128)(2,1)S(1)} collective-permute-done((bf16[960,128]{1,0:T(8,128)(2,1)S(1)}, bf16[960,128]{1,0:T(8,128)(2,1)S(1)}, u32[]{:S(2)}, u32[]{:S(2)}) %collective-permute-start.14) | collective-permute-done | bytes 245792 | tf_op jit(solution)/shard_map/ppermute | solution.py:389
  102.7 3.1 %attend_first.1 = (bf16[16,832,128]{2,1,0:T(8,128)(2,1)S(1)}, bf16[4,256,128]{2,1,0:T(8,128)(2,1)S(1)}) custom-call(s32[1]{0:T(128)} %bitcast.me_ref, s32[576]{0:T(1024)S(1)} %reshape.10.lists_ref, s32[48]{0:T(128)S(1)} %reshape.11.counts_ref, bf16[960,128]{1,0:T(8,128)(2,1)S(1)} %get-tuple-element.56.rest_0_, ...), custom_call_target="tpu_custom_call" | custom-call | flops 268435456 | bytes 1048576 | tf_op jit(solution)/shard_map/attend_first/pallas_call | solution.py:250
  105.9 1.8 %attend_second.1 = (bf16[2,16,128,128]{3,2,1,0:T(8,128)(2,1)S(1)}, bf16[320,128]{1,0:T(8,128)(2,1)S(1)}, bf16[320,128]{1,0:T(8,128)(2,1)S(1)}, bf16[320,128]{1,0:T(8,128)(2,1)S(1)}, bf16[320,128]{1,0:T(8,128)(2,1)S(1)}) custom-call(s32[1]{0:T(128)} %bitcast.me_ref, s32[576]{0:T(1024)S(1)} %reshape.10.lists_ref, s32[48]{0:T(128)S(1)} %reshape.11.counts_ref, ...), custom_call_target="tpu_custom_call" | custom-call | flops 134217728 | bytes 524288 | tf_op jit(solution)/shard_map/attend_second/pallas_call | solution.py:283
  107.7 1.9 %collective-permute-start.16 = (bf16[320,128]{1,0:T(8,128)(2,1)S(1)}, bf16[320,128]{1,0:T(8,128)(2,1)S(1)}, u32[]{:S(2)}, u32[]{:S(2)}) collective-permute-start(bf16[320,128]{1,0:T(8,128)(2,1)S(1)} %get-tuple-element.74), channel_id=1, source_target_pairs={{0,15},{1,14},{2,13},{3,12},{4,11},{5,10},{6,9},{7,8},{8,7},{9,6},... | collective-permute-start | bytes 245768 | tf_op jit(solution)/shard_map/ppermute | solution.py:389
  109.6 2.5 %collective-permute-start.17 = (bf16[320,128]{1,0:T(8,128)(2,1)S(1)}, bf16[320,128]{1,0:T(8,128)(2,1)S(1)}, u32[]{:S(2)}, u32[]{:S(2)}) collective-permute-start(bf16[320,128]{1,0:T(8,128)(2,1)S(1)} %get-tuple-element.76), channel_id=1, source_target_pairs={{0,14},{1,15},{2,12},{3,13},{4,10},{5,11},{6,8},{7,9},{8,6},{9,7},... | collective-permute-start | bytes 245768 | tf_op jit(solution)/shard_map/ppermute | solution.py:389
  112.0 1.6 %collective-permute-start.18 = (bf16[320,128]{1,0:T(8,128)(2,1)S(1)}, bf16[320,128]{1,0:T(8,128)(2,1)S(1)}, u32[]{:S(2)}, u32[]{:S(2)}) collective-permute-start(bf16[320,128]{1,0:T(8,128)(2,1)S(1)} %get-tuple-element.77), channel_id=1, source_target_pairs={{0,13},{1,12},{2,15},{3,14},{4,9},{5,8},{6,11},{7,10},{8,5},{9,4},... | collective-permute-start | bytes 245768 | tf_op jit(solution)/shard_map/ppermute | solution.py:389
  113.7 2.0 %collective-permute-start.19 = (bf16[320,128]{1,0:T(8,128)(2,1)S(1)}, bf16[320,128]{1,0:T(8,128)(2,1)S(1)}, u32[]{:S(2)}, u32[]{:S(2)}) collective-permute-start(bf16[320,128]{1,0:T(8,128)(2,1)S(1)} %get-tuple-element.78), channel_id=1, source_target_pairs={{0,12},{1,13},{2,14},{3,15},{4,8},{5,9},{6,10},{7,11},{8,4},{9,5},... | collective-permute-start | bytes 245768 | tf_op jit(solution)/shard_map/ppermute | solution.py:389
  115.7 9.8 %attend_rest.1 = (bf16[320,128]{1,0:T(8,128)(2,1)S(1)}, bf16[320,128]{1,0:T(8,128)(2,1)S(1)}, bf16[320,128]{1,0:T(8,128)(2,1)S(1)}, bf16[320,128]{1,0:T(8,128)(2...) custom-call(s32[1]{0:T(128)} %bitcast.me_ref, ...), custom_call_target="tpu_custom_call" | custom-call | flops 1207959552 | bytes 4718592 | tf_op jit(solution)/shard_map/attend_rest/pallas_call | solution.py:330
  126.9 2.0 %collective-permute-start.22 = (bf16[320,128]{1,0:T(8,128)(2,1)S(1)}, bf16[320,128]{1,0:T(8,128)(2,1)S(1)}, u32[]{:S(2)}, u32[]{:S(2)}) collective-permute-start(bf16[320,128]{1,0:T(8,128)(2,1)S(1)} %get-tuple-element.83), channel_id=1, source_target_pairs={{0,10},{1,11},{2,8},{3,9},{4,14},{5,15},{6,12},{7,13},{8,2},{9,3},... | collective-permute-start | bytes 245768 | tf_op jit(solution)/shard_map/ppermute | solution.py:389
  128.9 1.7 %collective-permute-start.23 = (bf16[320,128]{1,0:T(8,128)(2,1)S(1)}, bf16[320,128]{1,0:T(8,128)(2,1)S(1)}, u32[]{:S(2)}, u32[]{:S(2)}) collective-permute-start(bf16[320,128]{1,0:T(8,128)(2,1)S(1)} %get-tuple-element.84), channel_id=1, source_target_pairs={{0,5},{1,4},{2,7},{3,6},{4,1},{5,0},{6,3},{7,2},{8,13},{9,12},{10,... | collective-permute-start | bytes 245768 | tf_op jit(solution)/shard_map/ppermute | solution.py:389
  130.6 1.6 %collective-permute-done.20.rest_4_ = bf16[320,128]{1,0:T(8,128)(2,1)S(1)} collective-permute-done((bf16[320,128]{1,0:T(8,128)(2,1)S(1)}, bf16[320,128]{1,0:T(8,128)(2,1)S(1)}, u32[]{:S(2)}, u32[]{:S(2)}) %collective-permute-start.20) | collective-permute-done | bytes 81952 | tf_op jit(solution)/shard_map/ppermute | solution.py:389
  132.5 2.7 %collective-permute-start.26 = (bf16[320,128]{1,0:T(8,128)(2,1)S(1)}, bf16[320,128]{1,0:T(8,128)(2,1)S(1)}, u32[]{:S(2)}, u32[]{:S(2)}) collective-permute-start(bf16[320,128]{1,0:T(8,128)(2,1)S(1)} %get-tuple-element.87), channel_id=1, source_target_pairs={{0,8},{1,9},{2,10},{3,11},{4,12},{5,13},{6,14},{7,15},{8,0},{9,1},... | collective-permute-start | bytes 245768 | tf_op jit(solution)/shard_map/ppermute | solution.py:389
  138.0 1.8 %collective-permute-start.29 = (bf16[320,128]{1,0:T(8,128)(2,1)S(1)}, bf16[320,128]{1,0:T(8,128)(2,1)S(1)}, u32[]{:S(2)}, u32[]{:S(2)}) collective-permute-start(bf16[320,128]{1,0:T(8,128)(2,1)S(1)} %get-tuple-element.90), channel_id=1, source_target_pairs={{0,2},{1,3},{2,0},{3,1},{4,6},{5,7},{6,4},{7,5},{8,10},{9,11},{10,... | collective-permute-start | bytes 245768 | tf_op jit(solution)/shard_map/ppermute | solution.py:389
  139.8 1.9 %collective-permute-done.26.rest_10_ = bf16[320,128]{1,0:T(8,128)(2,1)S(1)} collective-permute-done((bf16[320,128]{1,0:T(8,128)(2,1)S(1)}, bf16[320,128]{1,0:T(8,128)(2,1)S(1)}, u32[]{:S(2)}, u32[]{:S(2)}) %collective-permute-start.26) | collective-permute-done | bytes 81952 | tf_op jit(solution)/shard_map/ppermute | solution.py:389
  142.6 1.5 %collective-permute-done.29.rest_13_ = bf16[320,128]{1,0:T(8,128)(2,1)S(1)} collective-permute-done((bf16[320,128]{1,0:T(8,128)(2,1)S(1)}, bf16[320,128]{1,0:T(8,128)(2,1)S(1)}, u32[]{:S(2)}, u32[]{:S(2)}) %collective-permute-start.29) | collective-permute-done | bytes 81952 | tf_op jit(solution)/shard_map/ppermute | solution.py:389
  144.1 1.7 %collective-permute-done.30.rest_14_ = bf16[320,128]{1,0:T(8,128)(2,1)S(1)} collective-permute-done((bf16[320,128]{1,0:T(8,128)(2,1)S(1)}, bf16[320,128]{1,0:T(8,128)(2,1)S(1)}, u32[]{:S(2)}, u32[]{:S(2)}) %collective-permute-start.30) | collective-permute-done | bytes 81952 | tf_op jit(solution)/shard_map/ppermute | solution.py:389
  (64 shorter events, 22.8 us)
Async XLA Ops:
  5.4 40.4 %copy-start.8 = (s32[40,16,12]{0,1,2:T(8,128)S(1)}, s32[40,16,12]{0,1,2:T(8,128)}, u32[]{:S(2)}) copy-start(s32[40,16,12]{0,1,2:T(8,128)} %param.12) | copy-start | bytes 92164
  11.8 11.8 %collective-permute-start = (bf16[960,128]{1,0:T(8,128)(2,1)S(1)}, bf16[960,128]{1,0:T(8,128)(2,1)S(1)}, u32[]{:S(2)}, u32[]{:S(2)}) collective-permute-start(bf16[960,128]{1,0:T(8,128)(2,1)S(1)} %get-tuple-element.51), channel_id=1, source_target_pairs={{0,15},{1,14},{2,13},{3,12},{4,11},{5,10},{6,9},{7,8},{8,7},{9,6},... | collective-permute-start | bytes 737288 | tf_op jit(solution)/shard_map/ppermute | solution.py:389
  17.2 13.0 %collective-permute-start.1 = (bf16[960,128]{1,0:T(8,128)(2,1)S(1)}, bf16[960,128]{1,0:T(8,128)(2,1)S(1)}, u32[]{:S(2)}, u32[]{:S(2)}) collective-permute-start(bf16[960,128]{1,0:T(8,128)(2,1)S(1)} %get-tuple-element.58), channel_id=1, source_target_pairs={{0,4},{1,5},{2,6},{3,7},{4,0},{5,1},{6,2},{7,3},{8,12},{9,13},{10,... | collective-permute-start | bytes 737288 | tf_op jit(solution)/shard_map/ppermute | solution.py:389
  17.2 18.0 %collective-permute-start.2 = (bf16[960,128]{1,0:T(8,128)(2,1)S(1)}, bf16[960,128]{1,0:T(8,128)(2,1)S(1)}, u32[]{:S(2)}, u32[]{:S(2)}) collective-permute-start(bf16[960,128]{1,0:T(8,128)(2,1)S(1)} %get-tuple-element.59), channel_id=1, source_target_pairs={{0,14},{1,15},{2,12},{3,13},{4,10},{5,11},{6,8},{7,9},{8,6},{9,7},... | collective-permute-start | bytes 737288 | tf_op jit(solution)/shard_map/ppermute | solution.py:389
  18.2 22.2 %collective-permute-start.3 = (bf16[960,128]{1,0:T(8,128)(2,1)S(1)}, bf16[960,128]{1,0:T(8,128)(2,1)S(1)}, u32[]{:S(2)}, u32[]{:S(2)}) collective-permute-start(bf16[960,128]{1,0:T(8,128)(2,1)S(1)} %get-tuple-element.60), channel_id=1, source_target_pairs={{0,5},{1,4},{2,7},{3,6},{4,1},{5,0},{6,3},{7,2},{8,13},{9,12},{10,... | collective-permute-start | bytes 737288 | tf_op jit(solution)/shard_map/ppermute | solution.py:389
  19.3 26.2 %collective-permute-start.4 = (bf16[960,128]{1,0:T(8,128)(2,1)S(1)}, bf16[960,128]{1,0:T(8,128)(2,1)S(1)}, u32[]{:S(2)}, u32[]{:S(2)}) collective-permute-start(bf16[960,128]{1,0:T(8,128)(2,1)S(1)} %get-tuple-element.61), channel_id=1, source_target_pairs={{0,13},{1,12},{2,15},{3,14},{4,9},{5,8},{6,11},{7,10},{8,5},{9,4},... | collective-permute-start | bytes 737288 | tf_op jit(solution)/shard_map/ppermute | solution.py:389
  23.6 27.4 %collective-permute-start.5 = (bf16[960,128]{1,0:T(8,128)(2,1)}, bf16[960,128]{1,0:T(8,128)(2,1)S(1)}, u32[]{:S(2)}, u32[]{:S(2)}) collective-permute-start(bf16[960,128]{1,0:T(8,128)(2,1)} %get-tuple-element.62), channel_id=1, source_target_pairs={{0,6},{1,7},{2,4},{3,5},{4,2},{5,3},{6,0},{7,1},{8,14},{9,15},{10,... | collective-permute-start | bytes 737288 | tf_op jit(solution)/shard_map/ppermute | solution.py:389
  30.3 25.9 %collective-permute-start.6 = (bf16[960,128]{1,0:T(8,128)(2,1)}, bf16[960,128]{1,0:T(8,128)(2,1)S(1)}, u32[]{:S(2)}, u32[]{:S(2)}) collective-permute-start(bf16[960,128]{1,0:T(8,128)(2,1)} %get-tuple-element.63), channel_id=1, source_target_pairs={{0,12},{1,13},{2,14},{3,15},{4,8},{5,9},{6,10},{7,11},{8,4},{9,5},... | collective-permute-start | bytes 737288 | tf_op jit(solution)/shard_map/ppermute | solution.py:389
  35.2 25.7 %collective-permute-start.7 = (bf16[960,128]{1,0:T(8,128)(2,1)}, bf16[960,128]{1,0:T(8,128)(2,1)S(1)}, u32[]{:S(2)}, u32[]{:S(2)}) collective-permute-start(bf16[960,128]{1,0:T(8,128)(2,1)} %get-tuple-element.64), channel_id=1, source_target_pairs={{0,7},{1,6},{2,5},{3,4},{4,3},{5,2},{6,1},{7,0},{8,15},{9,14},{10,... | collective-permute-start | bytes 737288 | tf_op jit(solution)/shard_map/ppermute | solution.py:389
  40.4 40.7 %collective-permute-start.8 = (bf16[960,128]{1,0:T(8,128)(2,1)}, bf16[960,128]{1,0:T(8,128)(2,1)S(1)}, u32[]{:S(2)}, u32[]{:S(2)}) collective-permute-start(bf16[960,128]{1,0:T(8,128)(2,1)} %get-tuple-element.65), channel_id=1, source_target_pairs={{0,11},{1,10},{2,9},{3,8},{4,15},{5,14},{6,13},{7,12},{8,3},{9,2},... | collective-permute-start | bytes 737288 | tf_op jit(solution)/shard_map/ppermute | solution.py:389
  45.5 37.1 %collective-permute-start.9 = (bf16[960,128]{1,0:T(8,128)(2,1)}, bf16[960,128]{1,0:T(8,128)(2,1)S(1)}, u32[]{:S(2)}, u32[]{:S(2)}) collective-permute-start(bf16[960,128]{1,0:T(8,128)(2,1)} %copy-done.7), channel_id=1, source_target_pairs={{0,1},{1,0},{2,3},{3,2},{4,5},{5,4},{6,7},{7,6},{8,9},{9,8},{10,11... | collective-permute-start | bytes 737288 | tf_op jit(solution)/shard_map/ppermute | solution.py:389
  51.0 41.0 %collective-permute-start.10 = (bf16[960,128]{1,0:T(8,128)(2,1)}, bf16[960,128]{1,0:T(8,128)(2,1)S(1)}, u32[]{:S(2)}, u32[]{:S(2)}) collective-permute-start(bf16[960,128]{1,0:T(8,128)(2,1)} %copy-done.6), channel_id=1, source_target_pairs={{0,10},{1,11},{2,8},{3,9},{4,14},{5,15},{6,12},{7,13},{8,2},{9,3},... | collective-permute-start | bytes 737288 | tf_op jit(solution)/shard_map/ppermute | solution.py:389
  56.1 35.9 %collective-permute-start.11 = (bf16[960,128]{1,0:T(8,128)(2,1)}, bf16[960,128]{1,0:T(8,128)(2,1)S(1)}, u32[]{:S(2)}, u32[]{:S(2)}) collective-permute-start(bf16[960,128]{1,0:T(8,128)(2,1)} %copy-done.5), channel_id=1, source_target_pairs={{0,2},{1,3},{2,0},{3,1},{4,6},{5,7},{6,4},{7,5},{8,10},{9,11},{10,... | collective-permute-start | bytes 737288 | tf_op jit(solution)/shard_map/ppermute | solution.py:389
  61.0 36.2 %collective-permute-start.12 = (bf16[960,128]{1,0:T(8,128)(2,1)S(1)}, bf16[960,128]{1,0:T(8,128)(2,1)S(1)}, u32[]{:S(2)}, u32[]{:S(2)}) collective-permute-start(bf16[960,128]{1,0:T(8,128)(2,1)S(1)} %get-tuple-element.69), channel_id=1, source_target_pairs={{0,9},{1,8},{2,11},{3,10},{4,13},{5,12},{6,15},{7,14},{8,1},{9,0},... | collective-permute-start | bytes 737288 | tf_op jit(solution)/shard_map/ppermute | solution.py:389
  81.2 16.1 %collective-permute-start.13 = (bf16[960,128]{1,0:T(8,128)(2,1)S(1)}, bf16[960,128]{1,0:T(8,128)(2,1)S(1)}, u32[]{:S(2)}, u32[]{:S(2)}) collective-permute-start(bf16[960,128]{1,0:T(8,128)(2,1)S(1)} %get-tuple-element.70), channel_id=1, source_target_pairs={{0,3},{1,2},{2,1},{3,0},{4,7},{5,6},{6,5},{7,4},{8,11},{9,10},{10,... | collective-permute-start | bytes 737288 | tf_op jit(solution)/shard_map/ppermute | solution.py:389
  82.6 19.9 %collective-permute-start.14 = (bf16[960,128]{1,0:T(8,128)(2,1)S(1)}, bf16[960,128]{1,0:T(8,128)(2,1)S(1)}, u32[]{:S(2)}, u32[]{:S(2)}) collective-permute-start(bf16[960,128]{1,0:T(8,128)(2,1)S(1)} %get-tuple-element.71), channel_id=1, source_target_pairs={{0,8},{1,9},{2,10},{3,11},{4,12},{5,13},{6,14},{7,15},{8,0},{9,1},... | collective-permute-start | bytes 737288 | tf_op jit(solution)/shard_map/ppermute | solution.py:389
  102.5 3.3 %collective-permute-start.15 = (bf16[16,128,128]{2,1,0:T(8,128)(2,1)S(1)}, bf16[16,128,128]{2,1,0:T(8,128)(2,1)S(1)}, u32[]{:S(2)}, u32[]{:S(2)}) collective-permute-start(bf16[16,128,128]{2,1,0:T(8,128)(2,1)S(1)} %collect_shared.1.own_ref), channel_id=1, source_target_pairs={{0,1},{1,0},{2,3},{3,2},{4,5},{5,4},{6,7},{7,6},{8,9},{9,8},{10,11... | collective-permute-start | bytes 1572872 | tf_op jit(solution)/shard_map/ppermute | solution.py:389
  107.7 8.1 %collective-permute-start.16 = (bf16[320,128]{1,0:T(8,128)(2,1)S(1)}, bf16[320,128]{1,0:T(8,128)(2,1)S(1)}, u32[]{:S(2)}, u32[]{:S(2)}) collective-permute-start(bf16[320,128]{1,0:T(8,128)(2,1)S(1)} %get-tuple-element.74), channel_id=1, source_target_pairs={{0,15},{1,14},{2,13},{3,12},{4,11},{5,10},{6,9},{7,8},{8,7},{9,6},... | collective-permute-start | bytes 245768 | tf_op jit(solution)/shard_map/ppermute | solution.py:389
  109.6 17.3 %collective-permute-start.17 = (bf16[320,128]{1,0:T(8,128)(2,1)S(1)}, bf16[320,128]{1,0:T(8,128)(2,1)S(1)}, u32[]{:S(2)}, u32[]{:S(2)}) collective-permute-start(bf16[320,128]{1,0:T(8,128)(2,1)S(1)} %get-tuple-element.76), channel_id=1, source_target_pairs={{0,14},{1,15},{2,12},{3,13},{4,10},{5,11},{6,8},{7,9},{8,6},{9,7},... | collective-permute-start | bytes 245768 | tf_op jit(solution)/shard_map/ppermute | solution.py:389
  112.0 16.9 %collective-permute-start.18 = (bf16[320,128]{1,0:T(8,128)(2,1)S(1)}, bf16[320,128]{1,0:T(8,128)(2,1)S(1)}, u32[]{:S(2)}, u32[]{:S(2)}) collective-permute-start(bf16[320,128]{1,0:T(8,128)(2,1)S(1)} %get-tuple-element.77), channel_id=1, source_target_pairs={{0,13},{1,12},{2,15},{3,14},{4,9},{5,8},{6,11},{7,10},{8,5},{9,4},... | collective-permute-start | bytes 245768 | tf_op jit(solution)/shard_map/ppermute | solution.py:389
  113.7 16.9 %collective-permute-start.19 = (bf16[320,128]{1,0:T(8,128)(2,1)S(1)}, bf16[320,128]{1,0:T(8,128)(2,1)S(1)}, u32[]{:S(2)}, u32[]{:S(2)}) collective-permute-start(bf16[320,128]{1,0:T(8,128)(2,1)S(1)} %get-tuple-element.78), channel_id=1, source_target_pairs={{0,12},{1,13},{2,14},{3,15},{4,8},{5,9},{6,10},{7,11},{8,4},{9,5},... | collective-permute-start | bytes 245768 | tf_op jit(solution)/shard_map/ppermute | solution.py:389
  125.5 6.7 %collective-permute-start.20 = (bf16[320,128]{1,0:T(8,128)(2,1)S(1)}, bf16[320,128]{1,0:T(8,128)(2,1)S(1)}, u32[]{:S(2)}, u32[]{:S(2)}) collective-permute-start(bf16[320,128]{1,0:T(8,128)(2,1)S(1)} %get-tuple-element.81), channel_id=1, source_target_pairs={{0,11},{1,10},{2,9},{3,8},{4,15},{5,14},{6,13},{7,12},{8,3},{9,2},... | collective-permute-start | bytes 245768 | tf_op jit(solution)/shard_map/ppermute | solution.py:389
  125.6 6.8 %collective-permute-start.21 = (bf16[320,128]{1,0:T(8,128)(2,1)S(1)}, bf16[320,128]{1,0:T(8,128)(2,1)S(1)}, u32[]{:S(2)}, u32[]{:S(2)}) collective-permute-start(bf16[320,128]{1,0:T(8,128)(2,1)S(1)} %get-tuple-element.82), channel_id=1, source_target_pairs={{0,4},{1,5},{2,6},{3,7},{4,0},{5,1},{6,2},{7,3},{8,12},{9,13},{10,... | collective-permute-start | bytes 245768 | tf_op jit(solution)/shard_map/ppermute | solution.py:389
  126.9 8.9 %collective-permute-start.22 = (bf16[320,128]{1,0:T(8,128)(2,1)S(1)}, bf16[320,128]{1,0:T(8,128)(2,1)S(1)}, u32[]{:S(2)}, u32[]{:S(2)}) collective-permute-start(bf16[320,128]{1,0:T(8,128)(2,1)S(1)} %get-tuple-element.83), channel_id=1, source_target_pairs={{0,10},{1,11},{2,8},{3,9},{4,14},{5,15},{6,12},{7,13},{8,2},{9,3},... | collective-permute-start | bytes 245768 | tf_op jit(solution)/shard_map/ppermute | solution.py:389
  128.9 7.4 %collective-permute-start.23 = (bf16[320,128]{1,0:T(8,128)(2,1)S(1)}, bf16[320,128]{1,0:T(8,128)(2,1)S(1)}, u32[]{:S(2)}, u32[]{:S(2)}) collective-permute-start(bf16[320,128]{1,0:T(8,128)(2,1)S(1)} %get-tuple-element.84), channel_id=1, source_target_pairs={{0,5},{1,4},{2,7},{3,6},{4,1},{5,0},{6,3},{7,2},{8,13},{9,12},{10,... | collective-permute-start | bytes 245768 | tf_op jit(solution)/shard_map/ppermute | solution.py:389
  130.6 7.3 %collective-permute-start.24 = (bf16[320,128]{1,0:T(8,128)(2,1)S(1)}, bf16[320,128]{1,0:T(8,128)(2,1)S(1)}, u32[]{:S(2)}, u32[]{:S(2)}) collective-permute-start(bf16[320,128]{1,0:T(8,128)(2,1)S(1)} %get-tuple-element.85), channel_id=1, source_target_pairs={{0,9},{1,8},{2,11},{3,10},{4,13},{5,12},{6,15},{7,14},{8,1},{9,0},... | collective-permute-start | bytes 245768 | tf_op jit(solution)/shard_map/ppermute | solution.py:389
  132.2 7.6 %collective-permute-start.25 = (bf16[320,128]{1,0:T(8,128)(2,1)S(1)}, bf16[320,128]{1,0:T(8,128)(2,1)S(1)}, u32[]{:S(2)}, u32[]{:S(2)}) collective-permute-start(bf16[320,128]{1,0:T(8,128)(2,1)S(1)} %get-tuple-element.86), channel_id=1, source_target_pairs={{0,6},{1,7},{2,4},{3,5},{4,2},{5,3},{6,0},{7,1},{8,14},{9,15},{10,... | collective-permute-start | bytes 245768 | tf_op jit(solution)/shard_map/ppermute | solution.py:389
  132.5 9.2 %collective-permute-start.26 = (bf16[320,128]{1,0:T(8,128)(2,1)S(1)}, bf16[320,128]{1,0:T(8,128)(2,1)S(1)}, u32[]{:S(2)}, u32[]{:S(2)}) collective-permute-start(bf16[320,128]{1,0:T(8,128)(2,1)S(1)} %get-tuple-element.87), channel_id=1, source_target_pairs={{0,8},{1,9},{2,10},{3,11},{4,12},{5,13},{6,14},{7,15},{8,0},{9,1},... | collective-permute-start | bytes 245768 | tf_op jit(solution)/shard_map/ppermute | solution.py:389
  135.8 6.8 %collective-permute-start.27 = (bf16[320,128]{1,0:T(8,128)(2,1)S(1)}, bf16[320,128]{1,0:T(8,128)(2,1)S(1)}, u32[]{:S(2)}, u32[]{:S(2)}) collective-permute-start(bf16[320,128]{1,0:T(8,128)(2,1)S(1)} %get-tuple-element.88), channel_id=1, source_target_pairs={{0,7},{1,6},{2,5},{3,4},{4,3},{5,2},{6,1},{7,0},{8,15},{9,14},{10,... | collective-permute-start | bytes 245768 | tf_op jit(solution)/shard_map/ppermute | solution.py:389
  136.4 6.2 %collective-permute-start.28 = (bf16[320,128]{1,0:T(8,128)(2,1)S(1)}, bf16[320,128]{1,0:T(8,128)(2,1)S(1)}, u32[]{:S(2)}, u32[]{:S(2)}) collective-permute-start(bf16[320,128]{1,0:T(8,128)(2,1)S(1)} %get-tuple-element.89), channel_id=1, source_target_pairs={{0,1},{1,0},{2,3},{3,2},{4,5},{5,4},{6,7},{7,6},{8,9},{9,8},{10,11... | collective-permute-start | bytes 245768 | tf_op jit(solution)/shard_map/ppermute | solution.py:389
  138.0 6.2 %collective-permute-start.29 = (bf16[320,128]{1,0:T(8,128)(2,1)S(1)}, bf16[320,128]{1,0:T(8,128)(2,1)S(1)}, u32[]{:S(2)}, u32[]{:S(2)}) collective-permute-start(bf16[320,128]{1,0:T(8,128)(2,1)S(1)} %get-tuple-element.90), channel_id=1, source_target_pairs={{0,2},{1,3},{2,0},{3,1},{4,6},{5,7},{6,4},{7,5},{8,10},{9,11},{10,... | collective-permute-start | bytes 245768 | tf_op jit(solution)/shard_map/ppermute | solution.py:389
  139.8 6.0 %collective-permute-start.30 = (bf16[320,128]{1,0:T(8,128)(2,1)S(1)}, bf16[320,128]{1,0:T(8,128)(2,1)S(1)}, u32[]{:S(2)}, u32[]{:S(2)}) collective-permute-start(bf16[320,128]{1,0:T(8,128)(2,1)S(1)} %get-tuple-element.91), channel_id=1, source_target_pairs={{0,3},{1,2},{2,1},{3,0},{4,7},{5,6},{6,5},{7,4},{8,11},{9,10},{10,... | collective-permute-start | bytes 245768 | tf_op jit(solution)/shard_map/ppermute | solution.py:389
  (9 other events, 32.3 us)

commit v4 on v3

--- a/solution.py
+++ b/solution.py
@@ -18,8 +18,9 @@
 MASKED = -1e30
 EXP2_SCALE = HEAD_DIM ** (-0.5) * math.log2(math.e)
 SIZES = (2, 4, 6, 8, 10, 12)
-TOGETHER = 4
+TOGETHER = 8
 VMEM_LIMIT = 12 * 1024 * 1024
+PACK_VMEM_LIMIT = 58 * 1024 * 1024
 
 HEAD_ROWS = 3 * TILE
 SHARED_Q = 2 * HEAD_ROWS
@@ -58,10 +59,14 @@
     return order
 
 
+def even_first(masks):
+    return sorted(masks, key=lambda mask: (mask % 2, mask))
+
+
 def partners(devices):
-    half = devices // 2
-    far = list(range(devices - 1, half - 1, -1))
-    near = list(range(half // 2, half)) + list(range(1, half // 2))
+    half, quarter = devices // 2, devices // 4
+    far = even_first(range(half, devices))
+    near = alternate(even_first(range(quarter, half)), even_first(range(1, quarter)))
     return far, near
 
 
@@ -137,7 +142,7 @@
         + [gain] * 2
         + [pltpu.VMEM(query.shape, jnp.bfloat16)] * 2
         + [pltpu.SemaphoreType.DMA((5,))],
-        compiler_params=PARAMS,
+        compiler_params=pltpu.CompilerParams(vmem_limit_bytes=PACK_VMEM_LIMIT),
         name="norm_pack",
     )(me, query, key, value, query_gain[None, :], key_gain[None, :])
 
@@ -235,14 +240,17 @@
     for mask, ref in zip(masks, in_refs):
         held[lax.bitwise_xor(me, mask)] = ref[0:SHARED_KV]
 
-    def step(head, carry):
+    def step(index, carry):
+        start, head = index // 2 * TOGETHER, index % 2
+
         def store(unit, values):
-            results[unit, pl.ds(pl.multiple_of(head * TILE, TILE), TILE)] = values
-
-        attend_own(me, first, head, lists_ref, counts_ref, held, store)
+            results[start + unit, pl.ds(pl.multiple_of(head * TILE, TILE), TILE)] = values
+
+        some = [min(first) + start + unit for unit in range(TOGETHER)]
+        attend_own(me, some, head, lists_ref, counts_ref, held, store)
         return carry
 
-    lax.fori_loop(0, 2, step, 0)
+    lax.fori_loop(0, 2 * len(first) // TOGETHER, step, 0)
 
 
 def attend_first(me, tables, arrived, masks, first):
@@ -262,19 +270,28 @@
 
 
 def attend_second_kernel(
-    first, me_ref, lists_ref, counts_ref, held, own_ref, other_ref, begun, shared, *out_refs
+    first, me_ref, lists_ref, counts_ref, held, own_ref, other_ref, begun, shared, *rest
 ):
+    out_refs, results = rest[: len(first)], rest[len(first)]
     me = me_ref[0]
     core = me % 2
     shared[core] = own_ref[...]
     shared[1 - core] = other_ref[...]
-    for unit, out in enumerate(out_refs):
-        out[0 : 2 * TILE] = begun[unit]
-
-    def store(unit, values):
-        out_refs[unit][2 * TILE : BACK_ROWS] = values
-
-    attend_shared(me, first, lists_ref, counts_ref, held, shared, store)
+
+    def step(group, carry):
+        start = group * TOGETHER
+
+        def store(unit, values):
+            results[start + unit] = values
+
+        some = [min(first) + start + unit for unit in range(TOGETHER)]
+        attend_shared(me, some, lists_ref, counts_ref, held, shared, store)
+        return carry
+
+    lax.fori_loop(0, len(first) // TOGETHER, step, 0)
+    for mask, out in zip(first, out_refs):
+        out[0 : 2 * TILE] = begun[mask - min(first)]
+        out[2 * TILE : BACK_ROWS] = results[mask - min(first)]
 
 
 def attend_second(me, tables, held, own, other, begun, first):
@@ -286,57 +303,12 @@
         + [back] * len(first),
         in_specs=[SMEM] * 3 + [VMEM] * 4,
         out_specs=[VMEM] * (1 + len(first)),
+        scratch_shapes=[pltpu.VMEM((len(first), HALF, HEAD_DIM), jnp.bfloat16)],
         compiler_params=PARAMS,
         cost_estimate=attend_cost(len(first)),
         name="attend_second",
     )(me, *tables, held, own, other, begun)
     return outs[0], list(outs[1:])
-
-
-def attend_rest_kernel(masks, me_ref, lists_ref, counts_ref, held, shared, *rest):
-    out_refs, results = rest[: len(masks)], rest[len(masks)]
-    me = me_ref[0]
-    groups = len(masks) // TOGETHER
-
-    def own_step(index, carry):
-        group, head = index // 2, index % 2
-        start = group * TOGETHER
-
-        def store(unit, values):
-            results[start + unit, pl.ds(pl.multiple_of(head * TILE, TILE), TILE)] = values
-
-        some = [start + unit for unit in range(TOGETHER)]
-        attend_own(me, some, head, lists_ref, counts_ref, held, store)
-        return carry
-
-    def shared_step(group, carry):
-        start = group * TOGETHER
-
-        def store(unit, values):
-            results[start + unit, 2 * TILE : BACK_ROWS] = values
-
-        some = [start + unit for unit in range(TOGETHER)]
-        attend_shared(me, some, lists_ref, counts_ref, held, shared, store)
-        return carry
-
-    lax.fori_loop(0, 2 * groups, own_step, 0)
-    lax.fori_loop(0, groups, shared_step, 0)
-    for mask, out in zip(masks, out_refs):
-        out[...] = results[mask]
-
-
-def attend_rest(me, tables, held, shared, masks):
-    back = jax.ShapeDtypeStruct((BACK_ROWS, HEAD_DIM), jnp.bfloat16)
-    return pl.pallas_call(
-        functools.partial(attend_rest_kernel, masks),
-        out_shape=[back] * len(masks),
-        in_specs=[SMEM] * 3 + [VMEM] * 2,
-        out_specs=[VMEM] * len(masks),
-        scratch_shapes=[pltpu.VMEM((len(masks), BACK_ROWS, HEAD_DIM), jnp.bfloat16)],
-        compiler_params=PARAMS,
-        cost_estimate=attend_cost(3 * len(masks)),
-        name="attend_rest",
-    )(me, *tables, held, shared)
 
 
 def attend_cost(units):
@@ -398,8 +370,6 @@
     me = index.astype(jnp.int32).reshape(1)
     far, near = partners(devices)
     masks = [0] + alternate(far, near)
-    first, later = far[:TOGETHER], far[TOGETHER:]
-    rest = alternate(later, near) + [0]
 
     leaving = pack(me, query, key, value, query_gain, key_gain, masks, heads_pair)
     early = exchange(leaving[:2], masks[:2], devices)
@@ -415,13 +385,10 @@
     arrived = early + exchange(leaving[2:middle] + late, masks[2:], devices)
     own = collect(me, arrived, masks)
     (other,) = exchange([own], [1], devices)
-    held, begun = attend_first(me, tables, arrived, masks, first)
-    shared, results = attend_second(me, tables, held, own, other, begun, first)
-    back = exchange(results, first, devices)
-    back[0], held = lax.optimization_barrier((back[0], held))
-    results = attend_rest(me, tables, held, shared, rest)
-    back += exchange(results, rest, devices)
-    return assemble(me, back, query.shape[1], first + rest, heads_pair)
+    held, begun = attend_first(me, tables, arrived, masks, masks)
+    _, results = attend_second(me, tables, held, own, other, begun, masks)
+    back = exchange(results, masks, devices)
+    return assemble(me, back, query.shape[1], masks, heads_pair)
 
 
 def pick_group():

time: 148 us -> 143 us (0.966)
  starting transfers between devices: 50.4 us -> 72.3 us
  waiting for transfers between devices: 66.6 us -> 45 us
  local copies, waits for them, and re-layouts: 9.51 us -> 1.54 us
  Pallas kernels: 20.5 us -> 23.3 us
    ppermute x31, starting transfers between devices: 50.4 us -> 72.3 us  [exchange(): lax.ppermute(part, 'ulysses', [(index, index ^ mask) for index in range(d...]
    ppermute x31, waiting for transfers between devices: 66.6 us -> 45 us  [exchange(): lax.ppermute(part, 'ulysses', [(index, index ^ mask) for index in range(d...]
    pallas_call x1 -> x0, Pallas kernels: 9.83 us -> none  [attend_rest(): pl.pallas_call(functools.partial(attend_rest_kernel, masks), out_shape=[b...]
    pallas_call x1, Pallas kernels: 3.13 us -> 10.6 us  [attend_first(): pl.pallas_call(functools.partial(attend_first_kernel, masks, first), out_...]
    unnamed x20 -> x6, local copies, waits for them, and re-layouts: 7.5 us -> 0.95 us
    pallas_call x1, Pallas kernels: 1.79 us -> 4.77 us  [attend_second(): pl.pallas_call(functools.partial(attend_second_kernel, first), out_shape=...]
    pallas_call x1, Pallas kernels: 4.27 us -> 6.43 us  [pack(): pl.pallas_call(functools.partial(pack_kernel, masks, heads_pair), out_sha...]
  transfers between devices with their start and end apart: 31 -> 31, of which waited for: 17 -> 8; matrix products, arithmetic and copies ran while one was open for 1% -> 0% of each run, Pallas kernels for 9% -> 7%
where the time goes in v4:
time: 143 us
  starting transfers between devices  72.3 us (51%)
  waiting for transfers between devices  45 us (31%)
  Pallas kernels  23.3 us (16%)
  local copies, waits for them, and re-layouts  1.54 us (1%)
    ppermute x31, starting transfers between devices, exchange(): lax.ppermute(part, 'ulysses', [(index, index ^ mask) for index in range(d...  72.3 us
    ppermute x31, waiting for transfers between devices, exchange(): lax.ppermute(part, 'ulysses', [(index, index ^ mask) for index in range(d...  45 us
    pallas_call x1, Pallas kernels, attend_first(): pl.pallas_call(functools.partial(attend_first_kernel, masks, first), out_...  10.6 us
    pallas_call x1, Pallas kernels, pack(): pl.pallas_call(functools.partial(pack_kernel, masks, heads_pair), out_sha...  6.43 us
    pallas_call x1, Pallas kernels, attend_second(): pl.pallas_call(functools.partial(attend_second_kernel, first), out_shape=...  4.77 us
  transfers between devices with their start and end apart: 31, of which 8 were waited for; matrix products, arithmetic and copies ran while one was open for 0% of the time, Pallas kernels for 7%

profile of v4, /device:TPU:0, one launch (start us, length us, event | category | flops | bytes accessed | tf_op | source)
XLA Modules:
  0.0 142.5 jit_solution(9764043659320105943)
XLA Ops:
  0.0 6.4 %norm_pack.1 = (bf16[960,128]{1,0:T(8,128)(2,1)}, bf16[960,128]{1,0:T(8,128)(2,1)}, bf16[960,128]{1,0:T(8,128)(2,1)}, bf16[960,128]{1,0:T(8,128)(2,1)}, bf16[960...) custom-call(s32[1]{0:T(128)} %bitcast.me_ref, ...), custom_call_target="tpu_custom_call" | custom-call | tf_op jit(solution)/shard_map/norm_pack/pallas_call | solution.py:136
  6.4 4.1 %collective-permute-start = (bf16[960,128]{1,0:T(8,128)(2,1)}, bf16[960,128]{1,0:T(8,128)(2,1)S(1)}, u32[]{:S(2)}, u32[]{:S(2)}) collective-permute-start(bf16[960,128]{1,0:T(8,128)(2,1)} %get-tuple-element.48), channel_id=1, source_target_pairs={{0,8},{1,9},{2,10},{3,11},{4,12},{5,13},{6,14},{7,15},{8,0},{9,1},... | collective-permute-start | bytes 737288 | tf_op jit(solution)/shard_map/ppermute | solution.py:361
  10.5 1.6 %collective-permute-start.1 = (bf16[960,128]{1,0:T(8,128)(2,1)}, bf16[960,128]{1,0:T(8,128)(2,1)S(1)}, u32[]{:S(2)}, u32[]{:S(2)}) collective-permute-start(bf16[960,128]{1,0:T(8,128)(2,1)} %get-tuple-element.55), channel_id=1, source_target_pairs={{0,4},{1,5},{2,6},{3,7},{4,0},{5,1},{6,2},{7,3},{8,12},{9,13},{10,... | collective-permute-start | bytes 737288 | tf_op jit(solution)/shard_map/ppermute | solution.py:361
  12.1 1.3 collective-permute-start.2
  13.9 2.5 %collective-permute-start.4 = (bf16[960,128]{1,0:T(8,128)(2,1)}, bf16[960,128]{1,0:T(8,128)(2,1)S(1)}, u32[]{:S(2)}, u32[]{:S(2)}) collective-permute-start(bf16[960,128]{1,0:T(8,128)(2,1)} %get-tuple-element.58), channel_id=1, source_target_pairs={{0,12},{1,13},{2,14},{3,15},{4,8},{5,9},{6,10},{7,11},{8,4},{9,5},... | collective-permute-start | bytes 737288 | tf_op jit(solution)/shard_map/ppermute | solution.py:361
  16.4 7.3 %collective-permute-done.rest_1_ = bf16[960,128]{1,0:T(8,128)(2,1)S(1)} collective-permute-done((bf16[960,128]{1,0:T(8,128)(2,1)}, bf16[960,128]{1,0:T(8,128)(2,1)S(1)}, u32[]{:S(2)}, u32[]{:S(2)}) %collective-permute-start) | collective-permute-done | bytes 245792 | tf_op jit(solution)/shard_map/ppermute | solution.py:361
  23.7 1.0 collective-permute-start.5
  24.8 3.0 %collective-permute-start.6 = (bf16[960,128]{1,0:T(8,128)(2,1)}, bf16[960,128]{1,0:T(8,128)(2,1)S(1)}, u32[]{:S(2)}, u32[]{:S(2)}) collective-permute-start(bf16[960,128]{1,0:T(8,128)(2,1)} %get-tuple-element.60), channel_id=1, source_target_pairs={{0,14},{1,15},{2,12},{3,13},{4,10},{5,11},{6,8},{7,9},{8,6},{9,7},... | collective-permute-start | bytes 737288 | tf_op jit(solution)/shard_map/ppermute | solution.py:361
  27.8 13.3 %collective-permute-done.2.rest_3_ = bf16[960,128]{1,0:T(8,128)(2,1)S(1)} collective-permute-done((bf16[960,128]{1,0:T(8,128)(2,1)}, bf16[960,128]{1,0:T(8,128)(2,1)S(1)}, u32[]{:S(2)}, u32[]{:S(2)}) %collective-permute-start.2) | collective-permute-done | bytes 245792 | tf_op jit(solution)/shard_map/ppermute | solution.py:361
  41.1 12.9 %collective-permute-start.9 = (bf16[960,128]{1,0:T(8,128)(2,1)}, bf16[960,128]{1,0:T(8,128)(2,1)S(1)}, u32[]{:S(2)}, u32[]{:S(2)}) collective-permute-start(bf16[960,128]{1,0:T(8,128)(2,1)} %get-tuple-element.63), channel_id=1, source_target_pairs={{0,5},{1,4},{2,7},{3,6},{4,1},{5,0},{6,3},{7,2},{8,13},{9,12},{10,... | collective-permute-start | bytes 737288 | tf_op jit(solution)/shard_map/ppermute | solution.py:361
  54.7 2.8 %collective-permute-start.10 = (bf16[960,128]{1,0:T(8,128)(2,1)}, bf16[960,128]{1,0:T(8,128)(2,1)S(1)}, u32[]{:S(2)}, u32[]{:S(2)}) collective-permute-start(bf16[960,128]{1,0:T(8,128)(2,1)} %get-tuple-element.64), channel_id=1, source_target_pairs={{0,11},{1,10},{2,9},{3,8},{4,15},{5,14},{6,13},{7,12},{8,3},{9,2},... | collective-permute-start | bytes 737288 | tf_op jit(solution)/shard_map/ppermute | solution.py:361
  58.2 1.1 collective-permute-start.12
  59.4 4.0 %collective-permute-done.8.rest_9_ = bf16[960,128]{1,0:T(8,128)(2,1)S(1)} collective-permute-done((bf16[960,128]{1,0:T(8,128)(2,1)}, bf16[960,128]{1,0:T(8,128)(2,1)S(1)}, u32[]{:S(2)}, u32[]{:S(2)}) %collective-permute-start.8) | collective-permute-done | bytes 245792 | tf_op jit(solution)/shard_map/ppermute | solution.py:361
  63.4 12.7 %collective-permute-start.13 = (bf16[960,128]{1,0:T(8,128)(2,1)}, bf16[960,128]{1,0:T(8,128)(2,1)S(1)}, u32[]{:S(2)}, u32[]{:S(2)}) collective-permute-start(bf16[960,128]{1,0:T(8,128)(2,1)} %get-tuple-element.67), channel_id=1, source_target_pairs={{0,7},{1,6},{2,5},{3,4},{4,3},{5,2},{6,1},{7,0},{8,15},{9,14},{10,... | collective-permute-start | bytes 737288 | tf_op jit(solution)/shard_map/ppermute | solution.py:361
  76.1 2.9 %collective-permute-start.14 = (bf16[960,128]{1,0:T(8,128)(2,1)}, bf16[960,128]{1,0:T(8,128)(2,1)S(1)}, u32[]{:S(2)}, u32[]{:S(2)}) collective-permute-start(bf16[960,128]{1,0:T(8,128)(2,1)} %get-tuple-element.68), channel_id=1, source_target_pairs={{0,15},{1,14},{2,13},{3,12},{4,11},{5,10},{6,9},{7,8},{8,7},{9,6},... | collective-permute-start | bytes 737288 | tf_op jit(solution)/shard_map/ppermute | solution.py:361
  79.0 1.0 collective-permute-done.10.rest_11_
  80.0 11.5 %collective-permute-done.13.rest_14_ = bf16[960,128]{1,0:T(8,128)(2,1)S(1)} collective-permute-done((bf16[960,128]{1,0:T(8,128)(2,1)}, bf16[960,128]{1,0:T(8,128)(2,1)S(1)}, u32[]{:S(2)}, u32[]{:S(2)}) %collective-permute-start.13) | collective-permute-done | bytes 245792 | tf_op jit(solution)/shard_map/ppermute | solution.py:361
  91.5 0.9 copy-done
  92.7 10.6 %attend_first.1 = (bf16[16,832,128]{2,1,0:T(8,128)(2,1)S(1)}, bf16[16,256,128]{2,1,0:T(8,128)(2,1)S(1)}) custom-call(s32[1]{0:T(128)} %bitcast.me_ref, s32[576]{0:T(1024)S(1)} %reshape.10.lists_ref, s32[48]{0:T(128)S(1)} %reshape.11.counts_ref, bf16[960,128]{1,0:T(8,128)(2,1)S(1)} %copy-done, bf16[960,128]{1,0:T(8,128)(2,1)S(1)} %collective-permute-done.rest_1_, ...), custom_call_target="tpu_custom_call" | custom-call | flops 1073741824 | bytes 4194304 | tf_op jit(solution)/shard_map/attend_first/pallas_call | solution.py:258
  103.3 4.8 %attend_second.1 = (bf16[2,16,128,128]{3,2,1,0:T(8,128)(2,1)}, bf16[320,128]{1,0:T(8,128)(2,1)S(1)}, bf16[320,128]{1,0:T(8,128)(2,1)S(1)}, bf16[320,128]{1,0:T(8...) custom-call(s32[1]{0:T(128)} %bitcast.me_ref, ...), custom_call_target="tpu_custom_call" | custom-call | flops 536870912 | bytes 2097152 | tf_op jit(solution)/shard_map/attend_second/pallas_call | solution.py:300
  108.1 6.0 %collective-permute-start.16 = (bf16[320,128]{1,0:T(8,128)(2,1)S(1)}, bf16[320,128]{1,0:T(8,128)(2,1)S(1)}, u32[]{:S(2)}, u32[]{:S(2)}) collective-permute-start(bf16[320,128]{1,0:T(8,128)(2,1)S(1)} %get-tuple-element.72), channel_id=1, source_target_pairs={{0,8},{1,9},{2,10},{3,11},{4,12},{5,13},{6,14},{7,15},{8,0},{9,1},... | collective-permute-start | bytes 245768 | tf_op jit(solution)/shard_map/ppermute | solution.py:361
  114.1 2.4 %collective-permute-start.18 = (bf16[320,128]{1,0:T(8,128)(2,1)S(1)}, bf16[320,128]{1,0:T(8,128)(2,1)S(1)}, u32[]{:S(2)}, u32[]{:S(2)}) collective-permute-start(bf16[320,128]{1,0:T(8,128)(2,1)S(1)} %get-tuple-element.74), channel_id=1, source_target_pairs={{0,10},{1,11},{2,8},{3,9},{4,14},{5,15},{6,12},{7,13},{8,2},{9,3},... | collective-permute-start | bytes 245768 | tf_op jit(solution)/shard_map/ppermute | solution.py:361
  116.6 3.4 %collective-permute-start.20 = (bf16[320,128]{1,0:T(8,128)(2,1)S(1)}, bf16[320,128]{1,0:T(8,128)(2,1)S(1)}, u32[]{:S(2)}, u32[]{:S(2)}) collective-permute-start(bf16[320,128]{1,0:T(8,128)(2,1)S(1)} %get-tuple-element.76), channel_id=1, source_target_pairs={{0,12},{1,13},{2,14},{3,15},{4,8},{5,9},{6,10},{7,11},{8,4},{9,5},... | collective-permute-start | bytes 245768 | tf_op jit(solution)/shard_map/ppermute | solution.py:361
  120.0 2.7 %collective-permute-start.22 = (bf16[320,128]{1,0:T(8,128)(2,1)S(1)}, bf16[320,128]{1,0:T(8,128)(2,1)S(1)}, u32[]{:S(2)}, u32[]{:S(2)}) collective-permute-start(bf16[320,128]{1,0:T(8,128)(2,1)S(1)} %get-tuple-element.78), channel_id=1, source_target_pairs={{0,14},{1,15},{2,12},{3,13},{4,10},{5,11},{6,8},{7,9},{8,6},{9,7},... | collective-permute-start | bytes 245768 | tf_op jit(solution)/shard_map/ppermute | solution.py:361
  122.6 2.5 %collective-permute-done.18.rest_3_ = bf16[320,128]{1,0:T(8,128)(2,1)S(1)} collective-permute-done((bf16[320,128]{1,0:T(8,128)(2,1)S(1)}, bf16[320,128]{1,0:T(8,128)(2,1)S(1)}, u32[]{:S(2)}, u32[]{:S(2)}) %collective-permute-start.18) | collective-permute-done | bytes 81952 | tf_op jit(solution)/shard_map/ppermute | solution.py:361
  125.2 3.7 %collective-permute-start.25 = (bf16[320,128]{1,0:T(8,128)(2,1)S(1)}, bf16[320,128]{1,0:T(8,128)(2,1)S(1)}, u32[]{:S(2)}, u32[]{:S(2)}) collective-permute-start(bf16[320,128]{1,0:T(8,128)(2,1)S(1)} %get-tuple-element.81), channel_id=1, source_target_pairs={{0,5},{1,4},{2,7},{3,6},{4,1},{5,0},{6,3},{7,2},{8,13},{9,12},{10,... | collective-permute-start | bytes 245768 | tf_op jit(solution)/shard_map/ppermute | solution.py:361
  128.9 2.0 %collective-permute-start.27 = (bf16[320,128]{1,0:T(8,128)(2,1)S(1)}, bf16[320,128]{1,0:T(8,128)(2,1)S(1)}, u32[]{:S(2)}, u32[]{:S(2)}) collective-permute-start(bf16[320,128]{1,0:T(8,128)(2,1)S(1)} %get-tuple-element.83), channel_id=1, source_target_pairs={{0,3},{1,2},{2,1},{3,0},{4,7},{5,6},{6,5},{7,4},{8,11},{9,10},{10,... | collective-permute-start | bytes 245768 | tf_op jit(solution)/shard_map/ppermute | solution.py:361
  130.9 1.8 %collective-permute-start.28 = (bf16[320,128]{1,0:T(8,128)(2,1)S(1)}, bf16[320,128]{1,0:T(8,128)(2,1)S(1)}, u32[]{:S(2)}, u32[]{:S(2)}) collective-permute-start(bf16[320,128]{1,0:T(8,128)(2,1)S(1)} %get-tuple-element.84), channel_id=1, source_target_pairs={{0,13},{1,12},{2,15},{3,14},{4,9},{5,8},{6,11},{7,10},{8,5},{9,4},... | collective-permute-start | bytes 245768 | tf_op jit(solution)/shard_map/ppermute | solution.py:361
  133.6 2.0 %collective-permute-start.30 = (bf16[320,128]{1,0:T(8,128)(2,1)S(1)}, bf16[320,128]{1,0:T(8,128)(2,1)S(1)}, u32[]{:S(2)}, u32[]{:S(2)}) collective-permute-start(bf16[320,128]{1,0:T(8,128)(2,1)S(1)} %get-tuple-element.86), channel_id=1, source_target_pairs={{0,15},{1,14},{2,13},{3,12},{4,11},{5,10},{6,9},{7,8},{8,7},{9,6},... | collective-permute-start | bytes 245768 | tf_op jit(solution)/shard_map/ppermute | solution.py:361
  135.5 2.7 %collective-permute-done.26.rest_11_ = bf16[320,128]{1,0:T(8,128)(2,1)S(1)} collective-permute-done((bf16[320,128]{1,0:T(8,128)(2,1)S(1)}, bf16[320,128]{1,0:T(8,128)(2,1)S(1)}, u32[]{:S(2)}, u32[]{:S(2)}) %collective-permute-start.26) | collective-permute-done | bytes 81952 | tf_op jit(solution)/shard_map/ppermute | solution.py:361
  138.2 2.6 %collective-permute-done.29.rest_14_ = bf16[320,128]{1,0:T(8,128)(2,1)S(1)} collective-permute-done((bf16[320,128]{1,0:T(8,128)(2,1)S(1)}, bf16[320,128]{1,0:T(8,128)(2,1)S(1)}, u32[]{:S(2)}, u32[]{:S(2)}) %collective-permute-start.29) | collective-permute-done | bytes 81952 | tf_op jit(solution)/shard_map/ppermute | solution.py:361
  140.9 1.5 %assemble.1 = bf16[128,5120]{1,0:T(8,128)(2,1)} custom-call(s32[1]{0:T(128)} %bitcast.me_ref, bf16[320,128]{1,0:T(8,128)(2,1)S(1)} %get-tuple-element.71.rest_0_, bf16[320,128]{1,0:T(8,128)(2,1)S(1)} %collective-permute-done.16.rest_1_, bf16[320,128]{1,0:T(8,128)(2,1)S(1)} %collective-permute-done.17.rest_2_, ...), custom_call_target="tpu_custom_call" | custom-call | tf_op jit(solution)/shard_map/assemble/pallas_call | solution.py:346
  (49 shorter events, 3.0 us)
Async XLA Ops:
  0.0 54.3 %copy-start.1 = (s32[40,16,12]{0,1,2:T(8,128)S(1)}, s32[40,16,12]{0,1,2:T(8,128)}, u32[]{:S(2)}) copy-start(s32[40,16,12]{0,1,2:T(8,128)} %param.12) | copy-start | bytes 92164
  6.4 17.3 %collective-permute-start = (bf16[960,128]{1,0:T(8,128)(2,1)}, bf16[960,128]{1,0:T(8,128)(2,1)S(1)}, u32[]{:S(2)}, u32[]{:S(2)}) collective-permute-start(bf16[960,128]{1,0:T(8,128)(2,1)} %get-tuple-element.48), channel_id=1, source_target_pairs={{0,8},{1,9},{2,10},{3,11},{4,12},{5,13},{6,14},{7,15},{8,0},{9,1},... | collective-permute-start | bytes 737288 | tf_op jit(solution)/shard_map/ppermute | solution.py:361
  10.5 14.3 %collective-permute-start.1 = (bf16[960,128]{1,0:T(8,128)(2,1)}, bf16[960,128]{1,0:T(8,128)(2,1)S(1)}, u32[]{:S(2)}, u32[]{:S(2)}) collective-permute-start(bf16[960,128]{1,0:T(8,128)(2,1)} %get-tuple-element.55), channel_id=1, source_target_pairs={{0,4},{1,5},{2,6},{3,7},{4,0},{5,1},{6,2},{7,3},{8,12},{9,13},{10,... | collective-permute-start | bytes 737288 | tf_op jit(solution)/shard_map/ppermute | solution.py:361
  12.1 29.0 %collective-permute-start.2 = (bf16[960,128]{1,0:T(8,128)(2,1)}, bf16[960,128]{1,0:T(8,128)(2,1)S(1)}, u32[]{:S(2)}, u32[]{:S(2)}) collective-permute-start(bf16[960,128]{1,0:T(8,128)(2,1)} %get-tuple-element.56), channel_id=1, source_target_pairs={{0,10},{1,11},{2,8},{3,9},{4,14},{5,15},{6,12},{7,13},{8,2},{9,3},... | collective-permute-start | bytes 737288 | tf_op jit(solution)/shard_map/ppermute | solution.py:361
  13.4 27.7 %collective-permute-start.3 = (bf16[960,128]{1,0:T(8,128)(2,1)}, bf16[960,128]{1,0:T(8,128)(2,1)S(1)}, u32[]{:S(2)}, u32[]{:S(2)}) collective-permute-start(bf16[960,128]{1,0:T(8,128)(2,1)} %get-tuple-element.57), channel_id=1, source_target_pairs={{0,2},{1,3},{2,0},{3,1},{4,6},{5,7},{6,4},{7,5},{8,10},{9,11},{10,... | collective-permute-start | bytes 737288 | tf_op jit(solution)/shard_map/ppermute | solution.py:361
  13.9 27.2 %collective-permute-start.4 = (bf16[960,128]{1,0:T(8,128)(2,1)}, bf16[960,128]{1,0:T(8,128)(2,1)S(1)}, u32[]{:S(2)}, u32[]{:S(2)}) collective-permute-start(bf16[960,128]{1,0:T(8,128)(2,1)} %get-tuple-element.58), channel_id=1, source_target_pairs={{0,12},{1,13},{2,14},{3,15},{4,8},{5,9},{6,10},{7,11},{8,4},{9,5},... | collective-permute-start | bytes 737288 | tf_op jit(solution)/shard_map/ppermute | solution.py:361
  23.7 31.0 %collective-permute-start.5 = (bf16[960,128]{1,0:T(8,128)(2,1)}, bf16[960,128]{1,0:T(8,128)(2,1)S(1)}, u32[]{:S(2)}, u32[]{:S(2)}) collective-permute-start(bf16[960,128]{1,0:T(8,128)(2,1)} %get-tuple-element.59), channel_id=1, source_target_pairs={{0,6},{1,7},{2,4},{3,5},{4,2},{5,3},{6,0},{7,1},{8,14},{9,15},{10,... | collective-permute-start | bytes 737288 | tf_op jit(solution)/shard_map/ppermute | solution.py:361
  24.8 32.7 %collective-permute-start.6 = (bf16[960,128]{1,0:T(8,128)(2,1)}, bf16[960,128]{1,0:T(8,128)(2,1)S(1)}, u32[]{:S(2)}, u32[]{:S(2)}) collective-permute-start(bf16[960,128]{1,0:T(8,128)(2,1)} %get-tuple-element.60), channel_id=1, source_target_pairs={{0,14},{1,15},{2,12},{3,13},{4,10},{5,11},{6,8},{7,9},{8,6},{9,7},... | collective-permute-start | bytes 737288 | tf_op jit(solution)/shard_map/ppermute | solution.py:361
  41.1 17.1 %collective-permute-start.7 = (bf16[960,128]{1,0:T(8,128)(2,1)}, bf16[960,128]{1,0:T(8,128)(2,1)S(1)}, u32[]{:S(2)}, u32[]{:S(2)}) collective-permute-start(bf16[960,128]{1,0:T(8,128)(2,1)} %get-tuple-element.61), channel_id=1, source_target_pairs={{0,1},{1,0},{2,3},{3,2},{4,5},{5,4},{6,7},{7,6},{8,9},{9,8},{10,11... | collective-permute-start | bytes 737288 | tf_op jit(solution)/shard_map/ppermute | solution.py:361
  41.1 22.3 %collective-permute-start.8 = (bf16[960,128]{1,0:T(8,128)(2,1)}, bf16[960,128]{1,0:T(8,128)(2,1)S(1)}, u32[]{:S(2)}, u32[]{:S(2)}) collective-permute-start(bf16[960,128]{1,0:T(8,128)(2,1)} %get-tuple-element.62), channel_id=1, source_target_pairs={{0,9},{1,8},{2,11},{3,10},{4,13},{5,12},{6,15},{7,14},{8,1},{9,0},... | collective-permute-start | bytes 737288 | tf_op jit(solution)/shard_map/ppermute | solution.py:361
  41.1 35.0 %collective-permute-start.9 = (bf16[960,128]{1,0:T(8,128)(2,1)}, bf16[960,128]{1,0:T(8,128)(2,1)S(1)}, u32[]{:S(2)}, u32[]{:S(2)}) collective-permute-start(bf16[960,128]{1,0:T(8,128)(2,1)} %get-tuple-element.63), channel_id=1, source_target_pairs={{0,5},{1,4},{2,7},{3,6},{4,1},{5,0},{6,3},{7,2},{8,13},{9,12},{10,... | collective-permute-start | bytes 737288 | tf_op jit(solution)/shard_map/ppermute | solution.py:361
  54.7 25.3 %collective-permute-start.10 = (bf16[960,128]{1,0:T(8,128)(2,1)}, bf16[960,128]{1,0:T(8,128)(2,1)S(1)}, u32[]{:S(2)}, u32[]{:S(2)}) collective-permute-start(bf16[960,128]{1,0:T(8,128)(2,1)} %get-tuple-element.64), channel_id=1, source_target_pairs={{0,11},{1,10},{2,9},{3,8},{4,15},{5,14},{6,13},{7,12},{8,3},{9,2},... | collective-permute-start | bytes 737288 | tf_op jit(solution)/shard_map/ppermute | solution.py:361
  57.5 22.5 %collective-permute-start.11 = (bf16[960,128]{1,0:T(8,128)(2,1)}, bf16[960,128]{1,0:T(8,128)(2,1)S(1)}, u32[]{:S(2)}, u32[]{:S(2)}) collective-permute-start(bf16[960,128]{1,0:T(8,128)(2,1)} %get-tuple-element.65), channel_id=1, source_target_pairs={{0,3},{1,2},{2,1},{3,0},{4,7},{5,6},{6,5},{7,4},{8,11},{9,10},{10,... | collective-permute-start | bytes 737288 | tf_op jit(solution)/shard_map/ppermute | solution.py:361
  58.2 21.8 %collective-permute-start.12 = (bf16[960,128]{1,0:T(8,128)(2,1)}, bf16[960,128]{1,0:T(8,128)(2,1)S(1)}, u32[]{:S(2)}, u32[]{:S(2)}) collective-permute-start(bf16[960,128]{1,0:T(8,128)(2,1)} %get-tuple-element.66), channel_id=1, source_target_pairs={{0,13},{1,12},{2,15},{3,14},{4,9},{5,8},{6,11},{7,10},{8,5},{9,4},... | collective-permute-start | bytes 737288 | tf_op jit(solution)/shard_map/ppermute | solution.py:361
  63.4 28.1 %collective-permute-start.13 = (bf16[960,128]{1,0:T(8,128)(2,1)}, bf16[960,128]{1,0:T(8,128)(2,1)S(1)}, u32[]{:S(2)}, u32[]{:S(2)}) collective-permute-start(bf16[960,128]{1,0:T(8,128)(2,1)} %get-tuple-element.67), channel_id=1, source_target_pairs={{0,7},{1,6},{2,5},{3,4},{4,3},{5,2},{6,1},{7,0},{8,15},{9,14},{10,... | collective-permute-start | bytes 737288 | tf_op jit(solution)/shard_map/ppermute | solution.py:361
  76.1 15.3 %collective-permute-start.14 = (bf16[960,128]{1,0:T(8,128)(2,1)}, bf16[960,128]{1,0:T(8,128)(2,1)S(1)}, u32[]{:S(2)}, u32[]{:S(2)}) collective-permute-start(bf16[960,128]{1,0:T(8,128)(2,1)} %get-tuple-element.68), channel_id=1, source_target_pairs={{0,15},{1,14},{2,13},{3,12},{4,11},{5,10},{6,9},{7,8},{8,7},{9,6},... | collective-permute-start | bytes 737288 | tf_op jit(solution)/shard_map/ppermute | solution.py:361
  92.5 10.8 %collective-permute-start.15 = (bf16[16,128,128]{2,1,0:T(8,128)(2,1)S(1)}, bf16[16,128,128]{2,1,0:T(8,128)(2,1)S(1)}, u32[]{:S(2)}, u32[]{:S(2)}) collective-permute-start(bf16[16,128,128]{2,1,0:T(8,128)(2,1)S(1)} %collect_shared.1.own_ref), channel_id=1, source_target_pairs={{0,1},{1,0},{2,3},{3,2},{4,5},{5,4},{6,7},{7,6},{8,9},{9,8},{10,11... | collective-permute-start | bytes 1572872 | tf_op jit(solution)/shard_map/ppermute | solution.py:361
  108.1 11.9 %collective-permute-start.16 = (bf16[320,128]{1,0:T(8,128)(2,1)S(1)}, bf16[320,128]{1,0:T(8,128)(2,1)S(1)}, u32[]{:S(2)}, u32[]{:S(2)}) collective-permute-start(bf16[320,128]{1,0:T(8,128)(2,1)S(1)} %get-tuple-element.72), channel_id=1, source_target_pairs={{0,8},{1,9},{2,10},{3,11},{4,12},{5,13},{6,14},{7,15},{8,0},{9,1},... | collective-permute-start | bytes 245768 | tf_op jit(solution)/shard_map/ppermute | solution.py:361
  114.1 5.9 %collective-permute-start.17 = (bf16[320,128]{1,0:T(8,128)(2,1)S(1)}, bf16[320,128]{1,0:T(8,128)(2,1)S(1)}, u32[]{:S(2)}, u32[]{:S(2)}) collective-permute-start(bf16[320,128]{1,0:T(8,128)(2,1)S(1)} %get-tuple-element.73), channel_id=1, source_target_pairs={{0,4},{1,5},{2,6},{3,7},{4,0},{5,1},{6,2},{7,3},{8,12},{9,13},{10,... | collective-permute-start | bytes 245768 | tf_op jit(solution)/shard_map/ppermute | solution.py:361
  114.1 11.0 %collective-permute-start.18 = (bf16[320,128]{1,0:T(8,128)(2,1)S(1)}, bf16[320,128]{1,0:T(8,128)(2,1)S(1)}, u32[]{:S(2)}, u32[]{:S(2)}) collective-permute-start(bf16[320,128]{1,0:T(8,128)(2,1)S(1)} %get-tuple-element.74), channel_id=1, source_target_pairs={{0,10},{1,11},{2,8},{3,9},{4,14},{5,15},{6,12},{7,13},{8,2},{9,3},... | collective-permute-start | bytes 245768 | tf_op jit(solution)/shard_map/ppermute | solution.py:361
  116.6 8.6 %collective-permute-start.19 = (bf16[320,128]{1,0:T(8,128)(2,1)S(1)}, bf16[320,128]{1,0:T(8,128)(2,1)S(1)}, u32[]{:S(2)}, u32[]{:S(2)}) collective-permute-start(bf16[320,128]{1,0:T(8,128)(2,1)S(1)} %get-tuple-element.75), channel_id=1, source_target_pairs={{0,2},{1,3},{2,0},{3,1},{4,6},{5,7},{6,4},{7,5},{8,10},{9,11},{10,... | collective-permute-start | bytes 245768 | tf_op jit(solution)/shard_map/ppermute | solution.py:361
  116.6 8.6 %collective-permute-start.20 = (bf16[320,128]{1,0:T(8,128)(2,1)S(1)}, bf16[320,128]{1,0:T(8,128)(2,1)S(1)}, u32[]{:S(2)}, u32[]{:S(2)}) collective-permute-start(bf16[320,128]{1,0:T(8,128)(2,1)S(1)} %get-tuple-element.76), channel_id=1, source_target_pairs={{0,12},{1,13},{2,14},{3,15},{4,8},{5,9},{6,10},{7,11},{8,4},{9,5},... | collective-permute-start | bytes 245768 | tf_op jit(solution)/shard_map/ppermute | solution.py:361
  120.0 8.9 %collective-permute-start.21 = (bf16[320,128]{1,0:T(8,128)(2,1)S(1)}, bf16[320,128]{1,0:T(8,128)(2,1)S(1)}, u32[]{:S(2)}, u32[]{:S(2)}) collective-permute-start(bf16[320,128]{1,0:T(8,128)(2,1)S(1)} %get-tuple-element.77), channel_id=1, source_target_pairs={{0,6},{1,7},{2,4},{3,5},{4,2},{5,3},{6,0},{7,1},{8,14},{9,15},{10,... | collective-permute-start | bytes 245768 | tf_op jit(solution)/shard_map/ppermute | solution.py:361
  120.0 8.9 %collective-permute-start.22 = (bf16[320,128]{1,0:T(8,128)(2,1)S(1)}, bf16[320,128]{1,0:T(8,128)(2,1)S(1)}, u32[]{:S(2)}, u32[]{:S(2)}) collective-permute-start(bf16[320,128]{1,0:T(8,128)(2,1)S(1)} %get-tuple-element.78), channel_id=1, source_target_pairs={{0,14},{1,15},{2,12},{3,13},{4,10},{5,11},{6,8},{7,9},{8,6},{9,7},... | collective-permute-start | bytes 245768 | tf_op jit(solution)/shard_map/ppermute | solution.py:361
  125.2 5.8 %collective-permute-start.23 = (bf16[320,128]{1,0:T(8,128)(2,1)S(1)}, bf16[320,128]{1,0:T(8,128)(2,1)S(1)}, u32[]{:S(2)}, u32[]{:S(2)}) collective-permute-start(bf16[320,128]{1,0:T(8,128)(2,1)S(1)} %get-tuple-element.79), channel_id=1, source_target_pairs={{0,1},{1,0},{2,3},{3,2},{4,5},{5,4},{6,7},{7,6},{8,9},{9,8},{10,11... | collective-permute-start | bytes 245768 | tf_op jit(solution)/shard_map/ppermute | solution.py:361
  125.2 7.6 %collective-permute-start.24 = (bf16[320,128]{1,0:T(8,128)(2,1)S(1)}, bf16[320,128]{1,0:T(8,128)(2,1)S(1)}, u32[]{:S(2)}, u32[]{:S(2)}) collective-permute-start(bf16[320,128]{1,0:T(8,128)(2,1)S(1)} %get-tuple-element.80), channel_id=1, source_target_pairs={{0,9},{1,8},{2,11},{3,10},{4,13},{5,12},{6,15},{7,14},{8,1},{9,0},... | collective-permute-start | bytes 245768 | tf_op jit(solution)/shard_map/ppermute | solution.py:361
  125.2 8.4 %collective-permute-start.25 = (bf16[320,128]{1,0:T(8,128)(2,1)S(1)}, bf16[320,128]{1,0:T(8,128)(2,1)S(1)}, u32[]{:S(2)}, u32[]{:S(2)}) collective-permute-start(bf16[320,128]{1,0:T(8,128)(2,1)S(1)} %get-tuple-element.81), channel_id=1, source_target_pairs={{0,5},{1,4},{2,7},{3,6},{4,1},{5,0},{6,3},{7,2},{8,13},{9,12},{10,... | collective-permute-start | bytes 245768 | tf_op jit(solution)/shard_map/ppermute | solution.py:361
  128.9 9.3 %collective-permute-start.26 = (bf16[320,128]{1,0:T(8,128)(2,1)S(1)}, bf16[320,128]{1,0:T(8,128)(2,1)S(1)}, u32[]{:S(2)}, u32[]{:S(2)}) collective-permute-start(bf16[320,128]{1,0:T(8,128)(2,1)S(1)} %get-tuple-element.82), channel_id=1, source_target_pairs={{0,11},{1,10},{2,9},{3,8},{4,15},{5,14},{6,13},{7,12},{8,3},{9,2},... | collective-permute-start | bytes 245768 | tf_op jit(solution)/shard_map/ppermute | solution.py:361
  128.9 9.3 %collective-permute-start.27 = (bf16[320,128]{1,0:T(8,128)(2,1)S(1)}, bf16[320,128]{1,0:T(8,128)(2,1)S(1)}, u32[]{:S(2)}, u32[]{:S(2)}) collective-permute-start(bf16[320,128]{1,0:T(8,128)(2,1)S(1)} %get-tuple-element.83), channel_id=1, source_target_pairs={{0,3},{1,2},{2,1},{3,0},{4,7},{5,6},{6,5},{7,4},{8,11},{9,10},{10,... | collective-permute-start | bytes 245768 | tf_op jit(solution)/shard_map/ppermute | solution.py:361
  130.9 7.3 %collective-permute-start.28 = (bf16[320,128]{1,0:T(8,128)(2,1)S(1)}, bf16[320,128]{1,0:T(8,128)(2,1)S(1)}, u32[]{:S(2)}, u32[]{:S(2)}) collective-permute-start(bf16[320,128]{1,0:T(8,128)(2,1)S(1)} %get-tuple-element.84), channel_id=1, source_target_pairs={{0,13},{1,12},{2,15},{3,14},{4,9},{5,8},{6,11},{7,10},{8,5},{9,4},... | collective-permute-start | bytes 245768 | tf_op jit(solution)/shard_map/ppermute | solution.py:361
  132.7 8.2 %collective-permute-start.29 = (bf16[320,128]{1,0:T(8,128)(2,1)S(1)}, bf16[320,128]{1,0:T(8,128)(2,1)S(1)}, u32[]{:S(2)}, u32[]{:S(2)}) collective-permute-start(bf16[320,128]{1,0:T(8,128)(2,1)S(1)} %get-tuple-element.85), channel_id=1, source_target_pairs={{0,7},{1,6},{2,5},{3,4},{4,3},{5,2},{6,1},{7,0},{8,15},{9,14},{10,... | collective-permute-start | bytes 245768 | tf_op jit(solution)/shard_map/ppermute | solution.py:361
  133.6 7.3 %collective-permute-start.30 = (bf16[320,128]{1,0:T(8,128)(2,1)S(1)}, bf16[320,128]{1,0:T(8,128)(2,1)S(1)}, u32[]{:S(2)}, u32[]{:S(2)}) collective-permute-start(bf16[320,128]{1,0:T(8,128)(2,1)S(1)} %get-tuple-element.86), channel_id=1, source_target_pairs={{0,15},{1,14},{2,13},{3,12},{4,11},{5,10},{6,9},{7,8},{8,7},{9,6},... | collective-permute-start | bytes 245768 | tf_op jit(solution)/shard_map/ppermute | solution.py:361
  (2 other events, 25.7 us)
